TPU v7x, 32 devices: a whole 2x2x4 slice. The times are simulated.
32 devices in a mesh: req: 8 (over y, x, core), seq: 4 (over z).
Axes of the slice: x: 2, y: 2, z: 4, core: 2. Of those that a mesh axis runs over, the one named last changes fastest.
Arguments:
- qkv_proj: bfloat16 [8, 512, 4096], P('req', 'seq'), may hold values from -6 to 6
- gate_proj: bfloat16 [8, 512, 2048], P('req', 'seq'), may hold values from -6 to 6
- residual: bfloat16 [8, 512, 2048], P('req', 'seq'), may hold values from -6 to 6
- log_decay: float32 [8, 512, 8], P('req', 'seq'), may hold values from -1 to 0, as said below
- beta_logit: bfloat16 [8, 512, 8], P('req', 'seq'), may hold values from -6 to 6
- lengths: int32 [8], replicated, may hold values from 1 to 512, 2048 in all
- slot_request: int32 [8], replicated, may hold values from 0 to 7, each once
- conv_weight: float32 [4, 4096], replicated, may hold values from -3 to 3
- norm_gain: float32 [256], replicated, may hold values from 0.1 to 1.9
- out_weight: bfloat16 [2048, 2048], P(('req', 'seq')), may hold values from -0.125 to 0.125
- mlp_gain: float32 [2048], replicated, may hold values from 0.1 to 1.9
- w_gate: bfloat16 [2048, 5632], P('req', 'seq'), may hold values from -0.125 to 0.125
- w_up: bfloat16 [2048, 5632], P('req', 'seq'), may hold values from -0.125 to 0.125
- w_down: bfloat16 [5632, 2048], P('seq', 'req'), may hold values from -0.078125 to 0.078125
Outputs:
- hidden_out: bfloat16 [8, 512, 2048], P('req', 'seq')
- final_state: float32 [8, 8, 128, 256], P('req', 'seq')
- conv_edge: bfloat16 [8, 3, 4096], P('req', None, 'seq')
Inputs may be any that keep to these rules, and one draw needn't show every extreme that they name: Slot s of the req axis holds request slot_request[s]. The 8 lengths sum to 2048, and the longest is exactly 512. `log_decay`: every entry is negative.
All inputs are finite; a program needn't handle non-finite values.
Results may differ from a plain program's by a relative error of at most 0.014.
Values may be sent and summed in bfloat16 or wider, within the bound.
No kernel may reach another device: no remote copies, remote signals or barrier semaphores. Data moves between devices by JAX's collectives and lax.ppermute only.
A program may use at most 128 MiB of HBM per device.

v0:
```python
import jax
import jax.numpy as jnp
from jax import lax
from jax.sharding import PartitionSpec as P

LOCAL_HEADS = 8
DK = 128
DV = 256
CONV = 4
BLOCK = 64
HK = 1024


EPS_NORM = 1e-05
EPS_UNIT = 1e-06
HIGHEST = lax.Precision.HIGHEST


def shifted(value, axis, steps):
    count = lax.axis_size(axis)
    initial, last = (max(0, -steps), min(count, count - steps))
    return lax.ppermute(value, axis, [(source, source + steps) for source in range(initial, last)])


def unit_norm(vector):
    return vector * lax.rsqrt(jnp.sum(vector * vector, axis=-1, keepdims=True) + EPS_UNIT)


def to_blocks(tensor, block_len):
    length = tensor.shape[0]
    grouped = tensor.reshape((length // block_len, block_len) + tensor.shape[1:])
    return jnp.moveaxis(grouped, 2, 0)


def block_tables(query_vec, key_vecs, beta_gate, decay_log, block_len):
    query_b = to_blocks(query_vec, block_len)
    keys_b = to_blocks(key_vecs, block_len)
    beta_b = to_blocks(beta_gate, block_len)
    cumulative = jnp.cumsum(to_blocks(decay_log, block_len), axis=-1)
    spread = cumulative[..., :, None] - cumulative[..., None, :]
    lower_full = jnp.tril(jnp.ones((block_len, block_len), jnp.float32))
    lower_strict = jnp.tril(jnp.ones((block_len, block_len), jnp.float32), -1)
    within = jnp.exp(jnp.where(lower_full > 0, spread, 0.0)) * lower_full
    key_inner = jnp.einsum("hnik,hnjk->hnij", keys_b, keys_b, precision=HIGHEST)
    couple = beta_b[..., :, None] * within * lower_strict * key_inner
    identity = jnp.broadcast_to(jnp.eye(block_len, dtype=jnp.float32), couple.shape)
    inverse = lax.linalg.triangular_solve(
        identity + couple, identity, left_side=True, lower=True, unit_diagonal=True
    )
    growth = jnp.exp(cumulative)
    weighted_keys = jnp.einsum(
        "hnij,hnjk->hnik", inverse, (beta_b * growth)[..., None] * keys_b, precision=HIGHEST
    )
    query_keys = jnp.einsum("hnik,hnjk->hnij", query_b, keys_b, precision=HIGHEST) * within
    grown_query = growth[..., None] * query_b
    keys_to_end = jnp.exp(cumulative[..., -1:] - cumulative)[..., None] * keys_b
    end_growth = growth[..., -1]
    return (inverse, beta_b, (weighted_keys, query_keys, grown_query, keys_to_end, end_growth))


def solve_values(inverse, beta_b, values_b):
    return jnp.einsum("hnij,hnjx->hnix", inverse, beta_b[..., None] * values_b, precision=HIGHEST)


def run_blocks(initial, solved, tables):
    weighted_keys, query_keys, grown_query, keys_to_end, end_growth = tables
    sequence = tuple(
        (
            jnp.moveaxis(tensor, 1, 0)
            for tensor in (solved, weighted_keys, query_keys, grown_query, keys_to_end, end_growth)
        )
    )

    def advance(running, inputs_now):
        solved_now, weighted_now, inner_now, query_now, keys_now, growth_now = inputs_now
        corrected = solved_now - jnp.einsum(
            "hck,hkx->hcx", weighted_now, running, precision=HIGHEST
        )
        output_now = jnp.einsum("hck,hkx->hcx", query_now, running, precision=HIGHEST) + jnp.einsum(
            "hcd,hdx->hcx", inner_now, corrected, precision=HIGHEST
        )
        running = growth_now[:, None, None] * running + jnp.einsum(
            "hck,hcx->hkx", keys_now, corrected, precision=HIGHEST
        )
        return (running, output_now)

    return lax.scan(advance, initial, sequence)


def local(
    qkv_proj,
    gate_proj,
    residual,
    log_decay,
    beta_logit,
    lengths,
    slot_request,
    conv_weight,
    norm_gain,
    out_weight,
    mlp_gain,
    w_gate,
    w_up,
    w_down,
):
    seq_index = lax.axis_index("seq")
    req_index = lax.axis_index("req")
    seq_size = lax.axis_size("seq")
    piece_len = qkv_proj.shape[1]
    channels = qkv_proj.shape[2]
    request_ids = jnp.arange(slot_request.shape[0], dtype=jnp.int32)
    request = jnp.sum(jnp.where(request_ids == req_index, slot_request, 0))
    length = jnp.sum(jnp.where(request_ids == request, lengths, 0))
    position = seq_index * piece_len + jnp.arange(piece_len, dtype=jnp.int32)
    live_mask = position < length
    tokens = qkv_proj[0]
    rim_rows = shifted(tokens[piece_len - (CONV - 1) :], "seq", 1)
    extended = jnp.concatenate([rim_rows, tokens], axis=0)
    convolved = jnp.zeros((piece_len, channels), jnp.float32)
    for offset in range(CONV):
        convolved = convolved + conv_weight[offset] * extended[offset : offset + piece_len].astype(
            jnp.float32
        )
    activated = jax.nn.silu(convolved)
    query_vec = unit_norm(activated[:, :HK].reshape(piece_len, LOCAL_HEADS, DK)) * DK ** (-0.5)
    key_vecs = unit_norm(activated[:, HK : 2 * HK].reshape(piece_len, LOCAL_HEADS, DK))
    values = activated[:, 2 * HK :].reshape(piece_len, LOCAL_HEADS, DV)
    beta_gate = jax.nn.sigmoid(beta_logit[0].astype(jnp.float32)) * live_mask[:, None]
    decay_log = jnp.where(live_mask[:, None], log_decay[0], 0.0)
    inverse, beta_b, tables = block_tables(query_vec, key_vecs, beta_gate, decay_log, BLOCK)
    values_b = to_blocks(values, BLOCK)
    solved = solve_values(inverse, beta_b, values_b)
    zero_state = jnp.zeros((LOCAL_HEADS, DK, DV), jnp.float32)
    incoming = zero_state
    for section_index in range(seq_size - 1):
        ending, discarded = run_blocks(incoming, solved, tables)
        incoming = shifted(ending.astype(jnp.bfloat16), "seq", 1).astype(ending.dtype)
    ending, outputs = run_blocks(incoming, solved, tables)
    outputs = jnp.moveaxis(outputs, 1, 2).reshape(piece_len, LOCAL_HEADS, DV)
    is_last = seq_index == seq_size - 1
    state_term = jnp.where(is_last, ending, 0.0)
    targets = length - (CONV - 1) + jnp.arange(CONV - 1, dtype=jnp.int32)
    select = (position[None, :] == targets[:, None]).astype(jnp.bfloat16)
    edge_term = jnp.dot(select, tokens, preferred_element_type=jnp.float32)
    state_part, edge_part = (
        lax.psum_scatter(
            state_term.astype(jnp.bfloat16), "seq", scatter_dimension=0, tiled=True
        ).astype(jnp.float32),
        lax.psum_scatter(
            edge_term.astype(jnp.bfloat16), "seq", scatter_dimension=1, tiled=True
        ).astype(jnp.float32),
    )
    gate_values = gate_proj[0].astype(jnp.float32).reshape(piece_len, LOCAL_HEADS, DV)
    scaled = outputs * lax.rsqrt(jnp.mean(outputs * outputs, axis=-1, keepdims=True) + EPS_NORM)
    mixed_heads = (
        (scaled * norm_gain * jax.nn.silu(gate_values))
        .reshape(piece_len, LOCAL_HEADS * DV)
        .astype(jnp.bfloat16)
    )
    attended = jnp.dot(
        mixed_heads,
        lax.all_gather(out_weight, ("req", "seq"), axis=0, tiled=True),
        preferred_element_type=jnp.float32,
    )
    hidden_state = (residual[0].astype(jnp.float32) + attended).astype(jnp.bfloat16)
    stream = hidden_state.astype(jnp.float32)
    normed = (
        stream * lax.rsqrt(jnp.mean(stream * stream, axis=-1, keepdims=True) + EPS_NORM) * mlp_gain
    ).astype(jnp.bfloat16)
    gate_full, up_full = (
        lax.all_gather(w_gate, "req", axis=0, tiled=True),
        lax.all_gather(w_up, "req", axis=0, tiled=True),
    )
    down_full = lax.all_gather(w_down, "req", axis=1, tiled=True)
    shard_rows = lax.all_gather(normed, "seq", axis=0, tiled=True)
    gate_part = jnp.dot(shard_rows, gate_full, preferred_element_type=jnp.float32)
    upward = jnp.dot(shard_rows, up_full, preferred_element_type=jnp.float32)
    inner_units = (jax.nn.silu(gate_part) * upward).astype(jnp.bfloat16)
    summed = lax.psum_scatter(
        jnp.dot(inner_units, down_full, preferred_element_type=jnp.float32).astype(jnp.bfloat16),
        "seq",
        scatter_dimension=0,
        tiled=True,
    ).astype(jnp.float32)
    combined = stream + summed
    hidden_out = jnp.where(live_mask[:, None], combined, 0.0).astype(jnp.bfloat16)
    return (hidden_out[None], state_part[None], edge_part.astype(jnp.bfloat16)[None])


def solution(mesh):
    return jax.shard_map(
        local,
        mesh=mesh,
        in_specs=(
            P("req", "seq", None),
            P("req", "seq", None),
            P("req", "seq", None),
            P("req", "seq", None),
            P("req", "seq", None),
            P(),
            P(),
            P(),
            P(),
            P(("req", "seq"), None),
            P(),
            P("req", "seq"),
            P("req", "seq"),
            P("seq", "req"),
        ),
        out_specs=(P("req", "seq", None), P("req", "seq", None, None), P("req", None, "seq")),
        check_vma=False,
    )
```

profile of v0, /device:TPU:0, one launch (start us, length us, event | category | flops | bytes accessed | tf_op | source)
XLA Modules:
  0.0 437.3 jit_solution(13415387928112284025)
XLA Ops:
  8.0 0.9 slice_bitcast_fusion.2
  8.8 4.9 %collective-permute-start = (bf16[3,4096]{1,0:T(4,128)(2,1)S(1)}, bf16[3,4096]{1,0:T(4,128)(2,1)S(1)}, u32[]{:S(2)}, u32[]{:S(2)}) collective-permute-start(bf16[3,4096]{1,0:T(4,128)(2,1)S(1)} %slice_bitcast_fusion.2), channel_id=1, source_target_pairs={{0,1},{1,2},{2,3},{4,5},{5,6},{6,7},{8,9},{9,10},{10,11},{12,13},{... | collective-permute-start | bytes 73736 | tf_op jit(solution)/shard_map/ppermute | solution.py:22
  14.0 0.8 squeeze.62
  15.6 1.1 fusion.86
  16.7 1.3 fusion.78
  17.9 2.0 fusion.79
  21.8 1.5 divide_multiply_fusion
  23.3 1.4 multiply_bitcast_fusion
  25.9 0.8 copy-done.11
  26.6 1.8 fusion.45
  28.5 80.1 %custom-call.3 = f32[8,2,1,64,64]{3,4,2,1,0:T(8,128)} custom-call(f32[8,2,1,64,64]{4,3,2,1,0:T(8,128)} %fusion.45), custom_call_target="InvertDiagBlocksLowerTriangular" | custom-call | tf_op jit(solution)/shard_map/triangular_solve | solution.py:47
  108.6 2.0 fusion.58
  111.7 1.3 convolution_bitcast_fusion
  113.5 4.1 while.46
  113.6 0.7 convolution_subtract_fusion.11
  114.3 1.3 convolution_add_fusion.13
  115.6 0.7 convolution_subtract_fusion.11
  116.4 1.3 convolution_add_fusion.13
  117.7 0.9 convert_element_type.105
  118.6 4.3 collective-permute-start.1
  122.8 10.4 %collective-permute-done.1 = bf16[8,128,256]{2,1,0:T(8,128)(2,1)} collective-permute-done((bf16[8,128,256]{2,1,0:T(8,128)(2,1)}, bf16[8,128,256]{2,1,0:T(8,128)(2,1)}, u32[]{:S(2)}, u32[]{:S(2)}) %collective-permute-start.1) | collective-permute-done | bytes 524320 | tf_op jit(solution)/shard_map/ppermute | solution.py:22
  133.2 1.1 convert_element_type.106
  134.4 4.2 while.43
  135.1 1.3 convolution_add_fusion.10
  137.2 1.3 convolution_add_fusion.10
  138.5 0.9 convert_element_type.107
  139.4 5.4 %collective-permute-start.2 = (bf16[8,128,256]{2,1,0:T(8,128)(2,1)}, bf16[8,128,256]{2,1,0:T(8,128)(2,1)}, u32[]{:S(2)}, u32[]{:S(2)}) collective-permute-start(bf16[8,128,256]{2,1,0:T(8,128)(2,1)} %convert_element_type.107), channel_id=1, source_target_pairs={{0,1},{1,2},{2,3},{4,5},{5,6},{6,7},{8,9},{9,10},{10,11},{12,13},{... | collective-permute-start | bytes 1572872 | tf_op jit(solution)/shard_map/ppermute | solution.py:22
  144.9 1.1 copy.203
  146.4 0.9 copy.202
  147.3 6.9 %collective-permute-done.2 = bf16[8,128,256]{2,1,0:T(8,128)(2,1)} collective-permute-done((bf16[8,128,256]{2,1,0:T(8,128)(2,1)}, bf16[8,128,256]{2,1,0:T(8,128)(2,1)}, u32[]{:S(2)}, u32[]{:S(2)}) %collective-permute-start.2) | collective-permute-done | bytes 524320 | tf_op jit(solution)/shard_map/ppermute | solution.py:22
  154.2 1.1 convert_element_type.108
  155.4 4.2 while.44
  156.1 1.3 convolution_add_fusion.11
  158.2 1.3 convolution_add_fusion.11
  159.6 4.5 %collective-permute-start.3 = (bf16[8,128,256]{2,1,0:T(8,128)(2,1)S(1)}, bf16[8,128,256]{2,1,0:T(8,128)(2,1)S(1)}, u32[]{:S(2)}, u32[]{:S(2)}) collective-permute-start(bf16[8,128,256]{2,1,0:T(8,128)(2,1)S(1)} %convert_element_type.109), channel_id=1, source_target_pairs={{0,1},{1,2},{2,3},{4,5},{5,6},{6,7},{8,9},{9,10},{10,11},{12,13},{... | collective-permute-start | bytes 1572872 | tf_op jit(solution)/shard_map/ppermute | solution.py:22
  164.2 1.2 fusion.68
  165.4 1.1 bitcast_multiply_fusion.4
  166.6 1.9 fusion.43
  168.4 4.7 %collective-permute-done.3 = bf16[8,128,256]{2,1,0:T(8,128)(2,1)S(1)} collective-permute-done((bf16[8,128,256]{2,1,0:T(8,128)(2,1)S(1)}, bf16[8,128,256]{2,1,0:T(8,128)(2,1)S(1)}, u32[]{:S(2)}, u32[]{:S(2)}) %collective-permute-start.3) | collective-permute-done | bytes 524320 | tf_op jit(solution)/shard_map/ppermute | solution.py:22
  173.3 9.4 %while.45 = (s32[]{:T(128)}, f32[8,128,256]{2,1,0:T(8,128)S(1)}, f32[2,8,64,256]{3,2,1,0:T(8,128)}, f32[2,8]{1,0:T(2,128)S(1)}, f32[2,8,64,128]{3,2,1,0:T(8,128)...) while((s32[]{:T(128)}, f32[8,128,256]{2,1,0:T(8,128)S(1)}, ...), condition=%wide.region_12.13_spmd, body=%wide.region_11.12_spmd.sunk | while | flops 705429504 | bytes 20973352 | solution.py:87
  174.9 0.7 fusion.149
  175.7 0.9 copy-done.9
  176.7 1.3 convolution_add_fusion.12
  179.7 0.7 fusion.149
  180.4 0.9 copy-done.9
  181.4 1.3 convolution_add_fusion.12
  182.7 1.5 multiply_reduce_fusion.1
  184.6 1.3 copy.205
  186.5 1.3 copy.204
  187.9 5.5 %multiply_reduce_fusion = (f32[128]{0:T(128)S(1)}, f32[128,2048]{1,0:T(8,128)S(1)}) fusion(bf16[2048,2048]{1,0:T(8,128)(2,1)} %all-gather.6.cloned.1.call-done, f32[128,2048]{1,0:T(8,128)} %bitcast.252, f32[128,2048]{1,0:T(8,128)S(1)} %bitcast.251, bf16[1,128,2048]{2,1,0:T(8,128)(2,1)} %param.23, f32[2048]{0:T(1024)S(1)} %bitcast.265, ...), kind=kOutput, calls=%fused_computation.86 | convolution fusion | flops 1077673856 | bytes 12591616 | tf_op jit(solution)/shard_map/dot_general | solution.py:160
  193.3 1.0 multiply_convert_fusion
  196.6 1.4 copy.194
  198.1 0.9 select_convert_fusion
  199.3 42.7 %all-gather.8.cloned.1.call-done = bf16[512,2048]{1,0:T(8,128)(2,1)} async-done(((bf16[128,2048]{1,0:T(8,128)(2,1)}), bf16[512,2048]{1,0:T(8,128)(2,1)}) %all-gather.8.cloned.1.call-update) | async-done | bytes 2097168 | tf_op jit(solution)/shard_map/all_gather | solution.py:175
  242.0 8.4 %fusion.87 = f32[512,1408]{1,0:T(8,128)} fusion(bf16[512,2048]{1,0:T(8,128)(2,1)} %all-gather.8.cloned.1.call-done, bf16[2048,1408]{1,0:T(8,128)(2,1)} %all-gather.10.cloned.1.call-done), kind=kOutput, calls=%fused_computation.156 | convolution fusion | flops 2952790016 | bytes 10747904 | tf_op jit(solution)/shard_map/dot_general | solution.py:176
  250.4 35.4 %all-gather.12.cloned.1.call-done = bf16[2048,1408]{1,0:T(8,128)(2,1)} async-done(((bf16[256,1408]{1,0:T(8,128)(2,1)}), bf16[2048,1408]{1,0:T(8,128)(2,1)}) %all-gather.12.cloned.1.call-update) | async-done | bytes 5767184 | tf_op jit(solution)/shard_map/all_gather | solution.py:172
  285.8 46.1 %all-gather.14.cloned.1.call-done = bf16[1408,2048]{1,0:T(8,128)(2,1)} async-done(((bf16[1408,256]{1,0:T(8,128)(2,1)}), bf16[1408,2048]{1,0:T(8,128)(2,1)}) %all-gather.14.cloned.1.call-update) | async-done | bytes 5767184 | tf_op jit(solution)/shard_map/all_gather | solution.py:174
  331.9 13.2 %convolution_convert_fusion.1 = bf16[512,2048]{1,0:T(8,128)(2,1)} fusion(bf16[1408,2048]{1,0:T(8,128)(2,1)} %all-gather.14.cloned.1.call-done, bf16[512,2048]{1,0:T(8,128)(2,1)S(1)} %copy-done.16, bf16[2048,1408]{1,0:T(8,128)(2,1)} %all-gather.12.cloned.1.call-done, f32[512,1408]{1,0:T(8,128)} %fusion.87), kind=kOutput, calls=%fused_computation.56 | convolution fusion | flops 5910953984 | bytes 18612224 | tf_op jit(solution)/shard_map/dot_general | solution.py:180
  345.9 15.4 %reduce-scatter.10.cloned.1.call-done = bf16[1024,3]{1,0:T(8,128)(2,1)} async-done(((bf16[4096,3]{1,0:T(8,128)(2,1)}), bf16[1024,3]{1,0:T(8,128)(2,1)}) %reduce-scatter.10.cloned.1.call-update) | async-done | bytes 6160
  361.2 1.7 copy.195
  362.9 21.0 %reduce-scatter.8.cloned.1.call-done = bf16[2,128,256]{2,1,0:T(8,128)(2,1)} async-done(((bf16[8,128,256]{2,1,0:T(8,128)(2,1)}), bf16[2,128,256]{2,1,0:T(8,128)(2,1)}) %reduce-scatter.8.cloned.1.call-update) | async-done | bytes 131088 | tf_op jit(solution)/shard_map/reduce_scatter | solution.py:146
  383.9 1.6 bitcast_convert_fusion
  385.5 43.0 %reduce-scatter.6.cloned.1.call-done = bf16[128,2048]{1,0:T(8,128)(2,1)} async-done(((bf16[512,2048]{1,0:T(8,128)(2,1)}), bf16[128,2048]{1,0:T(8,128)(2,1)}) %reduce-scatter.6.cloned.1.call-update) | async-done | bytes 524304 | tf_op jit(solution)/shard_map/reduce_scatter | solution.py:179
  428.5 2.0 fusion.55
  (129 shorter events, 16.6 us)
Async XLA Ops:
  7.2 137.7 %copy-start = (f32[256]{0:T(256)S(1)}, f32[256]{0:T(256)}, u32[]{:S(2)}) copy-start(f32[256]{0:T(256)} %param.30) | copy-start | bytes 3076
  7.2 14.6 %copy-start.6 = (bf16[1,128,4096]{2,1,0:T(8,128)(2,1)S(1)}, bf16[1,128,4096]{2,1,0:T(8,128)(2,1)}, u32[]{:S(2)}) copy-start(bf16[1,128,4096]{2,1,0:T(8,128)(2,1)} %param.22) | copy-start | bytes 3145732
  7.2 180.7 %all-gather.6.cloned.1.call-start = ((), (), s32[]{:S(2)}) async-start(), calls=%async_computation.3 | async-start | bytes 8650752 | tf_op jit(solution)/shard_map/all_gather | solution.py:162
  7.9 191.4 %all-gather.10.cloned.1.call-start = ((), (), s32[]{:S(2)}) async-start(), calls=%async_computation.5 | async-start | bytes 6488064 | tf_op jit(solution)/shard_map/all_gather | solution.py:171
  8.8 12.9 %collective-permute-start = (bf16[3,4096]{1,0:T(4,128)(2,1)S(1)}, bf16[3,4096]{1,0:T(4,128)(2,1)S(1)}, u32[]{:S(2)}, u32[]{:S(2)}) collective-permute-start(bf16[3,4096]{1,0:T(4,128)(2,1)S(1)} %slice_bitcast_fusion.2), channel_id=1, source_target_pairs={{0,1},{1,2},{2,3},{4,5},{5,6},{6,7},{8,9},{9,10},{10,11},{12,13},{... | collective-permute-start | bytes 73736 | tf_op jit(solution)/shard_map/ppermute | solution.py:22
  13.8 228.2 %all-gather.8.cloned.1.call-start = ((), (), s32[]{:S(2)}) async-start(), calls=%async_computation.4 | async-start | bytes 2621440 | tf_op jit(solution)/shard_map/all_gather | solution.py:175
  23.3 1.7 copy-start.2
  25.9 0.8 copy-start.11
  28.5 82.9 %slice-start = ((f32[128,4096]{1,0:T(8,128)}), f32[128,2048]{1,0:T(8,128)S(1)}, s32[]{:S(2)}) async-start(f32[128,4096]{1,0:T(8,128)} %copy-done.2), calls=%async_computation.11 | async-start | bytes 2097152 | tf_op jit(solution)/shard_map/slice | solution.py:127
  118.6 14.7 %collective-permute-start.1 = (bf16[8,128,256]{2,1,0:T(8,128)(2,1)}, bf16[8,128,256]{2,1,0:T(8,128)(2,1)}, u32[]{:S(2)}, u32[]{:S(2)}) collective-permute-start(bf16[8,128,256]{2,1,0:T(8,128)(2,1)} %convert_element_type.105), channel_id=1, source_target_pairs={{0,1},{1,2},{2,3},{4,5},{5,6},{6,7},{8,9},{9,10},{10,11},{12,13},{... | collective-permute-start | bytes 1572872 | tf_op jit(solution)/shard_map/ppermute | solution.py:22
  139.4 7.0 %copy-start.13 = (f32[16,8,8,128]{3,1,2,0:T(8,128)S(1)}, f32[16,8,8,128]{3,1,2,0:T(8,128)}, u32[]{:S(2)}) copy-start(f32[16,8,8,128]{3,1,2,0:T(8,128)} %get-tuple-element.370) | copy-start | bytes 1572868
  139.4 14.8 %collective-permute-start.2 = (bf16[8,128,256]{2,1,0:T(8,128)(2,1)}, bf16[8,128,256]{2,1,0:T(8,128)(2,1)}, u32[]{:S(2)}, u32[]{:S(2)}) collective-permute-start(bf16[8,128,256]{2,1,0:T(8,128)(2,1)} %convert_element_type.107), channel_id=1, source_target_pairs={{0,1},{1,2},{2,3},{4,5},{5,6},{6,7},{8,9},{9,10},{10,11},{12,13},{... | collective-permute-start | bytes 1572872 | tf_op jit(solution)/shard_map/ppermute | solution.py:22
  159.5 5.9 %copy-start.5 = (f32[16,8,8,128]{3,2,1,0:T(8,128)S(1)}, f32[16,8,8,128]{3,2,1,0:T(8,128)}, u32[]{:S(2)}) copy-start(f32[16,8,8,128]{3,2,1,0:T(8,128)} %copy.202) | copy-start | bytes 1572868
  159.5 7.0 %copy-start.12 = (f32[8,2,64,128]{3,0,2,1:T(8,128)S(1)}, f32[8,2,64,128]{3,0,2,1:T(8,128)}, u32[]{:S(2)}) copy-start(f32[8,2,64,128]{3,0,2,1:T(8,128)} %copy-done.11) | copy-start | bytes 1572868
  159.6 13.5 %collective-permute-start.3 = (bf16[8,128,256]{2,1,0:T(8,128)(2,1)S(1)}, bf16[8,128,256]{2,1,0:T(8,128)(2,1)S(1)}, u32[]{:S(2)}, u32[]{:S(2)}) collective-permute-start(bf16[8,128,256]{2,1,0:T(8,128)(2,1)S(1)} %convert_element_type.109), channel_id=1, source_target_pairs={{0,1},{1,2},{2,3},{4,5},{5,6},{6,7},{8,9},{9,10},{10,11},{12,13},{... | collective-permute-start | bytes 1572872 | tf_op jit(solution)/shard_map/ppermute | solution.py:22
  173.3 1.0 copy-start.3
  173.3 1.6 copy-start.4
  173.3 1.7 copy-start.8
  175.7 1.0 copy-start.9
  178.0 1.0 copy-start.3
  178.0 1.6 copy-start.4
  178.0 1.7 copy-start.8
  180.4 1.0 copy-start.9
  182.7 3.2 copy-start.10
  186.5 1.3 copy-start.14
  187.9 5.5 %copy-start.15 = (f32[2048]{0:T(1024)S(1)}, f32[2048]{0:T(1024)}, u32[]{:S(2)}) copy-start(f32[2048]{0:T(1024)} %param.32) | copy-start | bytes 24580
  193.3 2.9 copy-start.7
  194.3 91.5 %all-gather.12.cloned.1.call-start = ((), (), s32[]{:S(2)}) async-start(), calls=%async_computation.6 | async-start | bytes 6488064 | tf_op jit(solution)/shard_map/all_gather | solution.py:172
  194.9 137.0 %all-gather.14.cloned.1.call-start = ((), (), s32[]{:S(2)}) async-start(), calls=%async_computation.7 | async-start | bytes 6488064 | tf_op jit(solution)/shard_map/all_gather | solution.py:174
  195.5 165.7 %reduce-scatter.10.cloned.1.call-start = ((), (), s32[]{:S(2)}) async-start(), calls=%async_computation.10 | async-start | bytes 1310720
  198.0 185.9 %reduce-scatter.8.cloned.1.call-start = ((), (), s32[]{:S(2)}) async-start(), calls=%async_computation.9 | async-start | bytes 655360 | tf_op jit(solution)/shard_map/reduce_scatter | solution.py:146
  199.0 229.5 %reduce-scatter.6.cloned.1.call-start = ((), (), s32[]{:S(2)}) async-start(), calls=%async_computation.8 | async-start | bytes 2621440 | tf_op jit(solution)/shard_map/reduce_scatter | solution.py:179
  242.0 89.9 %copy-start.16 = (bf16[512,2048]{1,0:T(8,128)(2,1)S(1)}, bf16[512,2048]{1,0:T(8,128)(2,1)}, u32[]{:S(2)}) copy-start(bf16[512,2048]{1,0:T(8,128)(2,1)} %all-gather.8.cloned.1.call-done) | copy-start | bytes 6291460
  345.1 85.3 %copy-start.1 = (f32[256]{0:T(256)S(1)}, f32[256]{0:T(256)}, u32[]{:S(2)}) copy-start(f32[256]{0:T(256)} %param.30) | copy-start | bytes 3076
Sparse Core Ops, SparseCore 0:
  11.0 81.0 all-gather.5
  93.9 43.4 all-gather.9
  194.4 47.4 all-gather.7
  243.7 42.0 all-gather.11
  287.5 44.3 all-gather.13
  334.1 27.1 reduce-scatter.9
  363.6 20.2 reduce-scatter.7
  386.3 42.1 reduce-scatter.5
where the time goes:
time: 438 us; the launch traced here: 437 us
  waiting for transfers between devices  227 us (52%)
  other arithmetic  104 us (24%)
  matrix products  54 us (12%)
  starting transfers between devices  19.6 us (4%)
  local copies, waits for them, and re-layouts  16.8 us (4%)
  between operations  15.4 us (4%)
    another operation x4, other arithmetic, block_tables(): lax.linalg.triangular_solve(identity + couple, identity, left_side=True,...  80.2 us
    all_gather x1, waiting for transfers between devices, local(): down_full = lax.all_gather(w_down, 'req', axis=1, tiled=True)  46.1 us
    reduce_scatter x1, waiting for transfers between devices, local(): lax.psum_scatter(jnp.dot(inner_units, down_full, preferred_element_type=j...  43 us
    all_gather x1, waiting for transfers between devices, local(): shard_rows = lax.all_gather(normed, 'seq', axis=0, tiled=True)  42.7 us
    all_gather x1, waiting for transfers between devices, local(): lax.all_gather(w_up, 'req', axis=0, tiled=True)  35.4 us
    ppermute x4, waiting for transfers between devices, shifted(): lax.ppermute(value, axis, [(source, source + steps) for source in range(i...  22 us
    reduce_scatter x1, waiting for transfers between devices, local(): lax.psum_scatter(state_term.astype(jnp.bfloat16), 'seq', scatter_dimensio...  21 us
    ppermute x4, starting transfers between devices, shifted(): lax.ppermute(value, axis, [(source, source + steps) for source in range(i...  19.1 us
  transfers between devices with their start and end apart: 12, of which 9 were waited for; matrix products, arithmetic and copies ran while one was open for 39% of the time, Pallas kernels for 0%

commit v1 on v0

v1 whole, which is shorter than its diff:
```python
import functools

import jax
import jax.numpy as jnp
from jax import lax
from jax.experimental import pallas as pl
from jax.experimental.pallas import tpu as pltpu
from jax.sharding import PartitionSpec as P

HEADS = 8
DK = 128
DV = 256
CONV = 4
HK = HEADS * DK
EPS_NORM = 1e-05
EPS_UNIT = 1e-06
BF16 = jnp.bfloat16
F32 = jnp.float32
MIB = 1 << 20

VMEM = pl.BlockSpec(memory_space=pltpu.VMEM)
SMEM = pl.BlockSpec(memory_space=pltpu.SMEM)
ANY = pl.BlockSpec(memory_space=pl.ANY)


def dot(a, b):
    return jnp.dot(a.astype(BF16), b.astype(BF16), preferred_element_type=F32)


def dot_nt(a, b):
    return lax.dot_general(
        a.astype(BF16), b.astype(BF16), (((1,), (1,)), ((), ())), preferred_element_type=F32
    )


def silu(v):
    return v / (1.0 + jnp.exp(-v))


def shift(value, axis, count, steps):
    return lax.ppermute(value, axis, [(i, (i + steps) % count) for i in range(count)])


def flip(value, bits):
    return lax.ppermute(value, "req", [(i, i ^ bits) for i in range(lax.axis_size("req"))])


def cubic():
    return lax.axis_size("req") == 8


def gather_req(block, axis):
    if not cubic():
        return [lax.all_gather(block, "req", axis=axis, tiled=True)]
    half = block.shape[axis] // 2
    by_two, by_four = flip(block, 2), flip(block, 4)
    low = flip(lax.slice_in_dim(by_two, 0, half, axis=axis), 4)
    high = flip(lax.slice_in_dim(by_four, half, 2 * half, axis=axis), 2)
    mine = [[block], [by_two], [by_four], [low, high]]
    theirs = [[flip(part, 1) for part in parts] for parts in mine]
    out = []
    for a, b in zip(mine, theirs):
        out += [a, b]
    return out


def delta_kernel(count, heads, piece, *refs):
    x_refs, small_refs = refs[:count], refs[count : 2 * count]
    where, taps, gain = refs[2 * count : 2 * count + 3]
    attn, state, xs, bs = refs[2 * count + 3 :]
    me = where[0]
    q0, k0, v0 = 0, heads * DK, 2 * heads * DK
    xs[pl.ds(0, 8), :] = jnp.zeros((8, xs.shape[1]), F32)
    for k in range(count):
        c = lax.rem(me - k + count, count)
        xs[pl.ds(pl.multiple_of(8 + c * piece, 8), piece), :] = x_refs[k][...].astype(F32)
        bs[c] = small_refs[k][0:8, :]

    def activated(c, col, width):
        total = None
        for i in range(CONV):
            rows = xs[pl.ds(8 - (CONV - 1) + i + c * piece, piece), pl.ds(col, width)]
            term = taps[i : i + 1, col : col + width] * rows
            total = term if total is None else total + term
        return silu(total)

    def unit(v):
        return v * lax.rsqrt(jnp.sum(v * v, axis=-1, keepdims=True) + EPS_UNIT)

    row = lax.broadcasted_iota(jnp.int32, (piece, piece), 0)
    col = lax.broadcasted_iota(jnp.int32, (piece, piece), 1)
    upper = (row <= col).astype(F32)
    pairs = [(c, h) for c in range(count) for h in range(heads)]
    tabs = {}
    for c in range(count):
        rows = bs[c]
        cum = jnp.dot(rows, upper, precision=lax.Precision.HIGHEST, preferred_element_type=F32)
        wide = jnp.concatenate([cum, rows, jnp.zeros((piece - 16, piece), F32)], axis=0)
        tall = wide.T
        for h in range(heads):
            g_row = cum[heads + h : heads + h + 1, :]
            g_col = tall[:, heads + h : heads + h + 1]
            b_col = tall[:, 8 + h : 9 + h]
            tabs[c, h] = (g_row, g_col, b_col)
    couple, solve, first, second, ends = {}, {}, {}, {}, {}
    for c, h in pairs:
        g_row, g_col, b_col = tabs[c, h]
        q = unit(activated(c, q0 + h * DK, DK)) * DK ** (-0.5)
        k = unit(activated(c, k0 + h * DK, DK))
        v = activated(c, v0 + h * DV, DV)
        inner = dot_nt(jnp.concatenate([k, q], axis=0), k)
        spread = jnp.exp(jnp.where(row >= col, g_col - g_row, -1e30))
        couple[c, h] = jnp.where(row > col, inner[:piece] * spread * b_col, 0.0)
        grown = jnp.exp(g_col)
        g_end = g_row[:, piece - 1 : piece]
        to_end = jnp.exp(g_end - g_col) * k
        solve[c, h] = jnp.concatenate([b_col * v, (b_col * grown) * k], axis=1).astype(BF16)
        first[c, h] = (grown * q).astype(BF16)
        second[c, h] = jnp.concatenate([inner[piece:] * spread, to_end.T], axis=0).astype(BF16)
        ends[c, h] = jnp.exp(g_end)
    inverse = {}
    for p in pairs:
        inverse[p] = jnp.where(row == col, 1.0, 0.0) - jnp.where(
            (row >> 1) == (col >> 1), couple[p], 0.0
        )
    level = 1
    while (2 << level) <= piece:
        keep = ((row >> (level + 1)) == (col >> (level + 1))) & ((row >> level) != (col >> level))
        left = {p: dot(inverse[p], jnp.where(keep, couple[p], 0.0)) for p in pairs}
        for p in pairs:
            inverse[p] = inverse[p] - dot(left[p], inverse[p])
        level += 1
    solved = {p: dot(inverse[p], solve[p]) for p in pairs}
    running = [None] * heads
    for c in range(count):
        slot = lax.rem(c - me + count, count)
        for h in range(heads):
            values, weighted = solved[c, h][:, :DV], solved[c, h][:, DV:]
            if c == 0:
                corrected = values
                out = None
            else:
                both = dot(
                    jnp.concatenate([weighted.astype(BF16), first[c, h]], axis=0), running[h]
                )
                corrected = values - both[:piece]
                out = both[piece:]
            both = dot(second[c, h], corrected)
            out = both[:piece] if out is None else out + both[:piece]
            running[h] = both[piece:] if c == 0 else ends[c, h] * running[h] + both[piece:]
            scale = lax.rsqrt(jnp.mean(out * out, axis=-1, keepdims=True) + EPS_NORM)
            attn[slot, :, h * DV : (h + 1) * DV] = (out * scale * gain[...]).astype(BF16)
    for h in range(heads):
        state[h] = running[h]


def delta(xs, smalls, where, taps, gain, heads, piece):
    count = len(xs)
    width = heads * (2 * DK + DV)
    return pl.pallas_call(
        functools.partial(delta_kernel, count, heads, piece),
        out_shape=(
            jax.ShapeDtypeStruct((count, piece, heads * DV), BF16),
            jax.ShapeDtypeStruct((heads, DK, DV), F32),
        ),
        in_specs=[VMEM] * (2 * count) + [SMEM, VMEM, VMEM],
        out_specs=(VMEM, VMEM),
        scratch_shapes=[
            pltpu.VMEM((8 + count * piece, width), F32),
            pltpu.VMEM((count, 8, piece), F32),
        ],
        compiler_params=pltpu.CompilerParams(vmem_limit_bytes=40 * MIB),
        cost_estimate=pl.CostEstimate(flops=int(4e9), bytes_accessed=4 * MIB, transcendentals=0),
        name="delta_rule",
    )(*xs, *smalls, where, taps, gain)


def project_kernel(count, cube, n_pieces, *refs):
    a_refs = refs[:count]
    where, gate, residual, gain = refs[count : count + 4]
    w_refs = refs[count + 4 : count + 4 + n_pieces]
    stream_out, normed_out, mixed, stream, weights, sems = refs[count + 4 + n_pieces :]
    me, req = where[0], where[1]
    depth = w_refs[0].shape[0]
    copies = []
    for j in range(n_pieces):
        copy = pltpu.make_async_copy(w_refs[j], weights.at[j], sems.at[j])
        copy.start()
        copies.append(copy)
    width = a_refs[0].shape[1]
    for k in range(count):
        cols = pl.ds(pl.multiple_of(lax.rem(me - k + count, count) * width, width), width)
        opened = silu(gate[:, cols].astype(F32))
        mixed[:, cols] = (a_refs[k][...].astype(F32) * opened).astype(BF16)
    total = residual[...].astype(F32)
    for j in range(n_pieces):
        copies[j].wait()
        block = (req ^ j) if cube else j
        lhs = mixed[:, pl.ds(pl.multiple_of(block * depth, depth), depth)]
        total += jnp.dot(lhs, weights[j], preferred_element_type=F32)
    rounded = total.astype(BF16)
    wide = rounded.astype(F32)
    scale = lax.rsqrt(jnp.mean(wide * wide, axis=-1, keepdims=True) + EPS_NORM)
    if not cube:
        stream_out[...] = rounded
        normed_out[...] = (wide * scale * gain[...]).astype(BF16)
        return
    stream[...] = rounded
    for j in range(n_pieces):
        cols = pl.ds(pl.multiple_of((req ^ j) * depth, depth), depth)
        part = stream[:, cols]
        stream_out[:, j * depth : (j + 1) * depth] = part
        normed_out[:, j * depth : (j + 1) * depth] = (
            part.astype(F32) * scale * gain[:, cols]
        ).astype(BF16)


def project(blocks, where, gate, residual, gain, pieces, cube):
    rows, width = residual.shape
    count, n_pieces = len(blocks), len(pieces)
    return pl.pallas_call(
        functools.partial(project_kernel, count, cube, n_pieces),
        out_shape=(jax.ShapeDtypeStruct((rows, width), BF16),) * 2,
        in_specs=[VMEM] * count + [SMEM, VMEM, VMEM, VMEM] + [ANY] * n_pieces,
        out_specs=(VMEM, VMEM),
        scratch_shapes=[
            pltpu.VMEM((rows, width), BF16),
            pltpu.VMEM((rows, width), BF16),
            pltpu.VMEM((n_pieces,) + pieces[0].shape, BF16),
            pltpu.SemaphoreType.DMA((n_pieces,)),
        ],
        compiler_params=pltpu.CompilerParams(vmem_limit_bytes=32 * MIB),
        cost_estimate=pl.CostEstimate(
            flops=2 * rows * width * width, bytes_accessed=8 * MIB, transcendentals=0
        ),
        name="output_projection",
    )(*blocks, where, gate, residual, gain, *pieces)


def parts_of(pieces):
    flat, place = [], []
    for j, piece in enumerate(pieces):
        for number, part in enumerate(piece):
            flat.append(part)
            place.append((j, number))
    return flat, place


def forward_kernel(count, places, axes, n_pieces, *refs):
    x_refs = refs[:count]
    refs = refs[count:]
    groups = []
    for place in places:
        groups.append(refs[: len(place)])
        refs = refs[len(place) :]
    outs = refs[:count]
    x, inner, *bufs = refs[count : count + 5]
    sems = refs[count + 5]
    rows = x_refs[0].shape[0]
    waits = []
    for g, (place, group, buf, axis) in enumerate(zip(places, groups, bufs, axes)):
        wait = [[] for _ in range(n_pieces)]
        for (j, number), ref in zip(place, group):
            size = ref.shape[axis]
            span = pl.ds(number * size, size)
            target = buf.at[j, span, :] if axis == 0 else buf.at[j, :, span]
            copy = pltpu.make_async_copy(ref, target, sems.at[g, 2 * j + number])
            wait[j].append(copy)
        waits.append(wait)
    for j in range(n_pieces):
        for wait in waits[:2]:
            for copy in wait[j]:
                copy.start()
    for j in range(n_pieces):
        for copy in waits[2][j]:
            copy.start()
    for k in range(count):
        x[k * rows : (k + 1) * rows, :] = x_refs[k][...]
    depth = bufs[0].shape[1]
    gate = up = None
    for j in range(n_pieces):
        for wait in waits[:2]:
            for copy in wait[j]:
                copy.wait()
        lhs = x[:, j * depth : (j + 1) * depth]
        gate_term = jnp.dot(lhs, bufs[0][j], preferred_element_type=F32)
        up_term = jnp.dot(lhs, bufs[1][j], preferred_element_type=F32)
        gate = gate_term if gate is None else gate + gate_term
        up = up_term if up is None else up + up_term
    inner[...] = (silu(gate) * up).astype(BF16)
    width = bufs[2].shape[2]
    for j in range(n_pieces):
        for copy in waits[2][j]:
            copy.wait()
        term = jnp.dot(inner[...], bufs[2][j], preferred_element_type=F32).astype(BF16)
        for k in range(count):
            outs[k][:, j * width : (j + 1) * width] = term[k * rows : (k + 1) * rows]


def forward(xs, gates, ups, downs):
    count, rows, width = len(xs), *xs[0].shape
    lists = [gates, ups, downs]
    axes = (0, 0, 1)
    flats, places = zip(*[parts_of(pieces) for pieces in lists])
    n_pieces = len(gates)
    bufs = []
    for pieces, axis in zip(lists, axes):
        shape = list(pieces[0][0].shape)
        shape[axis] = sum(part.shape[axis] for part in pieces[0])
        bufs.append(pltpu.VMEM((n_pieces, *shape), BF16))
    hidden = gates[0][0].shape[1]
    return pl.pallas_call(
        functools.partial(forward_kernel, count, places, axes, n_pieces),
        out_shape=(jax.ShapeDtypeStruct((rows, width), BF16),) * count,
        in_specs=[VMEM] * count + [ANY] * sum(len(flat) for flat in flats),
        out_specs=(VMEM,) * count,
        scratch_shapes=[
            pltpu.VMEM((count * rows, width), BF16),
            pltpu.VMEM((count * rows, hidden), BF16),
            *bufs,
            pltpu.SemaphoreType.DMA((3, 2 * n_pieces)),
        ],
        compiler_params=pltpu.CompilerParams(vmem_limit_bytes=48 * MIB),
        cost_estimate=pl.CostEstimate(
            flops=6 * count * rows * width * hidden, bytes_accessed=20 * MIB, transcendentals=0
        ),
        name="feed_forward",
    )(*xs, *[part for flat in flats for part in flat])


def finish_kernel(count, cube, n_blocks, *refs):
    y_refs = refs[:count]
    where, stream, out = refs[count:]
    rows, width = stream.shape
    req, alive = where[1], where[2]
    position = lax.broadcasted_iota(jnp.int32, (rows, 1), 0)
    size = width // n_blocks
    for j in range(n_blocks):
        span = slice(j * size, (j + 1) * size)
        total = stream[:, span].astype(F32)
        for y in y_refs:
            total += y[:, span].astype(F32)
        block = (req ^ j) if cube else j
        out[:, pl.ds(pl.multiple_of(block * size, size), size)] = jnp.where(
            position < alive, total, 0.0
        ).astype(BF16)


def finish(ys, where, stream, cube):
    count = len(ys)
    n_blocks = 8 if cube else 1
    return pl.pallas_call(
        functools.partial(finish_kernel, count, cube, n_blocks),
        out_shape=jax.ShapeDtypeStruct(stream.shape, BF16),
        in_specs=[VMEM] * count + [SMEM, VMEM],
        out_specs=VMEM,
        name="last_sum",
    )(*ys, where, stream)


def local(
    qkv_proj,
    gate_proj,
    residual,
    log_decay,
    beta_logit,
    lengths,
    slot_request,
    conv_weight,
    norm_gain,
    out_weight,
    mlp_gain,
    w_gate,
    w_up,
    w_down,
):
    me = lax.axis_index("seq")
    req = lax.axis_index("req")
    count = lax.axis_size("seq")
    cube = cubic()
    piece = qkv_proj.shape[1]
    channels = qkv_proj.shape[2]
    heads = HEADS // count
    ids = jnp.arange(slot_request.shape[0], dtype=jnp.int32)
    request = jnp.sum(jnp.where(ids == req, slot_request, 0))
    length = jnp.sum(jnp.where(ids == request, lengths, 0))
    alive = length - me * piece
    where = jnp.stack([me, req, alive]).astype(jnp.int32)
    local_position = jnp.arange(piece, dtype=jnp.int32)
    live = local_position < alive
    tokens = qkv_proj[0]

    beta = jax.nn.sigmoid(beta_logit[0].astype(F32)) * live[:, None]
    decay = jnp.where(live[:, None], log_decay[0], 0.0)
    targets = alive - (CONV - 1) + jnp.arange(CONV - 1, dtype=jnp.int32)
    select = (local_position[None, :] == targets[:, None]).astype(BF16)
    edge = jnp.dot(select, tokens, preferred_element_type=F32)
    block = channels // count
    edge_rows = (CONV - 1) * block // piece

    def share(target):
        start = target * heads
        parts = [
            lax.dynamic_slice_in_dim(tokens, start * DK, heads * DK, axis=1),
            lax.dynamic_slice_in_dim(tokens, HK + start * DK, heads * DK, axis=1),
            lax.dynamic_slice_in_dim(tokens, 2 * HK + start * DV, heads * DV, axis=1),
        ]
        strength = lax.dynamic_slice_in_dim(beta, start, heads, axis=1).T
        slope = lax.dynamic_slice_in_dim(decay, start, heads, axis=1).T
        pad = jnp.zeros((8 - 2 * heads, piece), F32)
        rim = lax.dynamic_slice_in_dim(edge, target * block, block, axis=1)
        small = jnp.concatenate([strength, slope, pad, rim.reshape(edge_rows, piece)], axis=0)
        return jnp.concatenate(parts, axis=1), small

    xs, smalls = [], []
    for k in range(count):
        big, small = share(lax.rem(me + k, count))
        if k:
            big, small = shift(big, "seq", count, k), shift(small, "seq", count, k)
        xs.append(big)
        smalls.append(small)
    conv_edge = sum(small[8:] for small in smalls).reshape(CONV - 1, block).astype(BF16)
    start = me * heads
    taps = jnp.concatenate(
        [
            lax.dynamic_slice_in_dim(conv_weight, start * DK, heads * DK, axis=1),
            lax.dynamic_slice_in_dim(conv_weight, HK + start * DK, heads * DK, axis=1),
            lax.dynamic_slice_in_dim(conv_weight, 2 * HK + start * DV, heads * DV, axis=1),
        ],
        axis=1,
    )
    attn, state = delta(xs, smalls, where, taps, norm_gain[None, :], heads, piece)

    if cube:
        rows = out_weight.shape[0]
        ring = [out_weight] + [shift(out_weight, "seq", count, k) for k in range(1, count)]
        line = jnp.zeros((count,) + out_weight.shape, BF16)
        for k, part in enumerate(ring):
            line = lax.dynamic_update_index_in_dim(line, part, lax.rem(me - k + count, count), 0)
        line = line.reshape(count * rows, -1)
        out_pieces = [
            parts[0] if len(parts) == 1 else jnp.concatenate(parts, axis=0)
            for parts in gather_req(line, 0)
        ]
        gates, ups, downs = gather_req(w_gate, 0), gather_req(w_up, 0), gather_req(w_down, 1)
    else:
        out_pieces = [lax.all_gather(out_weight, ("req", "seq"), axis=0, tiled=True)]
        gates, ups, downs = [gather_req(w_gate, 0)], [gather_req(w_up, 0)], [gather_req(w_down, 1)]

    blocks = [attn[0]] + [shift(attn[k], "seq", count, k) for k in range(1, count)]
    stream, normed = project(
        blocks, where, gate_proj[0], residual[0], mlp_gain[None, :], out_pieces, cube
    )
    tokens_in = [normed] + [shift(normed, "seq", count, k) for k in range(1, count)]
    ys = forward(tokens_in, gates, ups, downs)
    back = [ys[0]] + [shift(ys[k], "seq", count, count - k) for k in range(1, count)]
    hidden = finish(back, where, stream, cube)
    return hidden[None], state[None], conv_edge[None]


def solution(mesh):
    return jax.shard_map(
        local,
        mesh=mesh,
        in_specs=(
            P("req", "seq", None),
            P("req", "seq", None),
            P("req", "seq", None),
            P("req", "seq", None),
            P("req", "seq", None),
            P(),
            P(),
            P(),
            P(),
            P(("req", "seq"), None),
            P(),
            P("req", "seq"),
            P("req", "seq"),
            P("seq", "req"),
        ),
        out_specs=(P("req", "seq", None), P("req", "seq", None, None), P("req", None, "seq")),
        check_vma=False,
    )
```

time: 438 us -> 300 us (0.68)
  other arithmetic: 104 us -> 2.41 us
  starting transfers between devices: 19.6 us -> 81.5 us
  waiting for transfers between devices: 227 us -> 169 us
  matrix products: 54 us -> 0.3 us
  Pallas kernels: 0 us -> 33.7 us
  between operations: 15.4 us -> 2.01 us
  local copies, waits for them, and re-layouts: 16.8 us -> 10.5 us
    ppermute x4 -> x54, waiting for transfers between devices: 22 us -> 169 us  [the longest x18 86.4 us: shift(): lax.ppermute(value, axis, [(i, (i + steps) % count) for i in range(count)])]
    all_gather x5 -> x0, waiting for transfers between devices: 124 us -> none  [the longest x1 46.1 us: local(): down_full = lax.all_gather(w_down, 'req', axis=1, tiled=True)]
    another operation x5 -> x1, other arithmetic: 80.6 us -> 0.08 us  [local(): where = jnp.stack([me, req, alive]).astype(jnp.int32)]
    reduce_scatter x2 -> x0, waiting for transfers between devices: 64 us -> none  [the longest x1 43 us: local(): lax.psum_scatter(jnp.dot(inner_units, down_full, preferred_element_type=j...]
    ppermute x4 -> x54, starting transfers between devices: 19.1 us -> 81.5 us  [the longest x18 57.8 us: shift(): lax.ppermute(value, axis, [(i, (i + steps) % count) for i in range(count)])]
    dot_general x28 -> x1, matrix products: 52 us -> 0.3 us  [local(): edge = jnp.dot(select, tokens, preferred_element_type=F32)]
    pallas_call x0 -> x4, Pallas kernels: none -> 33.7 us  [the longest x1 21 us: forward(): pl.pallas_call(functools.partial(forward_kernel, count, places, axes, n_p...]
    unnamed x9 -> x0, waiting for transfers between devices: 17.2 us -> none
  transfers between devices with their start and end apart: 12 -> 54, of which waited for: 9 -> 21; matrix products, arithmetic and copies ran while one was open for 39% -> 2% of each run, Pallas kernels for 0% -> 3%
where the time goes in v1:
time: 300 us; the launch traced here: 299 us
  waiting for transfers between devices  169 us (56%)
  starting transfers between devices  81.5 us (27%)
  Pallas kernels  33.7 us (11%)
  local copies, waits for them, and re-layouts  10.5 us (4%)
    ppermute x18, waiting for transfers between devices, shift(): lax.ppermute(value, axis, [(i, (i + steps) % count) for i in range(count)])  86.4 us
    ppermute x36, waiting for transfers between devices, flip(): lax.ppermute(value, 'req', [(i, i ^ bits) for i in range(lax.axis_size('r...  82.4 us
    ppermute x18, starting transfers between devices, shift(): lax.ppermute(value, axis, [(i, (i + steps) % count) for i in range(count)])  57.8 us
    ppermute x36, starting transfers between devices, flip(): lax.ppermute(value, 'req', [(i, i ^ bits) for i in range(lax.axis_size('r...  23.7 us
    pallas_call x1, Pallas kernels, forward(): pl.pallas_call(functools.partial(forward_kernel, count, places, axes, n_p...  21 us
    pallas_call x1, Pallas kernels, delta(): pl.pallas_call(functools.partial(delta_kernel, count, heads, piece), out_...  6.39 us
  transfers between devices with their start and end apart: 54, of which 21 were waited for; matrix products, arithmetic and copies ran while one was open for 2% of the time, Pallas kernels for 3%

profile of v1, /device:TPU:0, one launch (start us, length us, event | category | flops | bytes accessed | tf_op | source)
XLA Modules:
  0.0 299.3 jit_solution(9243015858493784172)
XLA Ops:
  0.7 1.2 dynamic-slice_bitcast_fusion
  2.2 5.1 %collective-permute-start.2 = (bf16[128,1024]{1,0:T(8,128)(2,1)S(1)}, bf16[128,1024]{1,0:T(8,128)(2,1)S(1)}, u32[]{:S(2)}, u32[]{:S(2)}) collective-permute-start(bf16[128,1024]{1,0:T(8,128)(2,1)S(1)} %pad_maximum_fusion.5), channel_id=1, source_target_pairs={{0,3},{1,0},{2,1},{3,2},{4,7},{5,4},{6,5},{7,6},{8,11},{9,8},{10,9... | collective-permute-start | bytes 786440 | tf_op jit(solution)/shard_map/ppermute | solution.py:41
  7.3 0.6 fusion.12
  8.0 1.3 fusion.13
  10.7 1.0 collective-permute-start.4
  11.7 2.0 collective-permute-start.1
  13.8 1.5 collective-permute-start
  15.3 0.7 constant_dynamic-slice_fusion
  16.0 0.7 constant_dynamic-slice_fusion.2
  16.7 2.5 collective-permute-start.5
  19.3 0.7 collective-permute-start.9
  19.9 6.6 %collective-permute-done.5.refs_7_ = f32[32,128]{1,0:T(8,128)S(1)} collective-permute-done((f32[32,128]{1,0:T(8,128)S(1)}, f32[32,128]{1,0:T(8,128)S(1)}, u32[]{:S(2)}, u32[]{:S(2)}) %collective-permute-start.5) | collective-permute-done | bytes 16416 | tf_op jit(solution)/shard_map/ppermute | solution.py:41
  26.5 11.8 %collective-permute-start.10 = (bf16[64,2048]{1,0:T(8,128)(2,1)S(1)}, bf16[64,2048]{1,0:T(8,128)(2,1)S(1)}, u32[]{:S(2)}, u32[]{:S(2)}) collective-permute-start(bf16[64,2048]{1,0:T(8,128)(2,1)S(1)} %copy-done.12), channel_id=1, source_target_pairs={{0,2},{1,3},{2,0},{3,1},{4,6},{5,7},{6,4},{7,5},{8,10},{9,11},{10,... | collective-permute-start | bytes 786440 | tf_op jit(solution)/shard_map/ppermute | solution.py:41
  38.4 3.4 %collective-permute-start.11 = (bf16[64,2048]{1,0:T(8,128)(2,1)S(1)}, bf16[64,2048]{1,0:T(8,128)(2,1)S(1)}, u32[]{:S(2)}, u32[]{:S(2)}) collective-permute-start(bf16[64,2048]{1,0:T(8,128)(2,1)S(1)} %copy-done.12), channel_id=1, source_target_pairs={{0,3},{1,0},{2,1},{3,2},{4,7},{5,4},{6,5},{7,6},{8,11},{9,8},{10,9... | collective-permute-start | bytes 786440 | tf_op jit(solution)/shard_map/ppermute | solution.py:41
  41.7 1.5 collective-permute-start.25
  43.2 1.5 collective-permute-start.27
  44.8 6.4 %delta_rule.1 = (bf16[4,128,512]{2,1,0:T(8,128)(2,1)S(1)}, f32[2,128,256]{2,1,0:T(8,128)}) custom-call(bf16[128,1024]{1,0:T(8,128)(2,1)S(1)} %pad_maximum_fusion.2.refs_0_, bf16[128,1024]{1,0:T(8,128)(2,1)S(1)} %collective-permute-done.refs_1_, bf16[128,1024]{1,0:T(8,128)(2,1)S(1)} %collective-permute-done.1.refs_2_, ...), custom_call_target="tpu_custom_call" | custom-call | flops 4000000000 | bytes 4194304 | tf_op jit(solution)/shard_map/delta_rule/pallas_call | solution.py:160
  51.1 0.7 slice_bitcast_fusion
  51.9 0.6 collective-permute-start.7
  52.6 8.6 %collective-permute-start.8 = (bf16[128,512]{1,0:T(8,128)(2,1)}, bf16[128,512]{1,0:T(8,128)(2,1)S(1)}, u32[]{:S(2)}, u32[]{:S(2)}) collective-permute-start(bf16[128,512]{1,0:T(8,128)(2,1)} %get-tuple-element.31), channel_id=1, source_target_pairs={{0,3},{1,0},{2,1},{3,2},{4,7},{5,4},{6,5},{7,6},{8,11},{9,8},{10,9... | collective-permute-start | bytes 393224 | tf_op jit(solution)/shard_map/ppermute | solution.py:41
  61.3 1.6 collective-permute-start.34
  62.9 1.5 collective-permute-start.36
  64.9 1.5 collective-permute-start.43
  66.4 1.5 collective-permute-start.45
  68.1 1.3 slice.62
  69.4 11.2 %collective-permute-done.34.refs_16_ = bf16[256,1408]{1,0:T(8,128)(2,1)S(1)} collective-permute-done((bf16[256,1408]{1,0:T(8,128)(2,1)}, bf16[256,1408]{1,0:T(8,128)(2,1)S(1)}, u32[]{:S(2)}, u32[]{:S(2)}) %collective-permute-start.34) | collective-permute-done | bytes 720928 | tf_op jit(solution)/shard_map/ppermute | solution.py:45
  80.7 1.5 collective-permute-done.36.refs_18_
  82.2 12.2 %collective-permute-done.43.refs_26_ = bf16[1408,256]{1,0:T(8,128)(2,1)S(1)} collective-permute-done((bf16[1408,256]{1,0:T(8,128)(2,1)}, bf16[1408,256]{1,0:T(8,128)(2,1)S(1)}, u32[]{:S(2)}, u32[]{:S(2)}) %collective-permute-start.43) | collective-permute-done | bytes 720928 | tf_op jit(solution)/shard_map/ppermute | solution.py:45
  94.4 1.5 collective-permute-start.29
  95.9 1.5 collective-permute-start.30
  97.4 0.6 collective-permute-start.13
  98.0 1.4 collective-permute-start.15
  99.5 0.7 collective-permute-start.38
  100.2 5.5 %collective-permute-done.29.refs_10_ = bf16[128,1408]{1,0:T(8,128)(2,1)S(1)} collective-permute-done((bf16[128,1408]{1,0:T(8,128)(2,1)S(1)}, bf16[128,1408]{1,0:T(8,128)(2,1)S(1)}, u32[]{:S(2)}, u32[]{:S(2)}) %collective-permute-start.29) | collective-permute-done | bytes 360480 | tf_op jit(solution)/shard_map/ppermute | solution.py:45
  105.7 1.5 collective-permute-start.39
  107.3 26.2 %collective-permute-done.38.refs_20_ = bf16[128,1408]{1,0:T(8,128)(2,1)S(1)} collective-permute-done((bf16[128,1408]{1,0:T(8,128)(2,1)S(1)}, bf16[128,1408]{1,0:T(8,128)(2,1)S(1)}, u32[]{:S(2)}, u32[]{:S(2)}) %collective-permute-start.38) | collective-permute-done | bytes 360480 | tf_op jit(solution)/shard_map/ppermute | solution.py:45
  133.5 1.5 collective-permute-start.47
  135.1 1.3 collective-permute-start.48
  136.3 5.2 %collective-permute-done.47.refs_30_ = bf16[1408,128]{1,0:T(8,128)(2,1)S(1)} collective-permute-done((bf16[1408,128]{1,0:T(8,128)(2,1)S(1)}, bf16[1408,128]{1,0:T(8,128)(2,1)S(1)}, u32[]{:S(2)}, u32[]{:S(2)}) %collective-permute-start.47) | collective-permute-done | bytes 360480 | tf_op jit(solution)/shard_map/ppermute | solution.py:45
  141.5 1.3 collective-permute-done.48.refs_31_
  144.0 0.6 collective-permute-done.32.refs_13_
  145.8 4.3 %collective-permute-done.49.refs_32_ = bf16[1408,128]{1,0:T(8,128)(2,1)S(1)} collective-permute-done((bf16[1408,128]{1,0:T(8,128)(2,1)S(1)}, bf16[1408,128]{1,0:T(8,128)(2,1)S(1)}, u32[]{:S(2)}, u32[]{:S(2)}) %collective-permute-start.49) | collective-permute-done | bytes 360480 | tf_op jit(solution)/shard_map/ppermute | solution.py:45
  150.1 0.7 collective-permute-start.17
  150.8 1.0 collective-permute-start.18
  151.8 12.3 %collective-permute-done.17 = bf16[128,2048]{1,0:T(8,128)(2,1)S(1)} collective-permute-done((bf16[128,2048]{1,0:T(8,128)(2,1)S(1)}, bf16[128,2048]{1,0:T(8,128)(2,1)S(1)}, u32[]{:S(2)}, u32[]{:S(2)}) %collective-permute-start.17) | collective-permute-done | bytes 524320 | tf_op jit(solution)/shard_map/ppermute | solution.py:45
  164.6 0.6 collective-permute-start.28
  166.1 0.6 collective-permute-done.20
  167.0 3.5 %output_projection.1 = (bf16[128,2048]{1,0:T(8,128)(2,1)S(1)}, bf16[128,2048]{1,0:T(8,128)(2,1)S(1)}) custom-call(bf16[128,512]{1,0:T(8,128)(2,1)S(1)} %get-tuple-element.34.refs_0_, bf16[128,512]{1,0:T(8,128)(2,1)S(1)} %collective-permute-done.6.refs_1_, bf16[128,512]{1,0:T(8,128)(2,1)S(1)} %collective-permute-done.7.refs_2_, ...), custom_call_target="tpu_custom_call" | custom-call | flops 1073741824 | bytes 8388608 | tf_op jit(solution)/shard_map/output_projection/pallas_call | solution.py:221
  170.5 0.8 copy-done.2
  171.3 4.6 %collective-permute-start.21 = (bf16[128,2048]{1,0:T(8,128)(2,1)S(1)}, bf16[128,2048]{1,0:T(8,128)(2,1)S(1)}, u32[]{:S(2)}, u32[]{:S(2)}) collective-permute-start(bf16[128,2048]{1,0:T(8,128)(2,1)S(1)} %get-tuple-element.12.refs_0_), channel_id=1, source_target_pairs={{0,1},{1,2},{2,3},{3,0},{4,5},{5,6},{6,7},{7,4},{8,9},{9,10},{10,1... | collective-permute-start | bytes 1572872 | tf_op jit(solution)/shard_map/ppermute | solution.py:41
  176.0 3.6 %collective-permute-start.22 = (bf16[128,2048]{1,0:T(8,128)(2,1)S(1)}, bf16[128,2048]{1,0:T(8,128)(2,1)S(1)}, u32[]{:S(2)}, u32[]{:S(2)}) collective-permute-start(bf16[128,2048]{1,0:T(8,128)(2,1)S(1)} %get-tuple-element.12.refs_0_), channel_id=1, source_target_pairs={{0,2},{1,3},{2,0},{3,1},{4,6},{5,7},{6,4},{7,5},{8,10},{9,11},{10,... | collective-permute-start | bytes 1572872 | tf_op jit(solution)/shard_map/ppermute | solution.py:41
  179.6 12.3 %collective-permute-done.21.refs_1_ = bf16[128,2048]{1,0:T(8,128)(2,1)S(1)} collective-permute-done((bf16[128,2048]{1,0:T(8,128)(2,1)S(1)}, bf16[128,2048]{1,0:T(8,128)(2,1)S(1)}, u32[]{:S(2)}, u32[]{:S(2)}) %collective-permute-start.21) | collective-permute-done | bytes 524320 | tf_op jit(solution)/shard_map/ppermute | solution.py:41
  191.9 22.1 %collective-permute-done.22.refs_2_ = bf16[128,2048]{1,0:T(8,128)(2,1)S(1)} collective-permute-done((bf16[128,2048]{1,0:T(8,128)(2,1)S(1)}, bf16[128,2048]{1,0:T(8,128)(2,1)S(1)}, u32[]{:S(2)}, u32[]{:S(2)}) %collective-permute-start.22) | collective-permute-done | bytes 524320 | tf_op jit(solution)/shard_map/ppermute | solution.py:41
  214.0 0.7 copy-done.32
  214.8 0.8 copy-done.33
  215.6 21.0 %feed_forward.1 = (bf16[128,2048]{1,0:T(8,128)(2,1)S(1)}, bf16[128,2048]{1,0:T(8,128)(2,1)S(1)}, bf16[128,2048]{1,0:T(8,128)(2,1)S(1)}, bf16[128,2048]{1,0:T(8,128)(2,1)}) custom-call(bf16[128,2048]{1,0:T(8,128)(2,1)} %copy-done.6, bf16[128,2048]{1,0:T(8,128)(2,1)} %copy-done.31, bf16[128,2048]{1,0:T(8,128)(2,1)} %copy-done.32, ...), custom_call_target="tpu_custom_call" | custom-call | flops 8858370048 | bytes 20971520 | tf_op jit(solution)/shard_map/feed_forward/pallas_call | solution.py:312
  236.6 0.8 copy-done.3
  237.4 10.5 %collective-permute-start.51 = (bf16[128,2048]{1,0:T(8,128)(2,1)S(1)}, bf16[128,2048]{1,0:T(8,128)(2,1)S(1)}, u32[]{:S(2)}, u32[]{:S(2)}) collective-permute-start(bf16[128,2048]{1,0:T(8,128)(2,1)S(1)} %get-tuple-element.14), channel_id=1, source_target_pairs={{0,3},{1,0},{2,1},{3,2},{4,7},{5,4},{6,5},{7,6},{8,11},{9,8},{10,9... | collective-permute-start | bytes 1572872 | tf_op jit(solution)/shard_map/ppermute | solution.py:41
  247.9 1.9 collective-permute-start.52
  249.9 0.6 convert_element_type.29
  250.5 10.1 %collective-permute-done.51.refs_1_ = bf16[128,2048]{1,0:T(8,128)(2,1)S(1)} collective-permute-done((bf16[128,2048]{1,0:T(8,128)(2,1)S(1)}, bf16[128,2048]{1,0:T(8,128)(2,1)S(1)}, u32[]{:S(2)}, u32[]{:S(2)}) %collective-permute-start.51) | collective-permute-done | bytes 524320 | tf_op jit(solution)/shard_map/ppermute | solution.py:41
  260.5 34.9 %collective-permute-done.52.refs_2_ = bf16[128,2048]{1,0:T(8,128)(2,1)S(1)} collective-permute-done((bf16[128,2048]{1,0:T(8,128)(2,1)S(1)}, bf16[128,2048]{1,0:T(8,128)(2,1)S(1)}, u32[]{:S(2)}, u32[]{:S(2)}) %collective-permute-start.52) | collective-permute-done | bytes 524320 | tf_op jit(solution)/shard_map/ppermute | solution.py:41
  295.4 0.8 copy-done.10
  296.4 2.9 last_sum.1
  (165 shorter events, 6.3 us)
Async XLA Ops:
  2.2 36.1 %collective-permute-start.2 = (bf16[128,1024]{1,0:T(8,128)(2,1)S(1)}, bf16[128,1024]{1,0:T(8,128)(2,1)S(1)}, u32[]{:S(2)}, u32[]{:S(2)}) collective-permute-start(bf16[128,1024]{1,0:T(8,128)(2,1)S(1)} %pad_maximum_fusion.5), channel_id=1, source_target_pairs={{0,3},{1,0},{2,1},{3,2},{4,7},{5,4},{6,5},{7,6},{8,11},{9,8},{10,9... | collective-permute-start | bytes 786440 | tf_op jit(solution)/shard_map/ppermute | solution.py:41
  10.7 6.0 %collective-permute-start.3 = (f32[32,128]{1,0:T(8,128)S(1)}, f32[32,128]{1,0:T(8,128)S(1)}, u32[]{:S(2)}, u32[]{:S(2)}) collective-permute-start(f32[32,128]{1,0:T(8,128)S(1)} %get-tuple-element.50), channel_id=1, source_target_pairs={{0,1},{1,2},{2,3},{3,0},{4,5},{5,6},{6,7},{7,4},{8,9},{9,10},{10,1... | collective-permute-start | bytes 49160 | tf_op jit(solution)/shard_map/ppermute | solution.py:41
  10.7 8.6 %collective-permute-start.4 = (f32[32,128]{1,0:T(8,128)S(1)}, f32[32,128]{1,0:T(8,128)S(1)}, u32[]{:S(2)}, u32[]{:S(2)}) collective-permute-start(f32[32,128]{1,0:T(8,128)S(1)} %get-tuple-element.51), channel_id=1, source_target_pairs={{0,2},{1,3},{2,0},{3,1},{4,6},{5,7},{6,4},{7,5},{8,10},{9,11},{10,... | collective-permute-start | bytes 49160 | tf_op jit(solution)/shard_map/ppermute | solution.py:41
  11.7 30.0 %collective-permute-start.1 = (bf16[128,1024]{1,0:T(8,128)(2,1)S(1)}, bf16[128,1024]{1,0:T(8,128)(2,1)S(1)}, u32[]{:S(2)}, u32[]{:S(2)}) collective-permute-start(bf16[128,1024]{1,0:T(8,128)(2,1)S(1)} %pad_maximum_fusion.4), channel_id=1, source_target_pairs={{0,2},{1,3},{2,0},{3,1},{4,6},{5,7},{6,4},{7,5},{8,10},{9,11},{10,... | collective-permute-start | bytes 786440 | tf_op jit(solution)/shard_map/ppermute | solution.py:41
  13.8 29.4 %collective-permute-start = (bf16[128,1024]{1,0:T(8,128)(2,1)S(1)}, bf16[128,1024]{1,0:T(8,128)(2,1)S(1)}, u32[]{:S(2)}, u32[]{:S(2)}) collective-permute-start(bf16[128,1024]{1,0:T(8,128)(2,1)S(1)} %pad_maximum_fusion.3), channel_id=1, source_target_pairs={{0,1},{1,2},{2,3},{3,0},{4,5},{5,6},{6,7},{7,4},{8,9},{9,10},{10,1... | collective-permute-start | bytes 786440 | tf_op jit(solution)/shard_map/ppermute | solution.py:41
  16.7 9.8 %collective-permute-start.5 = (f32[32,128]{1,0:T(8,128)S(1)}, f32[32,128]{1,0:T(8,128)S(1)}, u32[]{:S(2)}, u32[]{:S(2)}) collective-permute-start(f32[32,128]{1,0:T(8,128)S(1)} %get-tuple-element.49), channel_id=1, source_target_pairs={{0,3},{1,0},{2,1},{3,2},{4,7},{5,4},{6,5},{7,6},{8,11},{9,8},{10,9... | collective-permute-start | bytes 49160 | tf_op jit(solution)/shard_map/ppermute | solution.py:41
  19.3 147.7 %copy-start.5 = (s32[3]{0:T(128)}, s32[3]{0:T(128)S(1)}, u32[]{:S(2)}) copy-start(s32[3]{0:T(128)S(1)} %pad_add_fusion.refs_8_.refs_4_) | copy-start | bytes 40
  19.3 32.6 %collective-permute-start.9 = (bf16[64,2048]{1,0:T(8,128)(2,1)S(1)}, bf16[64,2048]{1,0:T(8,128)(2,1)S(1)}, u32[]{:S(2)}, u32[]{:S(2)}) collective-permute-start(bf16[64,2048]{1,0:T(8,128)(2,1)S(1)} %copy-done.12), channel_id=1, source_target_pairs={{0,1},{1,2},{2,3},{3,0},{4,5},{5,6},{6,7},{7,4},{8,9},{9,10},{10,1... | collective-permute-start | bytes 786440 | tf_op jit(solution)/shard_map/ppermute | solution.py:41
  26.5 25.4 %collective-permute-start.10 = (bf16[64,2048]{1,0:T(8,128)(2,1)S(1)}, bf16[64,2048]{1,0:T(8,128)(2,1)S(1)}, u32[]{:S(2)}, u32[]{:S(2)}) collective-permute-start(bf16[64,2048]{1,0:T(8,128)(2,1)S(1)} %copy-done.12), channel_id=1, source_target_pairs={{0,2},{1,3},{2,0},{3,1},{4,6},{5,7},{6,4},{7,5},{8,10},{9,11},{10,... | collective-permute-start | bytes 786440 | tf_op jit(solution)/shard_map/ppermute | solution.py:41
  38.4 14.2 %collective-permute-start.11 = (bf16[64,2048]{1,0:T(8,128)(2,1)S(1)}, bf16[64,2048]{1,0:T(8,128)(2,1)S(1)}, u32[]{:S(2)}, u32[]{:S(2)}) collective-permute-start(bf16[64,2048]{1,0:T(8,128)(2,1)S(1)} %copy-done.12), channel_id=1, source_target_pairs={{0,3},{1,0},{2,1},{3,2},{4,7},{5,4},{6,5},{7,6},{8,11},{9,8},{10,9... | collective-permute-start | bytes 786440 | tf_op jit(solution)/shard_map/ppermute | solution.py:41
  41.7 24.6 %collective-permute-start.25 = (bf16[256,1408]{1,0:T(8,128)(2,1)}, bf16[256,1408]{1,0:T(8,128)(2,1)}, u32[]{:S(2)}, u32[]{:S(2)}) collective-permute-start(bf16[256,1408]{1,0:T(8,128)(2,1)} %refs_4_.1), channel_id=1, source_target_pairs={{0,8},{4,12},{8,0},{12,4},{16,24},{20,28},{24,16},{28,20},{1,9},{5... | collective-permute-start | bytes 2162696 | tf_op jit(solution)/shard_map/ppermute | solution.py:45
  43.2 24.7 %collective-permute-start.27 = (bf16[256,1408]{1,0:T(8,128)(2,1)}, bf16[256,1408]{1,0:T(8,128)(2,1)S(1)}, u32[]{:S(2)}, u32[]{:S(2)}) collective-permute-start(bf16[256,1408]{1,0:T(8,128)(2,1)} %refs_4_.1), channel_id=1, source_target_pairs={{0,16},{4,20},{8,24},{12,28},{16,0},{20,4},{24,8},{28,12},{1,17},{... | collective-permute-start | bytes 2162696 | tf_op jit(solution)/shard_map/ppermute | solution.py:45
  51.9 9.4 %collective-permute-start.6 = (bf16[128,512]{1,0:T(8,128)(2,1)}, bf16[128,512]{1,0:T(8,128)(2,1)S(1)}, u32[]{:S(2)}, u32[]{:S(2)}) collective-permute-start(bf16[128,512]{1,0:T(8,128)(2,1)} %get-tuple-element.33), channel_id=1, source_target_pairs={{0,1},{1,2},{2,3},{3,0},{4,5},{5,6},{6,7},{7,4},{8,9},{9,10},{10,1... | collective-permute-start | bytes 393224 | tf_op jit(solution)/shard_map/ppermute | solution.py:41
  51.9 11.0 %collective-permute-start.7 = (bf16[128,512]{1,0:T(8,128)(2,1)}, bf16[128,512]{1,0:T(8,128)(2,1)S(1)}, u32[]{:S(2)}, u32[]{:S(2)}) collective-permute-start(bf16[128,512]{1,0:T(8,128)(2,1)} %get-tuple-element.32), channel_id=1, source_target_pairs={{0,2},{1,3},{2,0},{3,1},{4,6},{5,7},{6,4},{7,5},{8,10},{9,11},{10,... | collective-permute-start | bytes 393224 | tf_op jit(solution)/shard_map/ppermute | solution.py:41
  52.6 12.3 %collective-permute-start.8 = (bf16[128,512]{1,0:T(8,128)(2,1)}, bf16[128,512]{1,0:T(8,128)(2,1)S(1)}, u32[]{:S(2)}, u32[]{:S(2)}) collective-permute-start(bf16[128,512]{1,0:T(8,128)(2,1)} %get-tuple-element.31), channel_id=1, source_target_pairs={{0,3},{1,0},{2,1},{3,2},{4,7},{5,4},{6,5},{7,6},{8,11},{9,8},{10,9... | collective-permute-start | bytes 393224 | tf_op jit(solution)/shard_map/ppermute | solution.py:41
  61.3 19.3 %collective-permute-start.34 = (bf16[256,1408]{1,0:T(8,128)(2,1)}, bf16[256,1408]{1,0:T(8,128)(2,1)S(1)}, u32[]{:S(2)}, u32[]{:S(2)}) collective-permute-start(bf16[256,1408]{1,0:T(8,128)(2,1)} %refs_14_.1), channel_id=1, source_target_pairs={{0,8},{4,12},{8,0},{12,4},{16,24},{20,28},{24,16},{28,20},{1,9},{5... | collective-permute-start | bytes 2162696 | tf_op jit(solution)/shard_map/ppermute | solution.py:45
  62.9 19.3 %collective-permute-start.36 = (bf16[256,1408]{1,0:T(8,128)(2,1)}, bf16[256,1408]{1,0:T(8,128)(2,1)S(1)}, u32[]{:S(2)}, u32[]{:S(2)}) collective-permute-start(bf16[256,1408]{1,0:T(8,128)(2,1)} %refs_14_.1), channel_id=1, source_target_pairs={{0,16},{4,20},{8,24},{12,28},{16,0},{20,4},{24,8},{28,12},{1,17},{... | collective-permute-start | bytes 2162696 | tf_op jit(solution)/shard_map/ppermute | solution.py:45
  64.9 29.5 %collective-permute-start.43 = (bf16[1408,256]{1,0:T(8,128)(2,1)}, bf16[1408,256]{1,0:T(8,128)(2,1)S(1)}, u32[]{:S(2)}, u32[]{:S(2)}) collective-permute-start(bf16[1408,256]{1,0:T(8,128)(2,1)} %refs_24_.1), channel_id=1, source_target_pairs={{0,8},{4,12},{8,0},{12,4},{16,24},{20,28},{24,16},{28,20},{1,9},{5... | collective-permute-start | bytes 2162696 | tf_op jit(solution)/shard_map/ppermute | solution.py:45
  66.4 29.5 %collective-permute-start.45 = (bf16[1408,256]{1,0:T(8,128)(2,1)}, bf16[1408,256]{1,0:T(8,128)(2,1)S(1)}, u32[]{:S(2)}, u32[]{:S(2)}) collective-permute-start(bf16[1408,256]{1,0:T(8,128)(2,1)} %refs_24_.1), channel_id=1, source_target_pairs={{0,16},{4,20},{8,24},{12,28},{16,0},{20,4},{24,8},{28,12},{1,17},{... | collective-permute-start | bytes 2162696 | tf_op jit(solution)/shard_map/ppermute | solution.py:45
  67.9 96.7 %copy-start.13 = (bf16[256,1408]{1,0:T(8,128)(2,1)}, bf16[256,1408]{1,0:T(8,128)(2,1)S(1)}, u32[]{:S(2)}) copy-start(bf16[256,1408]{1,0:T(8,128)(2,1)S(1)} %collective-permute-done.27.refs_8_) | copy-start | bytes 2162692
  67.9 29.5 %collective-permute-start.24 = (bf16[256,1408]{1,0:T(8,128)(2,1)}, bf16[256,1408]{1,0:T(8,128)(2,1)S(1)}, u32[]{:S(2)}, u32[]{:S(2)}) collective-permute-start(bf16[256,1408]{1,0:T(8,128)(2,1)} %refs_4_.1), channel_id=1, source_target_pairs={{0,4},{4,0},{8,12},{12,8},{16,20},{20,16},{24,28},{28,24},{1,5},{5... | collective-permute-start | bytes 2162696 | tf_op jit(solution)/shard_map/ppermute | solution.py:45
  80.7 84.5 %copy-start.14 = (bf16[256,1408]{1,0:T(8,128)(2,1)}, bf16[256,1408]{1,0:T(8,128)(2,1)S(1)}, u32[]{:S(2)}) copy-start(bf16[256,1408]{1,0:T(8,128)(2,1)S(1)} %collective-permute-done.34.refs_16_) | copy-start | bytes 2162692
  80.7 17.3 %collective-permute-start.33 = (bf16[256,1408]{1,0:T(8,128)(2,1)S(1)}, bf16[256,1408]{1,0:T(8,128)(2,1)S(1)}, u32[]{:S(2)}, u32[]{:S(2)}) collective-permute-start(bf16[256,1408]{1,0:T(8,128)(2,1)S(1)} %copy-done.20), channel_id=1, source_target_pairs={{0,4},{4,0},{8,12},{12,8},{16,20},{20,16},{24,28},{28,24},{1,5},{5... | collective-permute-start | bytes 2162696 | tf_op jit(solution)/shard_map/ppermute | solution.py:45
  82.2 83.1 %copy-start.15 = (bf16[256,1408]{1,0:T(8,128)(2,1)}, bf16[256,1408]{1,0:T(8,128)(2,1)S(1)}, u32[]{:S(2)}) copy-start(bf16[256,1408]{1,0:T(8,128)(2,1)S(1)} %collective-permute-done.36.refs_18_) | copy-start | bytes 2162692
  82.2 17.3 %collective-permute-start.42 = (bf16[1408,256]{1,0:T(8,128)(2,1)S(1)}, bf16[1408,256]{1,0:T(8,128)(2,1)S(1)}, u32[]{:S(2)}, u32[]{:S(2)}) collective-permute-start(bf16[1408,256]{1,0:T(8,128)(2,1)S(1)} %copy-done.21), channel_id=1, source_target_pairs={{0,4},{4,0},{8,12},{12,8},{16,20},{20,16},{24,28},{28,24},{1,5},{5... | collective-permute-start | bytes 2162696 | tf_op jit(solution)/shard_map/ppermute | solution.py:45
  94.4 71.6 %copy-start.16 = (bf16[1408,256]{1,0:T(8,128)(2,1)}, bf16[1408,256]{1,0:T(8,128)(2,1)S(1)}, u32[]{:S(2)}) copy-start(bf16[1408,256]{1,0:T(8,128)(2,1)S(1)} %collective-permute-done.43.refs_26_) | copy-start | bytes 2162692
  94.4 11.4 %collective-permute-start.29 = (bf16[128,1408]{1,0:T(8,128)(2,1)S(1)}, bf16[128,1408]{1,0:T(8,128)(2,1)S(1)}, u32[]{:S(2)}, u32[]{:S(2)}) collective-permute-start(bf16[128,1408]{1,0:T(8,128)(2,1)S(1)} %slice.62), channel_id=1, source_target_pairs={{0,16},{4,20},{8,24},{12,28},{16,0},{20,4},{24,8},{28,12},{1,17},{... | collective-permute-start | bytes 1081352 | tf_op jit(solution)/shard_map/ppermute | solution.py:45
  95.9 70.9 %copy-start.17 = (bf16[1408,256]{1,0:T(8,128)(2,1)}, bf16[1408,256]{1,0:T(8,128)(2,1)S(1)}, u32[]{:S(2)}) copy-start(bf16[1408,256]{1,0:T(8,128)(2,1)S(1)} %collective-permute-done.45.refs_28_) | copy-start | bytes 2162692
  95.9 11.3 %collective-permute-start.30 = (bf16[128,1408]{1,0:T(8,128)(2,1)S(1)}, bf16[128,1408]{1,0:T(8,128)(2,1)S(1)}, u32[]{:S(2)}, u32[]{:S(2)}) collective-permute-start(bf16[128,1408]{1,0:T(8,128)(2,1)S(1)} %slice.63), channel_id=1, source_target_pairs={{0,8},{4,12},{8,0},{12,4},{16,24},{20,28},{24,16},{28,20},{1,9},{5... | collective-permute-start | bytes 1081352 | tf_op jit(solution)/shard_map/ppermute | solution.py:45
  97.4 68.4 %copy-start.22 = (bf16[256,1408]{1,0:T(8,128)(2,1)}, bf16[256,1408]{1,0:T(8,128)(2,1)S(1)}, u32[]{:S(2)}) copy-start(bf16[256,1408]{1,0:T(8,128)(2,1)S(1)} %collective-permute-done.24.refs_5_) | copy-start | bytes 2162692
  97.4 45.4 %collective-permute-start.13 = (bf16[256,2048]{1,0:T(8,128)(2,1)S(1)}, bf16[256,2048]{1,0:T(8,128)(2,1)S(1)}, u32[]{:S(2)}, u32[]{:S(2)}) collective-permute-start(bf16[256,2048]{1,0:T(8,128)(2,1)S(1)} %bitcast.73), channel_id=1, source_target_pairs={{0,8},{4,12},{8,0},{12,4},{16,24},{20,28},{24,16},{28,20},{1,9},{5... | collective-permute-start | bytes 3145736 | tf_op jit(solution)/shard_map/ppermute | solution.py:45
  98.0 67.8 %copy-start.23 = (bf16[256,1408]{1,0:T(8,128)(2,1)}, bf16[256,1408]{1,0:T(8,128)(2,1)S(1)}, u32[]{:S(2)}) copy-start(bf16[256,1408]{1,0:T(8,128)(2,1)S(1)} %collective-permute-done.33.refs_15_) | copy-start | bytes 2162692
  98.0 45.3 %collective-permute-start.15 = (bf16[256,2048]{1,0:T(8,128)(2,1)S(1)}, bf16[256,2048]{1,0:T(8,128)(2,1)S(1)}, u32[]{:S(2)}, u32[]{:S(2)}) collective-permute-start(bf16[256,2048]{1,0:T(8,128)(2,1)S(1)} %bitcast.74), channel_id=1, source_target_pairs={{0,16},{4,20},{8,24},{12,28},{16,0},{20,4},{24,8},{28,12},{1,17},{... | collective-permute-start | bytes 3145736 | tf_op jit(solution)/shard_map/ppermute | solution.py:45
  99.5 66.3 %copy-start.24 = (bf16[1408,256]{1,0:T(8,128)(2,1)}, bf16[1408,256]{1,0:T(8,128)(2,1)S(1)}, u32[]{:S(2)}) copy-start(bf16[1408,256]{1,0:T(8,128)(2,1)S(1)} %collective-permute-done.42.refs_25_) | copy-start | bytes 2162692
  99.5 34.0 %collective-permute-start.38 = (bf16[128,1408]{1,0:T(8,128)(2,1)S(1)}, bf16[128,1408]{1,0:T(8,128)(2,1)S(1)}, u32[]{:S(2)}, u32[]{:S(2)}) collective-permute-start(bf16[128,1408]{1,0:T(8,128)(2,1)S(1)} %slice.64), channel_id=1, source_target_pairs={{0,16},{4,20},{8,24},{12,28},{16,0},{20,4},{24,8},{28,12},{1,17},{... | collective-permute-start | bytes 1081352 | tf_op jit(solution)/shard_map/ppermute | solution.py:45
  105.7 29.3 %collective-permute-start.39 = (bf16[128,1408]{1,0:T(8,128)(2,1)S(1)}, bf16[128,1408]{1,0:T(8,128)(2,1)S(1)}, u32[]{:S(2)}, u32[]{:S(2)}) collective-permute-start(bf16[128,1408]{1,0:T(8,128)(2,1)S(1)} %slice.65), channel_id=1, source_target_pairs={{0,8},{4,12},{8,0},{12,4},{16,24},{20,28},{24,16},{28,20},{1,9},{5... | collective-permute-start | bytes 1081352 | tf_op jit(solution)/shard_map/ppermute | solution.py:45
  107.2 36.2 %collective-permute-start.12 = (bf16[256,2048]{1,0:T(8,128)(2,1)S(1)}, bf16[256,2048]{1,0:T(8,128)(2,1)S(1)}, u32[]{:S(2)}, u32[]{:S(2)}) collective-permute-start(bf16[256,2048]{1,0:T(8,128)(2,1)S(1)} %bitcast.75), channel_id=1, source_target_pairs={{0,4},{4,0},{8,12},{12,8},{16,20},{20,16},{24,28},{28,24},{1,5},{5... | collective-permute-start | bytes 3145736 | tf_op jit(solution)/shard_map/ppermute | solution.py:45
  133.5 8.0 %collective-permute-start.47 = (bf16[1408,128]{1,0:T(8,128)(2,1)S(1)}, bf16[1408,128]{1,0:T(8,128)(2,1)S(1)}, u32[]{:S(2)}, u32[]{:S(2)}) collective-permute-start(bf16[1408,128]{1,0:T(8,128)(2,1)S(1)} %slice.66), channel_id=1, source_target_pairs={{0,16},{4,20},{8,24},{12,28},{16,0},{20,4},{24,8},{28,12},{1,17},{... | collective-permute-start | bytes 1081352 | tf_op jit(solution)/shard_map/ppermute | solution.py:45
  135.1 7.8 %collective-permute-start.48 = (bf16[1408,128]{1,0:T(8,128)(2,1)S(1)}, bf16[1408,128]{1,0:T(8,128)(2,1)S(1)}, u32[]{:S(2)}, u32[]{:S(2)}) collective-permute-start(bf16[1408,128]{1,0:T(8,128)(2,1)S(1)} %slice.67), channel_id=1, source_target_pairs={{0,8},{4,12},{8,0},{12,4},{16,24},{20,28},{24,16},{28,20},{1,9},{5... | collective-permute-start | bytes 1081352 | tf_op jit(solution)/shard_map/ppermute | solution.py:45
  141.5 2.4 collective-permute-start.31
  142.9 1.7 collective-permute-start.32
  142.9 2.2 collective-permute-start.40
  143.4 2.2 collective-permute-start.41
  143.4 21.7 %collective-permute-start.14 = (bf16[256,2048]{1,0:T(8,128)(2,1)S(1)}, bf16[256,2048]{1,0:T(8,128)(2,1)S(1)}, u32[]{:S(2)}, u32[]{:S(2)}) collective-permute-start(bf16[256,2048]{1,0:T(8,128)(2,1)S(1)} %collective-permute-done.13.refs_10_), channel_id=1, source_target_pairs={{0,4},{4,0},{8,12},{12,8},{16,20},{20,16},{24,28},{28,24},{1,5},{5... | collective-permute-start | bytes 3145736 | tf_op jit(solution)/shard_map/ppermute | solution.py:45
  143.9 21.4 %collective-permute-start.16 = (bf16[256,2048]{1,0:T(8,128)(2,1)S(1)}, bf16[256,2048]{1,0:T(8,128)(2,1)S(1)}, u32[]{:S(2)}, u32[]{:S(2)}) collective-permute-start(bf16[256,2048]{1,0:T(8,128)(2,1)S(1)} %collective-permute-done.15.refs_12_), channel_id=1, source_target_pairs={{0,4},{4,0},{8,12},{12,8},{16,20},{20,16},{24,28},{28,24},{1,5},{5... | collective-permute-start | bytes 3145736 | tf_op jit(solution)/shard_map/ppermute | solution.py:45
  144.5 5.6 %collective-permute-start.49 = (bf16[1408,128]{1,0:T(8,128)(2,1)S(1)}, bf16[1408,128]{1,0:T(8,128)(2,1)S(1)}, u32[]{:S(2)}, u32[]{:S(2)}) collective-permute-start(bf16[1408,128]{1,0:T(8,128)(2,1)S(1)} %collective-permute-done.47.refs_30_), channel_id=1, source_target_pairs={{0,4},{4,0},{8,12},{12,8},{16,20},{20,16},{24,28},{28,24},{1,5},{5... | collective-permute-start | bytes 1081352 | tf_op jit(solution)/shard_map/ppermute | solution.py:45
  145.0 5.8 %collective-permute-start.50 = (bf16[1408,128]{1,0:T(8,128)(2,1)S(1)}, bf16[1408,128]{1,0:T(8,128)(2,1)S(1)}, u32[]{:S(2)}, u32[]{:S(2)}) collective-permute-start(bf16[1408,128]{1,0:T(8,128)(2,1)S(1)} %collective-permute-done.48.refs_31_), channel_id=1, source_target_pairs={{0,4},{4,0},{8,12},{12,8},{16,20},{20,16},{24,28},{28,24},{1,5},{5... | collective-permute-start | bytes 1081352 | tf_op jit(solution)/shard_map/ppermute | solution.py:45
  145.6 19.0 %collective-permute-start.26 = (bf16[256,1408]{1,0:T(8,128)(2,1)}, bf16[256,1408]{1,0:T(8,128)(2,1)S(1)}, u32[]{:S(2)}, u32[]{:S(2)}) collective-permute-start(bf16[256,1408]{1,0:T(8,128)(2,1)} %collective-permute-done.25.refs_6_), channel_id=1, source_target_pairs={{0,4},{4,0},{8,12},{12,8},{16,20},{20,16},{24,28},{28,24},{1,5},{5... | collective-permute-start | bytes 2162696 | tf_op jit(solution)/shard_map/ppermute | solution.py:45
  150.1 14.0 %collective-permute-start.17 = (bf16[128,2048]{1,0:T(8,128)(2,1)S(1)}, bf16[128,2048]{1,0:T(8,128)(2,1)S(1)}, u32[]{:S(2)}, u32[]{:S(2)}) collective-permute-start(bf16[128,2048]{1,0:T(8,128)(2,1)S(1)} %slice.60), channel_id=1, source_target_pairs={{0,16},{4,20},{8,24},{12,28},{16,0},{20,4},{24,8},{28,12},{1,17},{... | collective-permute-start | bytes 1572872 | tf_op jit(solution)/shard_map/ppermute | solution.py:45
  150.8 13.8 %collective-permute-start.18 = (bf16[128,2048]{1,0:T(8,128)(2,1)S(1)}, bf16[128,2048]{1,0:T(8,128)(2,1)S(1)}, u32[]{:S(2)}, u32[]{:S(2)}) collective-permute-start(bf16[128,2048]{1,0:T(8,128)(2,1)S(1)} %slice.61), channel_id=1, source_target_pairs={{0,8},{4,12},{8,0},{12,4},{16,24},{20,28},{24,16},{28,20},{1,9},{5... | collective-permute-start | bytes 1572872 | tf_op jit(solution)/shard_map/ppermute | solution.py:45
  164.1 1.9 collective-permute-start.19
  164.6 2.1 collective-permute-start.20
  164.6 6.7 %collective-permute-start.28 = (bf16[256,1408]{1,0:T(8,128)(2,1)S(1)}, bf16[256,1408]{1,0:T(8,128)(2,1)S(1)}, u32[]{:S(2)}, u32[]{:S(2)}) collective-permute-start(bf16[256,1408]{1,0:T(8,128)(2,1)S(1)} %collective-permute-done.27.refs_8_), channel_id=1, source_target_pairs={{0,4},{4,0},{8,12},{12,8},{16,20},{20,16},{24,28},{28,24},{1,5},{5... | collective-permute-start | bytes 2162696 | tf_op jit(solution)/shard_map/ppermute | solution.py:45
  165.2 10.8 %collective-permute-start.35 = (bf16[256,1408]{1,0:T(8,128)(2,1)S(1)}, bf16[256,1408]{1,0:T(8,128)(2,1)S(1)}, u32[]{:S(2)}, u32[]{:S(2)}) collective-permute-start(bf16[256,1408]{1,0:T(8,128)(2,1)S(1)} %collective-permute-done.34.refs_16_), channel_id=1, source_target_pairs={{0,4},{4,0},{8,12},{12,8},{16,20},{20,16},{24,28},{28,24},{1,5},{5... | collective-permute-start | bytes 2162696 | tf_op jit(solution)/shard_map/ppermute | solution.py:45
  165.3 14.3 %collective-permute-start.37 = (bf16[256,1408]{1,0:T(8,128)(2,1)S(1)}, bf16[256,1408]{1,0:T(8,128)(2,1)S(1)}, u32[]{:S(2)}, u32[]{:S(2)}) collective-permute-start(bf16[256,1408]{1,0:T(8,128)(2,1)S(1)} %collective-permute-done.36.refs_18_), channel_id=1, source_target_pairs={{0,4},{4,0},{8,12},{12,8},{16,20},{20,16},{24,28},{28,24},{1,5},{5... | collective-permute-start | bytes 2162696 | tf_op jit(solution)/shard_map/ppermute | solution.py:45
  166.0 13.6 %collective-permute-start.44 = (bf16[1408,256]{1,0:T(8,128)(2,1)S(1)}, bf16[1408,256]{1,0:T(8,128)(2,1)S(1)}, u32[]{:S(2)}, u32[]{:S(2)}) collective-permute-start(bf16[1408,256]{1,0:T(8,128)(2,1)S(1)} %collective-permute-done.43.refs_26_), channel_id=1, source_target_pairs={{0,4},{4,0},{8,12},{12,8},{16,20},{20,16},{24,28},{28,24},{1,5},{5... | collective-permute-start | bytes 2162696 | tf_op jit(solution)/shard_map/ppermute | solution.py:45
  166.7 12.8 %collective-permute-start.46 = (bf16[1408,256]{1,0:T(8,128)(2,1)S(1)}, bf16[1408,256]{1,0:T(8,128)(2,1)S(1)}, u32[]{:S(2)}, u32[]{:S(2)}) collective-permute-start(bf16[1408,256]{1,0:T(8,128)(2,1)S(1)} %collective-permute-done.45.refs_28_), channel_id=1, source_target_pairs={{0,4},{4,0},{8,12},{12,8},{16,20},{20,16},{24,28},{28,24},{1,5},{5... | collective-permute-start | bytes 2162696 | tf_op jit(solution)/shard_map/ppermute | solution.py:45
  171.3 42.6 %copy-start.26 = (bf16[256,1408]{1,0:T(8,128)(2,1)}, bf16[256,1408]{1,0:T(8,128)(2,1)S(1)}, u32[]{:S(2)}) copy-start(bf16[256,1408]{1,0:T(8,128)(2,1)S(1)} %collective-permute-done.28.refs_9_) | copy-start | bytes 2162692
  171.3 20.5 %collective-permute-start.21 = (bf16[128,2048]{1,0:T(8,128)(2,1)S(1)}, bf16[128,2048]{1,0:T(8,128)(2,1)S(1)}, u32[]{:S(2)}, u32[]{:S(2)}) collective-permute-start(bf16[128,2048]{1,0:T(8,128)(2,1)S(1)} %get-tuple-element.12.refs_0_), channel_id=1, source_target_pairs={{0,1},{1,2},{2,3},{3,0},{4,5},{5,6},{6,7},{7,4},{8,9},{9,10},{10,1... | collective-permute-start | bytes 1572872 | tf_op jit(solution)/shard_map/ppermute | solution.py:41
  176.0 38.0 %collective-permute-start.22 = (bf16[128,2048]{1,0:T(8,128)(2,1)S(1)}, bf16[128,2048]{1,0:T(8,128)(2,1)S(1)}, u32[]{:S(2)}, u32[]{:S(2)}) collective-permute-start(bf16[128,2048]{1,0:T(8,128)(2,1)S(1)} %get-tuple-element.12.refs_0_), channel_id=1, source_target_pairs={{0,2},{1,3},{2,0},{3,1},{4,6},{5,7},{6,4},{7,5},{8,10},{9,11},{10,... | collective-permute-start | bytes 1572872 | tf_op jit(solution)/shard_map/ppermute | solution.py:41
  179.5 34.4 %collective-permute-start.23 = (bf16[128,2048]{1,0:T(8,128)(2,1)S(1)}, bf16[128,2048]{1,0:T(8,128)(2,1)S(1)}, u32[]{:S(2)}, u32[]{:S(2)}) collective-permute-start(bf16[128,2048]{1,0:T(8,128)(2,1)S(1)} %get-tuple-element.12.refs_0_), channel_id=1, source_target_pairs={{0,3},{1,0},{2,1},{3,2},{4,7},{5,4},{6,5},{7,6},{8,11},{9,8},{10,9... | collective-permute-start | bytes 1572872 | tf_op jit(solution)/shard_map/ppermute | solution.py:41
  237.4 23.1 %collective-permute-start.51 = (bf16[128,2048]{1,0:T(8,128)(2,1)S(1)}, bf16[128,2048]{1,0:T(8,128)(2,1)S(1)}, u32[]{:S(2)}, u32[]{:S(2)}) collective-permute-start(bf16[128,2048]{1,0:T(8,128)(2,1)S(1)} %get-tuple-element.14), channel_id=1, source_target_pairs={{0,3},{1,0},{2,1},{3,2},{4,7},{5,4},{6,5},{7,6},{8,11},{9,8},{10,9... | collective-permute-start | bytes 1572872 | tf_op jit(solution)/shard_map/ppermute | solution.py:41
  247.9 47.5 %collective-permute-start.52 = (bf16[128,2048]{1,0:T(8,128)(2,1)S(1)}, bf16[128,2048]{1,0:T(8,128)(2,1)S(1)}, u32[]{:S(2)}, u32[]{:S(2)}) collective-permute-start(bf16[128,2048]{1,0:T(8,128)(2,1)S(1)} %get-tuple-element.15), channel_id=1, source_target_pairs={{0,2},{1,3},{2,0},{3,1},{4,6},{5,7},{6,4},{7,5},{8,10},{9,11},{10,... | collective-permute-start | bytes 1572872 | tf_op jit(solution)/shard_map/ppermute | solution.py:41
  249.9 45.6 %collective-permute-start.53 = (bf16[128,2048]{1,0:T(8,128)(2,1)}, bf16[128,2048]{1,0:T(8,128)(2,1)S(1)}, u32[]{:S(2)}, u32[]{:S(2)}) collective-permute-start(bf16[128,2048]{1,0:T(8,128)(2,1)} %get-tuple-element.16), channel_id=1, source_target_pairs={{0,1},{1,2},{2,3},{3,0},{4,5},{5,6},{6,7},{7,4},{8,9},{9,10},{10,1... | collective-permute-start | bytes 1572872 | tf_op jit(solution)/shard_map/ppermute | solution.py:41
  (26 other events, 350.3 us)

commit v2 on v1

v2 whole, which is shorter than its diff:
```python
import functools

import jax
import jax.numpy as jnp
from jax import lax
from jax.experimental import pallas as pl
from jax.experimental.pallas import tpu as pltpu
from jax.sharding import PartitionSpec as P

HEADS = 8
DK = 128
DV = 256
CONV = 4
HK = HEADS * DK
EPS_NORM = 1e-05
EPS_UNIT = 1e-06
BF16 = jnp.bfloat16
F32 = jnp.float32
MIB = 1 << 20
STRIP = 256

VMEM = pl.BlockSpec(memory_space=pltpu.VMEM)
SMEM = pl.BlockSpec(memory_space=pltpu.SMEM)
ANY = pl.BlockSpec(memory_space=pl.ANY)


def dot(a, b):
    return jnp.dot(a.astype(BF16), b.astype(BF16), preferred_element_type=F32)


def dot_nt(a, b):
    return lax.dot_general(
        a.astype(BF16), b.astype(BF16), (((1,), (1,)), ((), ())), preferred_element_type=F32
    )


def silu(v):
    return v / (1.0 + jnp.exp(-v))


def shift(value, axis, count, steps):
    return lax.ppermute(value, axis, [(i, (i + steps) % count) for i in range(count)])


def flip(value, bits):
    return lax.ppermute(value, "req", [(i, i ^ bits) for i in range(lax.axis_size("req"))])


def cubic():
    return lax.axis_size("req") == 8


def along(value, count, pairs):
    return lax.ppermute(value, "seq", pairs)


def owners_of(count):
    me = lax.axis_index("seq")
    if count != 4:
        return jnp.stack([lax.rem(me - k + count, count) for k in range(count)]).astype(jnp.int32)
    low = me < 2
    return jnp.stack([me, me ^ 1, jnp.where(low, 2, 1), jnp.where(low, 3, 0)]).astype(jnp.int32)


def gather_line(value, count):
    if count != 4:
        return [[value]] + [[shift(value, "seq", count, k)] for k in range(1, count)]
    near = along(value, count, [(0, 1), (1, 0), (2, 3), (3, 2)])
    middle = along(value, count, [(1, 2), (2, 1)])
    far = along(value, count, [(0, 2), (3, 1)])
    middle_on = along(middle, count, [(1, 0), (2, 3)])
    far_on = along(far, count, [(1, 0), (2, 3)])
    return [[value], [near], [middle, middle_on], [far, far_on]]


def sum_line(parts, count):
    if count != 4:
        return [parts[0]] + [shift(parts[k], "seq", count, count - k) for k in range(1, count)]
    mine, near, middle, far = parts
    far_in = along(far, count, [(0, 1), (3, 2)])
    middle_in = along(middle, count, [(0, 1), (3, 2)])
    near = along(near, count, [(0, 1), (1, 0), (2, 3), (3, 2)])
    add = lambda u, v: (u.astype(F32) + v.astype(F32)).astype(BF16)
    far = along(add(far, far_in), count, [(2, 0), (1, 3)])
    middle = along(add(middle, middle_in), count, [(1, 2), (2, 1)])
    return [mine, near, middle, far]


def after(value, *earlier):
    return lax.optimization_barrier((value, *earlier))[0]


def gather_cube(block):
    mine = jnp.concatenate([block] + [flip(block, bits) for bits in (2, 4, 6)], axis=0)
    return [mine, flip(mine, 1)]


def length_of(where, lengths, slot_request):
    return lengths[slot_request[where[1]]]


def pack_kernel(count, heads, *refs):
    where, lengths, slot_request, tokens, gate, decay, logit = refs[:7]
    outs, (columns, edge, extra) = refs[7 : 7 + count], refs[7 + count :]
    me = where[0]
    piece, channels = tokens.shape
    block = channels // count
    heads_all = decay.shape[0]
    high = decay[...].astype(BF16)
    rest = decay[...] - high.astype(F32)
    middle = rest.astype(BF16)
    low = (rest - middle.astype(F32)).astype(BF16)
    for number, rows in enumerate((logit[...], high, middle, low)):
        columns[number * heads_all : (number + 1) * heads_all, :] = rows.astype(F32)
    first = length_of(where, lengths, slot_request) - (CONV - 1) - me * piece
    entry = lax.broadcasted_iota(jnp.int32, (8, piece), 0)
    spot = lax.broadcasted_iota(jnp.int32, (8, piece), 1)
    select = ((spot == first + entry) & (entry < CONV - 1)).astype(BF16)
    edge[...] = jnp.dot(select, tokens[...], preferred_element_type=F32)
    for k in range(count):
        target = lax.rem(me + k, count)
        start = target * heads

        def span(base, size):
            return pl.ds(pl.multiple_of(base + target * size, size), size)

        outs[k][:piece, : heads * DK] = tokens[:, span(0, heads * DK)]
        outs[k][:piece, heads * DK : 2 * heads * DK] = tokens[:, span(HK, heads * DK)]
        outs[k][:piece, 2 * heads * DK : block] = tokens[:, span(2 * HK, heads * DV)]
        outs[k][:piece, block:] = gate[:, span(0, heads * DV)]
        extra[...] = jnp.zeros(extra.shape, F32)
        for number in range(4):
            for h in range(heads):
                at = (number * heads + h) * piece
                extra[0:1, at : at + piece] = columns[pl.ds(number * heads_all + start + h, 1), :]
        extra[1:CONV, :] = edge[0 : CONV - 1, span(0, block)]
        outs[k][piece:, :block] = extra[...].astype(BF16)
        outs[k][piece:, block:] = jnp.zeros((16, heads * DV), BF16)


def pack(where, lengths, slot_request, tokens, gate, decay, logit, count):
    piece, channels = tokens.shape
    heads = HEADS // count
    block = channels // count
    return pl.pallas_call(
        functools.partial(pack_kernel, count, heads),
        out_shape=(jax.ShapeDtypeStruct((piece + 16, block + heads * DV), BF16),) * count,
        in_specs=[SMEM] * 3 + [VMEM] * 4,
        out_specs=(VMEM,) * count,
        scratch_shapes=[
            pltpu.VMEM((4 * HEADS, piece), F32),
            pltpu.VMEM((8, channels), F32),
            pltpu.VMEM((16, block), F32),
        ],
        name="pack",
    )(where, lengths, slot_request, tokens, gate, decay, logit)


def delta_kernel(count, heads, piece, *refs):
    x_refs, refs = refs[:count], refs[count:]
    where, lengths, slot_request, all_taps, gain, opened, state, xs, bs = refs
    me = where[0]
    length = length_of(where, lengths, slot_request)
    q0, k0, v0 = 0, heads * DK, 2 * heads * DK
    block = xs.shape[1]
    xs[pl.ds(0, 8), :] = jnp.zeros((8, block), F32)
    group = heads * piece
    lane = lax.broadcasted_iota(jnp.int32, (1, piece), 1)
    for k in range(count):
        c = lax.rem(me - k + count, count)
        at = pl.multiple_of(8 + c * piece, 8)
        xs[pl.ds(at, piece), :] = x_refs[k][:piece, :block].astype(F32)
        opened[c] = x_refs[k][:piece, block:]
        line = x_refs[k][piece:, :block].astype(F32)[0:1]
        strength = 1.0 / (1.0 + jnp.exp(-line[:, :group]))
        slope = line[:, group : 2 * group] + line[:, 2 * group : 3 * group] + line[:, 3 * group :]
        live = c * piece + lane < length
        for h in range(heads):
            span = slice(h * piece, (h + 1) * piece)
            bs[c, h : h + 1, :] = jnp.where(live, strength[:, span], 0.0)
            bs[c, heads + h : heads + h + 1, :] = jnp.where(live, slope[:, span], 0.0)
        bs[c, 2 * heads :, :] = jnp.zeros((8 - 2 * heads, piece), F32)

    def taps(i, col, width):
        base, step = (0, DK) if col < k0 else (HK, DK) if col < v0 else (2 * HK, DV)
        inside = col - (q0 if col < k0 else k0 if col < v0 else v0)
        at = pl.multiple_of(base + me * heads * step + inside, DK)
        return all_taps[i : i + 1, pl.ds(at, width)]

    def activated(c, col, width):
        total = None
        for i in range(CONV):
            rows = xs[pl.ds(8 - (CONV - 1) + i + c * piece, piece), pl.ds(col, width)]
            term = taps(i, col, width) * rows
            total = term if total is None else total + term
        return silu(total)

    def unit(v):
        return v * lax.rsqrt(jnp.sum(v * v, axis=-1, keepdims=True) + EPS_UNIT)

    row = lax.broadcasted_iota(jnp.int32, (piece, piece), 0)
    col = lax.broadcasted_iota(jnp.int32, (piece, piece), 1)
    upper = (row <= col).astype(F32)
    pairs = [(c, h) for c in range(count) for h in range(heads)]
    tabs = {}
    for c in range(count):
        rows = bs[c]
        cum = jnp.dot(rows, upper, precision=lax.Precision.HIGHEST, preferred_element_type=F32)
        wide = jnp.concatenate([cum, rows, jnp.zeros((piece - 16, piece), F32)], axis=0)
        tall = wide.T
        for h in range(heads):
            g_row = cum[heads + h : heads + h + 1, :]
            g_col = tall[:, heads + h : heads + h + 1]
            b_col = tall[:, 8 + h : 9 + h]
            tabs[c, h] = (g_row, g_col, b_col)
    couple, solve, first, second, ends = {}, {}, {}, {}, {}
    for c, h in pairs:
        g_row, g_col, b_col = tabs[c, h]
        q = unit(activated(c, q0 + h * DK, DK)) * DK ** (-0.5)
        k = unit(activated(c, k0 + h * DK, DK))
        v = activated(c, v0 + h * DV, DV)
        inner = dot_nt(jnp.concatenate([k, q], axis=0), k)
        spread = jnp.exp(jnp.where(row >= col, g_col - g_row, -1e30))
        couple[c, h] = jnp.where(row > col, inner[:piece] * spread * b_col, 0.0)
        grown = jnp.exp(g_col)
        g_end = g_row[:, piece - 1 : piece]
        to_end = jnp.exp(g_end - g_col) * k
        solve[c, h] = jnp.concatenate([b_col * v, (b_col * grown) * k], axis=1).astype(BF16)
        first[c, h] = (grown * q).astype(BF16)
        second[c, h] = jnp.concatenate([inner[piece:] * spread, to_end.T], axis=0).astype(BF16)
        ends[c, h] = jnp.exp(g_end)
    inverse = {}
    for p in pairs:
        inverse[p] = jnp.where(row == col, 1.0, 0.0) - jnp.where(
            (row >> 1) == (col >> 1), couple[p], 0.0
        )
    level = 1
    while (2 << level) <= piece:
        keep = ((row >> (level + 1)) == (col >> (level + 1))) & ((row >> level) != (col >> level))
        left = {p: dot(inverse[p], jnp.where(keep, couple[p], 0.0)) for p in pairs}
        for p in pairs:
            inverse[p] = inverse[p] - dot(left[p], inverse[p])
        level += 1
    solved = {p: dot(inverse[p], solve[p]) for p in pairs}
    running = [None] * heads
    for c in range(count):
        for h in range(heads):
            values, weighted = solved[c, h][:, :DV], solved[c, h][:, DV:]
            if c == 0:
                corrected = values
                out = None
            else:
                both = dot(
                    jnp.concatenate([weighted.astype(BF16), first[c, h]], axis=0), running[h]
                )
                corrected = values - both[:piece]
                out = both[piece:]
            both = dot(second[c, h], corrected)
            out = both[:piece] if out is None else out + both[:piece]
            running[h] = both[piece:] if c == 0 else ends[c, h] * running[h] + both[piece:]
            scale = lax.rsqrt(jnp.mean(out * out, axis=-1, keepdims=True) + EPS_NORM)
            span = slice(h * DV, (h + 1) * DV)
            gate = silu(opened[c, :, span].astype(F32))
            opened[c, :, span] = (out * scale * gain[...] * gate).astype(BF16)
    for h in range(heads):
        state[h] = running[h]


def delta(xs, where, lengths, slot_request, taps, gain, heads):
    count = len(xs)
    piece = xs[0].shape[0] - 16
    block = heads * (2 * DK + DV)
    return pl.pallas_call(
        functools.partial(delta_kernel, count, heads, piece),
        out_shape=(
            jax.ShapeDtypeStruct((count, piece, heads * DV), BF16),
            jax.ShapeDtypeStruct((heads, DK, DV), F32),
        ),
        in_specs=[VMEM] * count + [SMEM] * 3 + [VMEM] * 2,
        out_specs=(VMEM, VMEM),
        scratch_shapes=[
            pltpu.VMEM((8 + count * piece, block), F32),
            pltpu.VMEM((count, 8, piece), F32),
        ],
        compiler_params=pltpu.CompilerParams(vmem_limit_bytes=40 * MIB),
        cost_estimate=pl.CostEstimate(flops=int(4e9), bytes_accessed=4 * MIB, transcendentals=0),
        name="delta_rule",
    )(*xs, where, lengths, slot_request, taps, gain)


def project_kernel(count, orders, *refs):
    where, owners, mixed, refs = refs[0], refs[1], refs[2], refs[3:]
    parts, refs = refs[: len(orders)], refs[len(orders) :]
    outs, (weights, sems) = refs[:count], refs[count:]
    req = where[1]
    copies = []
    for j, (part, order) in enumerate(zip(parts, orders)):
        size = part.shape[0] // len(order or (0,))
        for i, bits in enumerate(order or (None,)):
            at = 0 if bits is None else pl.multiple_of((req ^ bits) * size, size)
            copies.append(
                pltpu.make_async_copy(
                    part.at[pl.ds(i * size, size), :], weights.at[pl.ds(at, size), :], sems.at[j, i]
                )
            )
            copies[-1].start()
    for copy in copies:
        copy.wait()
    for k in reversed(range(count)):
        outs[k][...] = jnp.dot(
            mixed[owners[k]], weights[...], preferred_element_type=F32
        ).astype(BF16)


def project(mixed, where, owners, parts):
    count, piece, depth = mixed.shape
    width = parts[0].shape[1]
    orders = [None] if len(parts) == 1 else [(0, 2, 4, 6), (1, 3, 5, 7)]
    return pl.pallas_call(
        functools.partial(project_kernel, count, orders),
        out_shape=(jax.ShapeDtypeStruct((piece, width), BF16),) * count,
        in_specs=[SMEM] * 2 + [VMEM] + [ANY] * len(parts),
        out_specs=(VMEM,) * count,
        scratch_shapes=[pltpu.VMEM((depth, width), BF16), pltpu.SemaphoreType.DMA((2, 4))],
        compiler_params=pltpu.CompilerParams(vmem_limit_bytes=24 * MIB),
        cost_estimate=pl.CostEstimate(
            flops=2 * count * piece * width * depth, bytes_accessed=4 * MIB, transcendentals=0
        ),
        name="output_projection",
    )(where, owners, mixed, *parts)


def norm_kernel(count, *refs):
    y_refs, (residual, gain, stream_out, normed_out) = refs[:count], refs[count:]
    total = y_refs[0][...].astype(F32)
    for y in y_refs[1:]:
        total += y[...].astype(F32)
    rounded = (residual[...].astype(F32) + total).astype(BF16)
    wide = rounded.astype(F32)
    scale = lax.rsqrt(jnp.mean(wide * wide, axis=-1, keepdims=True) + EPS_NORM)
    stream_out[...] = rounded
    normed_out[...] = (wide * scale * gain[...]).astype(BF16)


def norm(ys, residual, gain):
    count = len(ys)
    return pl.pallas_call(
        functools.partial(norm_kernel, count),
        out_shape=(jax.ShapeDtypeStruct(residual.shape, BF16),) * 2,
        in_specs=[VMEM] * (count + 2),
        out_specs=(VMEM, VMEM),
        name="stream_norm",
    )(*ys, residual, gain)


def unflatten(refs, counts):
    refs = iter(refs)
    return [[next(refs) for _ in range(count)] for count in counts]


def forward_kernel(terms, shares, strips, *refs):
    x_refs, weights, refs = refs[: sum(terms)], refs[sum(terms)], refs[sum(terms) + 1 :]
    count = len(terms)
    outs, (x, inner, spare, sems) = refs[:count], refs[count:]
    rows = x_refs[0].shape[0]
    depth = x.shape[1] // shares
    copies, spares = [], iter(range(sum(terms)))
    for k, arrays in enumerate(unflatten(x_refs, terms)):
        copies.append([])
        for i, array in enumerate(arrays):
            spot = next(spares)
            target = x.at[pl.ds(k * rows, rows), :] if i == 0 else spare.at[spot - k - 1]
            copy = pltpu.make_async_copy(array, target, sems.at[spot])
            copy.start()
            copies[k].append((copy, None if i == 0 else spot - k - 1))
    for k, group in enumerate(copies):
        for copy, spot in group:
            copy.wait()
            if spot is not None:
                x[k * rows : (k + 1) * rows, :] += spare[spot]

    def product(which, start, size):
        total = None
        for r in range(shares):
            low = (3 * r + which) * depth
            term = jnp.dot(
                x[:, r * depth : (r + 1) * depth],
                weights[low : low + depth, start : start + size],
                preferred_element_type=F32,
            )
            total = term if total is None else total + term
        return total

    for start, size in strips:
        opened, upward = product(0, start, size), product(1, start, size)
        inner[:, start : start + size] = (silu(opened) * upward).astype(BF16)
    for r in range(shares):
        low = (3 * r + 2) * depth
        term = dot_nt(inner[...], weights[low : low + depth, :]).astype(BF16)
        for k in range(count):
            outs[k][:, r * depth : (r + 1) * depth] = term[k * rows : (k + 1) * rows]


def forward(xs, weights, shares):
    rows, width = xs[0][0].shape
    count, hidden = len(xs), weights.shape[1]
    total = count * rows
    strips = [(start, min(STRIP, hidden - start)) for start in range(0, hidden, STRIP)]
    terms = [len(arrays) for arrays in xs]
    return pl.pallas_call(
        functools.partial(forward_kernel, terms, shares, strips),
        out_shape=(jax.ShapeDtypeStruct((rows, width), BF16),) * count,
        in_specs=[ANY] * sum(terms) + [VMEM],
        out_specs=(VMEM,) * count,
        scratch_shapes=[
            pltpu.VMEM((total, width), BF16),
            pltpu.VMEM((total, hidden), BF16),
            pltpu.VMEM((max(1, sum(terms) - count), rows, width), BF16),
            pltpu.SemaphoreType.DMA((sum(terms),)),
        ],
        compiler_params=pltpu.CompilerParams(vmem_limit_bytes=28 * MIB),
        cost_estimate=pl.CostEstimate(
            flops=6 * total * width * hidden, bytes_accessed=4 * MIB, transcendentals=0
        ),
        name="feed_forward",
    )(*sum(xs, []), weights)


def finish_kernel(count, *refs):
    y_refs, (where, lengths, slot_request, stream, out) = refs[:count], refs[count:]
    rows = stream.shape[0]
    position = where[0] * rows + lax.broadcasted_iota(jnp.int32, (rows, 1), 0)
    total = stream[...].astype(F32)
    for y in y_refs:
        total += y[...].astype(F32)
    live = position < length_of(where, lengths, slot_request)
    out[...] = jnp.where(live, total, 0.0).astype(BF16)


def finish(ys, where, lengths, slot_request, stream):
    count = len(ys)
    return pl.pallas_call(
        functools.partial(finish_kernel, count),
        out_shape=jax.ShapeDtypeStruct(stream.shape, BF16),
        in_specs=[VMEM] * count + [SMEM] * 3 + [VMEM],
        out_specs=VMEM,
        name="last_sum",
    )(*ys, where, lengths, slot_request, stream)


def local(
    qkv_proj,
    gate_proj,
    residual,
    log_decay,
    beta_logit,
    lengths,
    slot_request,
    conv_weight,
    norm_gain,
    out_weight,
    mlp_gain,
    w_gate,
    w_up,
    w_down,
):
    me = lax.axis_index("seq")
    req = lax.axis_index("req")
    count = lax.axis_size("seq")
    n_req = lax.axis_size("req")
    piece = qkv_proj.shape[1]
    heads = HEADS // count
    where = jnp.stack([me, req]).astype(jnp.int32)

    packed = pack(
        where, lengths, slot_request, qkv_proj[0], gate_proj[0], log_decay[0].T, beta_logit[0].T, count
    )
    xs = [packed[0]] + [shift(packed[k], "seq", count, k) for k in range(1, count)]
    block = qkv_proj.shape[2] // count
    conv_edge = sum(x[piece + 1 : piece + CONV, :block].astype(F32) for x in xs).astype(BF16)

    placed = lax.ppermute(
        out_weight,
        ("req", "seq"),
        [(i, (i % n_req) * count + i // n_req) for i in range(n_req * count)],
    )
    if cubic():
        out_parts = gather_cube(placed)
    else:
        out_parts = [lax.all_gather(placed, "req", axis=0, tiled=True)]
    weights = jnp.concatenate([w_gate, w_up, w_down.T], axis=0)
    weights = lax.all_gather(after(weights, out_parts[0], *xs[1:]), "req", axis=0, tiled=True)
    mixed, state = delta(xs, where, lengths, slot_request, conv_weight, norm_gain[None, :], heads)
    ys = project(mixed, where, owners_of(count), out_parts)
    stream, normed = norm(sum_line(ys, count), residual[0], mlp_gain[None, :])
    ys = forward(gather_line(normed, count), weights, n_req)
    hidden = finish(sum_line(ys, count), where, lengths, slot_request, stream)
    return hidden[None], state[None], conv_edge[None]


def solution(mesh):
    return jax.shard_map(
        local,
        mesh=mesh,
        in_specs=(
            P("req", "seq", None),
            P("req", "seq", None),
            P("req", "seq", None),
            P("req", "seq", None),
            P("req", "seq", None),
            P(),
            P(),
            P(),
            P(),
            P(("req", "seq"), None),
            P(),
            P("req", "seq"),
            P("req", "seq"),
            P("seq", "req"),
        ),
        out_specs=(P("req", "seq", None), P("req", "seq", None, None), P("req", None, "seq")),
        check_vma=False,
    )
```

time: 300 us -> 235 us (0.78)
  waiting for transfers between devices: 169 us -> 108 us
  starting transfers between devices: 81.5 us -> 62.6 us
  between operations: 2.01 us -> 14.4 us
  local copies, waits for them, and re-layouts: 10.5 us -> 15.4 us
  Pallas kernels: 33.7 us -> 29.1 us
    ppermute x0 -> x16, waiting for transfers between devices: none -> 104 us  [the longest x15 104 us: along(): return lax.ppermute(value, 'seq', pairs)]
    ppermute x18 -> x3, waiting for transfers between devices: 86.4 us -> 0.01 us  [shift(): lax.ppermute(value, axis, [(i, (i + steps) % count) for i in range(count)])]
    ppermute x36 -> x4, waiting for transfers between devices: 82.4 us -> 4.34 us  [flip(): lax.ppermute(value, 'req', [(i, i ^ bits) for i in range(lax.axis_size('r...]
    ppermute x18 -> x3, starting transfers between devices: 57.8 us -> 8.53 us  [shift(): lax.ppermute(value, axis, [(i, (i + steps) % count) for i in range(count)])]
    ppermute x0 -> x16, starting transfers between devices: none -> 23.6 us  [the longest x15 22 us: along(): return lax.ppermute(value, 'seq', pairs)]
    unnamed x72 -> x44, local copies, waits for them, and re-layouts: 4.54 us -> 15.4 us
    ppermute x36 -> x4, starting transfers between devices: 23.7 us -> 30.4 us  [flip(): lax.ppermute(value, 'req', [(i, i ^ bits) for i in range(lax.axis_size('r...]
    pallas_call x3 -> x5, Pallas kernels: 27.4 us -> 22.5 us  [the longest x1 10.2 us: forward(): pl.pallas_call(functools.partial(forward_kernel, terms, shares, strips),...]
  transfers between devices with their start and end apart: 54 -> 24, of which waited for: 21 -> 14; matrix products, arithmetic and copies ran while one was open for 2% -> 3% of each run, Pallas kernels for 3% -> 7%
where the time goes in v2:
time: 235 us; the launch traced here: 234 us
  waiting for transfers between devices  108 us (46%)
  starting transfers between devices  62.6 us (27%)
  Pallas kernels  29.1 us (12%)
  local copies, waits for them, and re-layouts  15.4 us (7%)
  between operations  14.4 us (6%)
  other arithmetic  4.68 us (2%)
    ppermute x15, waiting for transfers between devices, along(): return lax.ppermute(value, 'seq', pairs)  104 us
    ppermute x4, starting transfers between devices, flip(): lax.ppermute(value, 'req', [(i, i ^ bits) for i in range(lax.axis_size('r...  30.4 us
    ppermute x15, starting transfers between devices, along(): return lax.ppermute(value, 'seq', pairs)  22 us
    unnamed x44, local copies, waits for them, and re-layouts  15.4 us
    pallas_call x1, Pallas kernels, forward(): pl.pallas_call(functools.partial(forward_kernel, terms, shares, strips),...  10.2 us
    ppermute x3, starting transfers between devices, shift(): lax.ppermute(value, axis, [(i, (i + steps) % count) for i in range(count)])  8.53 us
    pallas_call x1, Pallas kernels, delta(): pl.pallas_call(functools.partial(delta_kernel, count, heads, piece), out_...  6.59 us
  transfers between devices with their start and end apart: 24, of which 14 were waited for; matrix products, arithmetic and copies ran while one was open for 3% of the time, Pallas kernels for 7%

profile of v2, /device:TPU:0, one launch (start us, length us, event | category | flops | bytes accessed | tf_op | source)
XLA Modules:
  0.0 234.2 jit_solution(137035856862920221)
XLA Ops:
  7.2 0.0 all-gather.2.cloned.1.call-start
  7.2 1.6 collective-permute-start.3
  8.8 0.7 pad_add_fusion.refs_0_.refs_4_
  9.5 2.9 %pack.1 = (bf16[144,1536]{1,0:T(8,128)(2,1)}, bf16[144,1536]{1,0:T(8,128)(2,1)}, bf16[144,1536]{1,0:T(8,128)(2,1)}, bf16[144,1536]{1,0:T(8,128)(2,1)}) custom-call(s32[2]{0:T(128)} %pad_add_fusion.refs_0_.refs_4_, s32[8]{0:T(128)} %refs_5_.3, s32[8]{0:T(128)} %refs_6_.3, bf16[128,4096]{1,0:T(8,128)(2,1)} %bitcast.23, bf16[128,2048]{1,0:T(8,128)(2,1)} %bitcast.26, ...), custom_call_target="tpu_custom_call" | custom-call | tf_op jit(solution)/shard_map/pack/pallas_call | solution.py:145
  12.4 3.3 %collective-permute-start = (bf16[144,1536]{1,0:T(8,128)(2,1)}, bf16[144,1536]{1,0:T(8,128)(2,1)S(1)}, u32[]{:S(2)}, u32[]{:S(2)}) collective-permute-start(bf16[144,1536]{1,0:T(8,128)(2,1)} %get-tuple-element.21), channel_id=1, source_target_pairs={{0,1},{1,2},{2,3},{3,0},{4,5},{5,6},{6,7},{7,4},{8,9},{9,10},{10,1... | collective-permute-start | bytes 1327112 | tf_op jit(solution)/shard_map/ppermute | solution.py:42
  15.7 3.2 %collective-permute-start.1 = (bf16[144,1536]{1,0:T(8,128)(2,1)}, bf16[144,1536]{1,0:T(8,128)(2,1)S(1)}, u32[]{:S(2)}, u32[]{:S(2)}) collective-permute-start(bf16[144,1536]{1,0:T(8,128)(2,1)} %get-tuple-element.22), channel_id=1, source_target_pairs={{0,2},{1,3},{2,0},{3,1},{4,6},{5,7},{6,4},{7,5},{8,10},{9,11},{10,... | collective-permute-start | bytes 1327112 | tf_op jit(solution)/shard_map/ppermute | solution.py:42
  18.9 2.0 collective-permute-start.2
  20.9 1.4 copy.17
  22.5 25.3 %collective-permute-start.4 = (bf16[64,2048]{1,0:T(8,128)(2,1)S(1)}, bf16[64,2048]{1,0:T(8,128)(2,1)S(1)}, u32[]{:S(2)}, u32[]{:S(2)}) collective-permute-start(bf16[64,2048]{1,0:T(8,128)(2,1)S(1)} %collective-permute-done.3), channel_id=1, source_target_pairs={{0,8},{4,12},{8,0},{12,4},{16,24},{20,28},{24,16},{28,20},{1,9},{5... | collective-permute-start | bytes 786440 | tf_op jit(solution)/shard_map/ppermute | solution.py:46
  47.8 2.8 %pad_maximum_fusion = bf16[768,1408]{1,0:T(8,128)(2,1)} fusion(bf16[256,1408]{1,0:T(8,128)(2,1)S(1)} %bitcast.22, bf16[256,1408]{1,0:T(8,128)(2,1)} %param.26, bf16[256,1408]{1,0:T(8,128)(2,1)} %param.25), kind=kLoop, calls=%fused_computation | loop fusion | flops 6488064 | bytes 4325376 | tf_op jit(solution)/shard_map/concatenate | solution.py:491
  50.6 2.0 collective-permute-start.5
  52.6 3.0 %collective-permute-start.6 = (bf16[64,2048]{1,0:T(8,128)(2,1)S(1)}, bf16[64,2048]{1,0:T(8,128)(2,1)S(1)}, u32[]{:S(2)}, u32[]{:S(2)}) collective-permute-start(bf16[64,2048]{1,0:T(8,128)(2,1)S(1)} %collective-permute-done.3), channel_id=1, source_target_pairs={{0,24},{4,28},{8,16},{12,20},{16,8},{20,12},{24,0},{28,4},{1,25},{... | collective-permute-start | bytes 786440 | tf_op jit(solution)/shard_map/ppermute | solution.py:46
  55.6 3.7 %collective-permute-done.5 = bf16[64,2048]{1,0:T(8,128)(2,1)S(1)} collective-permute-done((bf16[64,2048]{1,0:T(8,128)(2,1)S(1)}, bf16[64,2048]{1,0:T(8,128)(2,1)S(1)}, u32[]{:S(2)}, u32[]{:S(2)}) %collective-permute-start.5) | collective-permute-done | bytes 262176 | tf_op jit(solution)/shard_map/ppermute | solution.py:46
  59.4 0.6 collective-permute-done.6
  60.0 0.0 all-gather.2.cloned.1.call-update
  60.1 0.1 collective-permute-start.7
  60.1 0.1 pad_add_fusion.1.refs_1_
  60.3 6.6 %delta_rule.1 = (bf16[4,128,512]{2,1,0:T(8,128)(2,1)S(1)}, f32[2,128,256]{2,1,0:T(8,128)}) custom-call(bf16[144,1536]{1,0:T(8,128)(2,1)S(1)} %copy-done.5, bf16[144,1536]{1,0:T(8,128)(2,1)S(1)} %collective-permute-done.refs_1_, bf16[144,1536]{1,0:T(8,128)(2,1)S(1)} %collective-permute-done.1.refs_2_, bf16[144,1536]{1,0:T(8,128)(2,1)S(1)} %collective-permute-done.2.refs_3_, ...), custom_call_target="tpu_custom_call" | custom-call | flops 4000000000 | bytes 4194304 | tf_op jit(solution)/shard_map/delta_rule/pallas_call | solution.py:273
  66.9 3.3 %output_projection.1 = (bf16[128,2048]{1,0:T(8,128)(2,1)S(1)}, bf16[128,2048]{1,0:T(8,128)(2,1)S(1)}, bf16[128,2048]{1,0:T(8,128)(2,1)S(1)}, bf16[128,2048]{1,0:T(8,128)(2,1)S(1)}) custom-call(s32[2]{0:T(128)S(1)} %copy-done.4, s32[4]{0:T(128)S(1)} %pad_add_fusion.1.refs_1_, bf16[4,128,512]{2,1,0:T(8,128)(2,1)S(1)} %get-tuple-element.24.refs_2_, ...), custom_call_target="tpu_custom_call" | custom-call | flops 1073741824 | bytes 4194304 | tf_op jit(solution)/shard_map/output_projection/pallas_call | solution.py:319
  70.2 0.8 copy-done.1
  71.0 7.9 %collective-permute-start.9 = (bf16[128,2048]{1,0:T(8,128)(2,1)S(1)}, bf16[128,2048]{1,0:T(8,128)(2,1)S(1)}, u32[]{:S(2)}, u32[]{:S(2)}) collective-permute-start(bf16[128,2048]{1,0:T(8,128)(2,1)S(1)} %get-tuple-element.27), channel_id=1, source_target_pairs={{0,1},{3,2},{4,5},{7,6},{8,9},{11,10},{12,13},{15,14},{16,17},{19,... | collective-permute-start | bytes 1572872 | tf_op jit(solution)/shard_map/ppermute | solution.py:54
  78.9 1.3 collective-permute-start.11
  80.2 0.1 collective-permute-start.8
  80.3 10.8 %collective-permute-done.9 = bf16[128,2048]{1,0:T(8,128)(2,1)S(1)} collective-permute-done((bf16[128,2048]{1,0:T(8,128)(2,1)S(1)}, bf16[128,2048]{1,0:T(8,128)(2,1)S(1)}, u32[]{:S(2)}, u32[]{:S(2)}) %collective-permute-start.9) | collective-permute-done | bytes 524320 | tf_op jit(solution)/shard_map/ppermute | solution.py:54
  91.1 0.1 add_convert_fusion.3
  91.2 0.7 collective-permute-start.10
  91.9 10.4 %collective-permute-done.11 = bf16[128,2048]{1,0:T(8,128)(2,1)S(1)} collective-permute-done((bf16[128,2048]{1,0:T(8,128)(2,1)S(1)}, bf16[128,2048]{1,0:T(8,128)(2,1)S(1)}, u32[]{:S(2)}, u32[]{:S(2)}) %collective-permute-start.11) | collective-permute-done | bytes 524320 | tf_op jit(solution)/shard_map/ppermute | solution.py:54
  102.3 0.1 add_convert_fusion.2
  102.4 1.3 collective-permute-start.12
  103.7 9.3 %collective-permute-done.8.refs_1_ = bf16[128,2048]{1,0:T(8,128)(2,1)S(1)} collective-permute-done((bf16[128,2048]{1,0:T(8,128)(2,1)S(1)}, bf16[128,2048]{1,0:T(8,128)(2,1)S(1)}, u32[]{:S(2)}, u32[]{:S(2)}) %collective-permute-start.8) | collective-permute-done | bytes 524320 | tf_op jit(solution)/shard_map/ppermute | solution.py:54
  113.1 6.3 %collective-permute-done.12.refs_3_ = bf16[128,2048]{1,0:T(8,128)(2,1)S(1)} collective-permute-done((bf16[128,2048]{1,0:T(8,128)(2,1)S(1)}, bf16[128,2048]{1,0:T(8,128)(2,1)S(1)}, u32[]{:S(2)}, u32[]{:S(2)}) %collective-permute-start.12) | collective-permute-done | bytes 524320 | tf_op jit(solution)/shard_map/ppermute | solution.py:54
  119.3 0.8 copy-done.19
  120.1 3.2 %stream_norm.1 = (bf16[128,2048]{1,0:T(8,128)(2,1)}, bf16[128,2048]{1,0:T(8,128)(2,1)}) custom-call(bf16[128,2048]{1,0:T(8,128)(2,1)} %copy-done.1, bf16[128,2048]{1,0:T(8,128)(2,1)} %copy-done.15, bf16[128,2048]{1,0:T(8,128)(2,1)} %copy-done.17, bf16[128,2048]{1,0:T(8,128)(2,1)} %copy-done.19, bf16[128,2048]{1,0:T(8,128)(2,1)} %bitcast.24, f32[1,2048]{1,0:T(1,128)} %bitcast.27), custom_call_target="tpu_custom_call" | custom-call | tf_op jit(solution)/shard_map/stream_norm/pallas_call | solution.py:347
  123.3 1.3 collective-permute-start.16
  124.7 0.7 collective-permute-start.14
  125.4 1.2 collective-permute-start.13
  126.5 10.8 %collective-permute-done.16.refs_4_ = bf16[128,2048]{1,0:T(8,128)(2,1)S(1)} collective-permute-done((bf16[128,2048]{1,0:T(8,128)(2,1)}, bf16[128,2048]{1,0:T(8,128)(2,1)S(1)}, u32[]{:S(2)}, u32[]{:S(2)}) %collective-permute-start.16) | collective-permute-done | bytes 524320 | tf_op jit(solution)/shard_map/ppermute | solution.py:54
  137.4 1.3 collective-permute-start.17
  138.6 1.5 collective-permute-start.15
  140.1 6.8 %collective-permute-done.13.refs_1_ = bf16[128,2048]{1,0:T(8,128)(2,1)S(1)} collective-permute-done((bf16[128,2048]{1,0:T(8,128)(2,1)}, bf16[128,2048]{1,0:T(8,128)(2,1)S(1)}, u32[]{:S(2)}, u32[]{:S(2)}) %collective-permute-start.13) | collective-permute-done | bytes 524320 | tf_op jit(solution)/shard_map/ppermute | solution.py:54
  147.0 3.0 %collective-permute-done.17.refs_5_ = bf16[128,2048]{1,0:T(8,128)(2,1)S(1)} collective-permute-done((bf16[128,2048]{1,0:T(8,128)(2,1)S(1)}, bf16[128,2048]{1,0:T(8,128)(2,1)S(1)}, u32[]{:S(2)}, u32[]{:S(2)}) %collective-permute-start.17) | collective-permute-done | bytes 524320 | tf_op jit(solution)/shard_map/ppermute | solution.py:54
  150.0 0.8 copy-done.8
  150.8 11.7 %collective-permute-done.15.refs_3_ = bf16[128,2048]{1,0:T(8,128)(2,1)S(1)} collective-permute-done((bf16[128,2048]{1,0:T(8,128)(2,1)S(1)}, bf16[128,2048]{1,0:T(8,128)(2,1)S(1)}, u32[]{:S(2)}, u32[]{:S(2)}) %collective-permute-start.15) | collective-permute-done | bytes 524320 | tf_op jit(solution)/shard_map/ppermute | solution.py:54
  162.4 0.8 copy-done.10
  163.2 5.9 %copy-done.6 = bf16[6144,1408]{1,0:T(8,128)(2,1)S(1)} copy-done((bf16[6144,1408]{1,0:T(8,128)(2,1)S(1)}, bf16[6144,1408]{1,0:T(8,128)(2,1)}, u32[]{:S(2)}) %copy-start.6) | copy-done | bytes 17301528
  169.2 1.0 copy-done.7
  170.2 1.0 copy-done.9
  171.2 1.0 copy-done.11
  172.3 10.2 %feed_forward.1 = (bf16[128,2048]{1,0:T(8,128)(2,1)S(1)}, bf16[128,2048]{1,0:T(8,128)(2,1)S(1)}, bf16[128,2048]{1,0:T(8,128)(2,1)S(1)}, bf16[128,2048]{1,0:T(8,128)(2,1)S(1)}) custom-call(bf16[128,2048]{1,0:T(8,128)(2,1)S(1)} %copy-done.7, bf16[128,2048]{1,0:T(8,128)(2,1)S(1)} %collective-permute-done.13.refs_1_, ...), custom_call_target="tpu_custom_call" | custom-call | flops 8858370048 | bytes 4194304 | tf_op jit(solution)/shard_map/feed_forward/pallas_call | solution.py:410
  182.5 0.8 copy-done
  183.3 1.5 collective-permute-start.19
  184.8 1.3 collective-permute-start.21
  186.1 0.1 collective-permute-start.18
  186.2 10.9 %collective-permute-done.19 = bf16[128,2048]{1,0:T(8,128)(2,1)S(1)} collective-permute-done((bf16[128,2048]{1,0:T(8,128)(2,1)S(1)}, bf16[128,2048]{1,0:T(8,128)(2,1)S(1)}, u32[]{:S(2)}, u32[]{:S(2)}) %collective-permute-start.19) | collective-permute-done | bytes 524320 | tf_op jit(solution)/shard_map/ppermute | solution.py:54
  197.1 0.1 add_convert_fusion.1
  197.2 0.7 collective-permute-start.20
  197.9 10.4 %collective-permute-done.21 = bf16[128,2048]{1,0:T(8,128)(2,1)S(1)} collective-permute-done((bf16[128,2048]{1,0:T(8,128)(2,1)S(1)}, bf16[128,2048]{1,0:T(8,128)(2,1)S(1)}, u32[]{:S(2)}, u32[]{:S(2)}) %collective-permute-start.21) | collective-permute-done | bytes 524320 | tf_op jit(solution)/shard_map/ppermute | solution.py:54
  208.3 0.1 add_convert_fusion
  208.5 1.3 collective-permute-start.22
  209.8 0.6 fusion
  210.4 7.9 %collective-permute-done.18.refs_1_ = bf16[128,2048]{1,0:T(8,128)(2,1)S(1)} collective-permute-done((bf16[128,2048]{1,0:T(8,128)(2,1)S(1)}, bf16[128,2048]{1,0:T(8,128)(2,1)S(1)}, u32[]{:S(2)}, u32[]{:S(2)}) %collective-permute-start.18) | collective-permute-done | bytes 524320 | tf_op jit(solution)/shard_map/ppermute | solution.py:54
  218.3 5.4 %collective-permute-done.22.refs_3_ = bf16[128,2048]{1,0:T(8,128)(2,1)S(1)} collective-permute-done((bf16[128,2048]{1,0:T(8,128)(2,1)S(1)}, bf16[128,2048]{1,0:T(8,128)(2,1)S(1)}, u32[]{:S(2)}, u32[]{:S(2)}) %collective-permute-start.22) | collective-permute-done | bytes 524320 | tf_op jit(solution)/shard_map/ppermute | solution.py:54
  223.8 0.8 copy-done.18
  224.5 2.8 %last_sum.1 = bf16[128,2048]{1,0:T(8,128)(2,1)} custom-call(bf16[128,2048]{1,0:T(8,128)(2,1)} %copy-done, bf16[128,2048]{1,0:T(8,128)(2,1)} %copy-done.14, bf16[128,2048]{1,0:T(8,128)(2,1)} %copy-done.16, bf16[128,2048]{1,0:T(8,128)(2,1)} %copy-done.18, s32[2]{0:T(128)} %pad_add_fusion.refs_0_.refs_4_, s32[8]{0:T(128)} %refs_5_.3, s32[8]{0:T(128)} %refs_6_.3, ...), custom_call_target="tpu_custom_call" | custom-call | tf_op jit(solution)/shard_map/last_sum/pallas_call | solution.py:442
  (44 shorter events, 0.2 us)
Async XLA Ops:
  7.2 156.1 %all-gather.2.cloned.1.call-start = ((), (), s32[]{:S(2)}) async-start(), calls=%async_computation | async-start | bytes 19464192 | tf_op jit(solution)/shard_map/all_gather | solution.py:492
  7.2 15.2 %collective-permute-start.3 = (bf16[64,2048]{1,0:T(8,128)(2,1)}, bf16[64,2048]{1,0:T(8,128)(2,1)S(1)}, u32[]{:S(2)}, u32[]{:S(2)}) collective-permute-start(bf16[64,2048]{1,0:T(8,128)(2,1)} %param.23), channel_id=1, source_target_pairs={{0,0},{1,4},{2,8},{3,12},{4,16},{5,20},{6,24},{7,28},{8,1},{9,5},{... | collective-permute-start | bytes 786440 | tf_op jit(solution)/shard_map/ppermute | solution.py:482
  12.4 47.6 %collective-permute-start = (bf16[144,1536]{1,0:T(8,128)(2,1)}, bf16[144,1536]{1,0:T(8,128)(2,1)S(1)}, u32[]{:S(2)}, u32[]{:S(2)}) collective-permute-start(bf16[144,1536]{1,0:T(8,128)(2,1)} %get-tuple-element.21), channel_id=1, source_target_pairs={{0,1},{1,2},{2,3},{3,0},{4,5},{5,6},{6,7},{7,4},{8,9},{9,10},{10,1... | collective-permute-start | bytes 1327112 | tf_op jit(solution)/shard_map/ppermute | solution.py:42
  15.7 44.3 %collective-permute-start.1 = (bf16[144,1536]{1,0:T(8,128)(2,1)}, bf16[144,1536]{1,0:T(8,128)(2,1)S(1)}, u32[]{:S(2)}, u32[]{:S(2)}) collective-permute-start(bf16[144,1536]{1,0:T(8,128)(2,1)} %get-tuple-element.22), channel_id=1, source_target_pairs={{0,2},{1,3},{2,0},{3,1},{4,6},{5,7},{6,4},{7,5},{8,10},{9,11},{10,... | collective-permute-start | bytes 1327112 | tf_op jit(solution)/shard_map/ppermute | solution.py:42
  18.9 41.1 %collective-permute-start.2 = (bf16[144,1536]{1,0:T(8,128)(2,1)}, bf16[144,1536]{1,0:T(8,128)(2,1)S(1)}, u32[]{:S(2)}, u32[]{:S(2)}) collective-permute-start(bf16[144,1536]{1,0:T(8,128)(2,1)} %get-tuple-element.23), channel_id=1, source_target_pairs={{0,3},{1,0},{2,1},{3,2},{4,7},{5,4},{6,5},{7,6},{8,11},{9,8},{10,9... | collective-permute-start | bytes 1327112 | tf_op jit(solution)/shard_map/ppermute | solution.py:42
  22.4 37.8 %copy-start.2 = (s32[8]{0:T(128)S(1)}, s32[8]{0:T(128)}, u32[]{:S(2)}) copy-start(s32[8]{0:T(128)} %refs_5_.3) | copy-start | bytes 100
  22.4 37.8 %copy-start.3 = (s32[8]{0:T(128)S(1)}, s32[8]{0:T(128)}, u32[]{:S(2)}) copy-start(s32[8]{0:T(128)} %refs_6_.3) | copy-start | bytes 100
  22.4 37.8 %copy-start.4 = (s32[2]{0:T(128)S(1)}, s32[2]{0:T(128)}, u32[]{:S(2)}) copy-start(s32[2]{0:T(128)} %pad_add_fusion.refs_0_.refs_4_) | copy-start | bytes 28
  22.4 37.8 %copy-start.5 = (bf16[144,1536]{1,0:T(8,128)(2,1)S(1)}, bf16[144,1536]{1,0:T(8,128)(2,1)}, u32[]{:S(2)}) copy-start(bf16[144,1536]{1,0:T(8,128)(2,1)} %get-tuple-element.20.refs_0_) | copy-start | bytes 1327108
  22.4 37.8 %copy-start.12 = (f32[4,4096]{1,0:T(4,128)S(1)}, f32[4,4096]{1,0:T(4,128)}, u32[]{:S(2)}) copy-start(f32[4,4096]{1,0:T(4,128)} %refs_7_.1) | copy-start | bytes 196612
  22.4 37.8 %copy-start.13 = (f32[256]{0:T(256)S(1)}, f32[256]{0:T(256)}, u32[]{:S(2)}) copy-start(f32[256]{0:T(256)} %param.22) | copy-start | bytes 3076
  22.5 30.2 %collective-permute-start.4 = (bf16[64,2048]{1,0:T(8,128)(2,1)S(1)}, bf16[64,2048]{1,0:T(8,128)(2,1)S(1)}, u32[]{:S(2)}, u32[]{:S(2)}) collective-permute-start(bf16[64,2048]{1,0:T(8,128)(2,1)S(1)} %collective-permute-done.3), channel_id=1, source_target_pairs={{0,8},{4,12},{8,0},{12,4},{16,24},{20,28},{24,16},{28,20},{1,9},{5... | collective-permute-start | bytes 786440 | tf_op jit(solution)/shard_map/ppermute | solution.py:46
  50.6 8.8 %collective-permute-start.5 = (bf16[64,2048]{1,0:T(8,128)(2,1)S(1)}, bf16[64,2048]{1,0:T(8,128)(2,1)S(1)}, u32[]{:S(2)}, u32[]{:S(2)}) collective-permute-start(bf16[64,2048]{1,0:T(8,128)(2,1)S(1)} %collective-permute-done.3), channel_id=1, source_target_pairs={{0,16},{4,20},{8,24},{12,28},{16,0},{20,4},{24,8},{28,12},{1,17},{... | collective-permute-start | bytes 786440 | tf_op jit(solution)/shard_map/ppermute | solution.py:46
  52.6 7.3 %collective-permute-start.6 = (bf16[64,2048]{1,0:T(8,128)(2,1)S(1)}, bf16[64,2048]{1,0:T(8,128)(2,1)S(1)}, u32[]{:S(2)}, u32[]{:S(2)}) collective-permute-start(bf16[64,2048]{1,0:T(8,128)(2,1)S(1)} %collective-permute-done.3), channel_id=1, source_target_pairs={{0,24},{4,28},{8,16},{12,20},{16,8},{20,12},{24,0},{28,4},{1,25},{... | collective-permute-start | bytes 786440 | tf_op jit(solution)/shard_map/ppermute | solution.py:46
  60.1 6.8 %collective-permute-start.7 = (bf16[256,2048]{1,0:T(8,128)(2,1)S(1)}, bf16[256,2048]{1,0:T(8,128)(2,1)}, u32[]{:S(2)}, u32[]{:S(2)}) collective-permute-start(bf16[256,2048]{1,0:T(8,128)(2,1)S(1)} %constant_dynamic-update-slice_fusion.refs_3_), channel_id=1, source_target_pairs={{0,4},{4,0},{8,12},{12,8},{16,20},{20,16},{24,28},{28,24},{1,5},{5... | collective-permute-start | bytes 3145736 | tf_op jit(solution)/shard_map/ppermute | solution.py:46
  70.2 0.8 copy-start.1
  71.0 20.1 %collective-permute-start.9 = (bf16[128,2048]{1,0:T(8,128)(2,1)S(1)}, bf16[128,2048]{1,0:T(8,128)(2,1)S(1)}, u32[]{:S(2)}, u32[]{:S(2)}) collective-permute-start(bf16[128,2048]{1,0:T(8,128)(2,1)S(1)} %get-tuple-element.27), channel_id=1, source_target_pairs={{0,1},{3,2},{4,5},{7,6},{8,9},{11,10},{12,13},{15,14},{16,17},{19,... | collective-permute-start | bytes 1572872 | tf_op jit(solution)/shard_map/ppermute | solution.py:54
  78.9 23.4 %collective-permute-start.11 = (bf16[128,2048]{1,0:T(8,128)(2,1)S(1)}, bf16[128,2048]{1,0:T(8,128)(2,1)S(1)}, u32[]{:S(2)}, u32[]{:S(2)}) collective-permute-start(bf16[128,2048]{1,0:T(8,128)(2,1)S(1)} %get-tuple-element.28), channel_id=1, source_target_pairs={{0,1},{3,2},{4,5},{7,6},{8,9},{11,10},{12,13},{15,14},{16,17},{19,... | collective-permute-start | bytes 1572872 | tf_op jit(solution)/shard_map/ppermute | solution.py:54
  80.2 32.9 %collective-permute-start.8 = (bf16[128,2048]{1,0:T(8,128)(2,1)S(1)}, bf16[128,2048]{1,0:T(8,128)(2,1)S(1)}, u32[]{:S(2)}, u32[]{:S(2)}) collective-permute-start(bf16[128,2048]{1,0:T(8,128)(2,1)S(1)} %get-tuple-element.26), channel_id=1, source_target_pairs={{0,1},{1,0},{2,3},{3,2},{4,5},{5,4},{6,7},{7,6},{8,9},{9,8},{10,11... | collective-permute-start | bytes 1572872 | tf_op jit(solution)/shard_map/ppermute | solution.py:54
  91.2 21.9 %collective-permute-start.10 = (bf16[128,2048]{1,0:T(8,128)(2,1)S(1)}, bf16[128,2048]{1,0:T(8,128)(2,1)S(1)}, u32[]{:S(2)}, u32[]{:S(2)}) collective-permute-start(bf16[128,2048]{1,0:T(8,128)(2,1)S(1)} %add_convert_fusion.3), channel_id=1, source_target_pairs={{1,2},{2,1},{5,6},{6,5},{9,10},{10,9},{13,14},{14,13},{17,18},{18,... | collective-permute-start | bytes 1572872 | tf_op jit(solution)/shard_map/ppermute | solution.py:54
  102.4 16.9 %collective-permute-start.12 = (bf16[128,2048]{1,0:T(8,128)(2,1)S(1)}, bf16[128,2048]{1,0:T(8,128)(2,1)S(1)}, u32[]{:S(2)}, u32[]{:S(2)}) collective-permute-start(bf16[128,2048]{1,0:T(8,128)(2,1)S(1)} %add_convert_fusion.2), channel_id=1, source_target_pairs={{2,0},{1,3},{6,4},{5,7},{10,8},{9,11},{14,12},{13,15},{18,16},{17,... | collective-permute-start | bytes 1572872 | tf_op jit(solution)/shard_map/ppermute | solution.py:54
  113.1 6.3 %copy-start.15 = (bf16[128,2048]{1,0:T(8,128)(2,1)}, bf16[128,2048]{1,0:T(8,128)(2,1)S(1)}, u32[]{:S(2)}) copy-start(bf16[128,2048]{1,0:T(8,128)(2,1)S(1)} %collective-permute-done.8.refs_1_) | copy-start | bytes 1572868
  113.1 6.3 %copy-start.17 = (bf16[128,2048]{1,0:T(8,128)(2,1)}, bf16[128,2048]{1,0:T(8,128)(2,1)S(1)}, u32[]{:S(2)}) copy-start(bf16[128,2048]{1,0:T(8,128)(2,1)S(1)} %collective-permute-done.10.refs_2_) | copy-start | bytes 1572868
  119.3 0.8 copy-start.19
  123.3 14.0 %collective-permute-start.16 = (bf16[128,2048]{1,0:T(8,128)(2,1)}, bf16[128,2048]{1,0:T(8,128)(2,1)S(1)}, u32[]{:S(2)}, u32[]{:S(2)}) collective-permute-start(bf16[128,2048]{1,0:T(8,128)(2,1)} %get-tuple-element.29.refs_0_), channel_id=1, source_target_pairs={{0,2},{3,1},{4,6},{7,5},{8,10},{11,9},{12,14},{15,13},{16,18},{19,... | collective-permute-start | bytes 1572872 | tf_op jit(solution)/shard_map/ppermute | solution.py:54
  124.7 14.0 %collective-permute-start.14 = (bf16[128,2048]{1,0:T(8,128)(2,1)}, bf16[128,2048]{1,0:T(8,128)(2,1)S(1)}, u32[]{:S(2)}, u32[]{:S(2)}) collective-permute-start(bf16[128,2048]{1,0:T(8,128)(2,1)} %get-tuple-element.29.refs_0_), channel_id=1, source_target_pairs={{1,2},{2,1},{5,6},{6,5},{9,10},{10,9},{13,14},{14,13},{17,18},{18,... | collective-permute-start | bytes 1572872 | tf_op jit(solution)/shard_map/ppermute | solution.py:54
  125.4 21.6 %collective-permute-start.13 = (bf16[128,2048]{1,0:T(8,128)(2,1)}, bf16[128,2048]{1,0:T(8,128)(2,1)S(1)}, u32[]{:S(2)}, u32[]{:S(2)}) collective-permute-start(bf16[128,2048]{1,0:T(8,128)(2,1)} %get-tuple-element.29.refs_0_), channel_id=1, source_target_pairs={{0,1},{1,0},{2,3},{3,2},{4,5},{5,4},{6,7},{7,6},{8,9},{9,8},{10,11... | collective-permute-start | bytes 1572872 | tf_op jit(solution)/shard_map/ppermute | solution.py:54
  137.4 12.6 %collective-permute-start.17 = (bf16[128,2048]{1,0:T(8,128)(2,1)S(1)}, bf16[128,2048]{1,0:T(8,128)(2,1)S(1)}, u32[]{:S(2)}, u32[]{:S(2)}) collective-permute-start(bf16[128,2048]{1,0:T(8,128)(2,1)S(1)} %collective-permute-done.16.refs_4_), channel_id=1, source_target_pairs={{1,0},{2,3},{5,4},{6,7},{9,8},{10,11},{13,12},{14,15},{17,16},{18,... | collective-permute-start | bytes 1572872 | tf_op jit(solution)/shard_map/ppermute | solution.py:54
  138.6 23.8 %collective-permute-start.15 = (bf16[128,2048]{1,0:T(8,128)(2,1)S(1)}, bf16[128,2048]{1,0:T(8,128)(2,1)S(1)}, u32[]{:S(2)}, u32[]{:S(2)}) collective-permute-start(bf16[128,2048]{1,0:T(8,128)(2,1)S(1)} %collective-permute-done.14.refs_2_), channel_id=1, source_target_pairs={{1,0},{2,3},{5,4},{6,7},{9,8},{10,11},{13,12},{14,15},{17,16},{18,... | collective-permute-start | bytes 1572872 | tf_op jit(solution)/shard_map/ppermute | solution.py:54
  150.0 0.8 copy-start.8
  162.4 0.8 copy-start.10
  163.2 5.9 %copy-start.6 = (bf16[6144,1408]{1,0:T(8,128)(2,1)S(1)}, bf16[6144,1408]{1,0:T(8,128)(2,1)}, u32[]{:S(2)}) copy-start(bf16[6144,1408]{1,0:T(8,128)(2,1)} %all-gather.2.cloned.1.call-done.refs_6_) | copy-start | bytes 51904516
  169.2 1.0 copy-start.7
  170.2 1.0 copy-start.9
  171.2 1.0 copy-start.11
  182.5 0.8 copy-start
  183.3 13.8 %collective-permute-start.19 = (bf16[128,2048]{1,0:T(8,128)(2,1)S(1)}, bf16[128,2048]{1,0:T(8,128)(2,1)S(1)}, u32[]{:S(2)}, u32[]{:S(2)}) collective-permute-start(bf16[128,2048]{1,0:T(8,128)(2,1)S(1)} %get-tuple-element.33), channel_id=1, source_target_pairs={{0,1},{3,2},{4,5},{7,6},{8,9},{11,10},{12,13},{15,14},{16,17},{19,... | collective-permute-start | bytes 1572872 | tf_op jit(solution)/shard_map/ppermute | solution.py:54
  184.8 23.5 %collective-permute-start.21 = (bf16[128,2048]{1,0:T(8,128)(2,1)S(1)}, bf16[128,2048]{1,0:T(8,128)(2,1)S(1)}, u32[]{:S(2)}, u32[]{:S(2)}) collective-permute-start(bf16[128,2048]{1,0:T(8,128)(2,1)S(1)} %get-tuple-element.34), channel_id=1, source_target_pairs={{0,1},{3,2},{4,5},{7,6},{8,9},{11,10},{12,13},{15,14},{16,17},{19,... | collective-permute-start | bytes 1572872 | tf_op jit(solution)/shard_map/ppermute | solution.py:54
  186.1 32.2 %collective-permute-start.18 = (bf16[128,2048]{1,0:T(8,128)(2,1)S(1)}, bf16[128,2048]{1,0:T(8,128)(2,1)S(1)}, u32[]{:S(2)}, u32[]{:S(2)}) collective-permute-start(bf16[128,2048]{1,0:T(8,128)(2,1)S(1)} %get-tuple-element.32), channel_id=1, source_target_pairs={{0,1},{1,0},{2,3},{3,2},{4,5},{5,4},{6,7},{7,6},{8,9},{9,8},{10,11... | collective-permute-start | bytes 1572872 | tf_op jit(solution)/shard_map/ppermute | solution.py:54
  197.2 21.1 %collective-permute-start.20 = (bf16[128,2048]{1,0:T(8,128)(2,1)S(1)}, bf16[128,2048]{1,0:T(8,128)(2,1)S(1)}, u32[]{:S(2)}, u32[]{:S(2)}) collective-permute-start(bf16[128,2048]{1,0:T(8,128)(2,1)S(1)} %add_convert_fusion.1), channel_id=1, source_target_pairs={{1,2},{2,1},{5,6},{6,5},{9,10},{10,9},{13,14},{14,13},{17,18},{18,... | collective-permute-start | bytes 1572872 | tf_op jit(solution)/shard_map/ppermute | solution.py:54
  208.5 15.3 %collective-permute-start.22 = (bf16[128,2048]{1,0:T(8,128)(2,1)S(1)}, bf16[128,2048]{1,0:T(8,128)(2,1)S(1)}, u32[]{:S(2)}, u32[]{:S(2)}) collective-permute-start(bf16[128,2048]{1,0:T(8,128)(2,1)S(1)} %add_convert_fusion), channel_id=1, source_target_pairs={{2,0},{1,3},{6,4},{5,7},{10,8},{9,11},{14,12},{13,15},{18,16},{17,... | collective-permute-start | bytes 1572872 | tf_op jit(solution)/shard_map/ppermute | solution.py:54
  218.3 5.4 %copy-start.14 = (bf16[128,2048]{1,0:T(8,128)(2,1)}, bf16[128,2048]{1,0:T(8,128)(2,1)S(1)}, u32[]{:S(2)}) copy-start(bf16[128,2048]{1,0:T(8,128)(2,1)S(1)} %collective-permute-done.18.refs_1_) | copy-start | bytes 1572868
  218.3 5.4 %copy-start.16 = (bf16[128,2048]{1,0:T(8,128)(2,1)}, bf16[128,2048]{1,0:T(8,128)(2,1)S(1)}, u32[]{:S(2)}) copy-start(bf16[128,2048]{1,0:T(8,128)(2,1)S(1)} %collective-permute-done.20.refs_2_) | copy-start | bytes 1572868
  223.7 0.8 copy-start.18
Sparse Core Ops, SparseCore 0:
  60.2 96.5 all-gather.1

commit v3 on v2

--- a/solution.py
+++ b/solution.py
@@ -65,11 +65,11 @@
 def gather_line(value, count):
     if count != 4:
         return [[value]] + [[shift(value, "seq", count, k)] for k in range(1, count)]
-    near = along(value, count, [(0, 1), (1, 0), (2, 3), (3, 2)])
     middle = along(value, count, [(1, 2), (2, 1)])
     far = along(value, count, [(0, 2), (3, 1)])
     middle_on = along(middle, count, [(1, 0), (2, 3)])
     far_on = along(far, count, [(1, 0), (2, 3)])
+    near = along(value, count, [(0, 1), (1, 0), (2, 3), (3, 2)])
     return [[value], [near], [middle, middle_on], [far, far_on]]
 
 
@@ -358,12 +358,12 @@
     return [[next(refs) for _ in range(count)] for count in counts]
 
 
-def forward_kernel(terms, shares, strips, *refs):
+def forward_kernel(terms, strips, *refs):
     x_refs, weights, refs = refs[: sum(terms)], refs[sum(terms)], refs[sum(terms) + 1 :]
     count = len(terms)
-    outs, (x, inner, spare, sems) = refs[:count], refs[count:]
+    outs, (x, inner, spare, gate_up, down, sems, weight_sems) = refs[:count], refs[count:]
     rows = x_refs[0].shape[0]
-    depth = x.shape[1] // shares
+    shares, depth, hidden = down.shape
     copies, spares = [], iter(range(sum(terms)))
     for k, arrays in enumerate(unflatten(x_refs, terms)):
         copies.append([])
@@ -373,6 +373,20 @@
             copy = pltpu.make_async_copy(array, target, sems.at[spot])
             copy.start()
             copies[k].append((copy, None if i == 0 else spot - k - 1))
+    weights = weights.reshape(shares, 3 * depth, hidden)
+    weight_copies = []
+    for i, strip in enumerate(strips):
+        columns = pl.ds(*strip)
+        weight_copies.append(
+            pltpu.make_async_copy(
+                weights.at[:, : 2 * depth, columns], gate_up.at[:, :, columns], weight_sems.at[i]
+            )
+        )
+    weight_copies.append(
+        pltpu.make_async_copy(weights.at[:, 2 * depth :, :], down, weight_sems.at[len(strips)])
+    )
+    for copy in weight_copies:
+        copy.start()
     for k, group in enumerate(copies):
         for copy, spot in group:
             copy.wait()
@@ -382,21 +396,21 @@
     def product(which, start, size):
         total = None
         for r in range(shares):
-            low = (3 * r + which) * depth
             term = jnp.dot(
                 x[:, r * depth : (r + 1) * depth],
-                weights[low : low + depth, start : start + size],
+                gate_up[r, which * depth : (which + 1) * depth, start : start + size],
                 preferred_element_type=F32,
             )
             total = term if total is None else total + term
         return total
 
-    for start, size in strips:
+    for (start, size), copy in zip(strips, weight_copies):
+        copy.wait()
         opened, upward = product(0, start, size), product(1, start, size)
         inner[:, start : start + size] = (silu(opened) * upward).astype(BF16)
+    weight_copies[-1].wait()
     for r in range(shares):
-        low = (3 * r + 2) * depth
-        term = dot_nt(inner[...], weights[low : low + depth, :]).astype(BF16)
+        term = dot_nt(inner[...], down[r]).astype(BF16)
         for k in range(count):
             outs[k][:, r * depth : (r + 1) * depth] = term[k * rows : (k + 1) * rows]
 
@@ -404,23 +418,27 @@
 def forward(xs, weights, shares):
     rows, width = xs[0][0].shape
     count, hidden = len(xs), weights.shape[1]
+    depth = width // shares
     total = count * rows
     strips = [(start, min(STRIP, hidden - start)) for start in range(0, hidden, STRIP)]
     terms = [len(arrays) for arrays in xs]
     return pl.pallas_call(
-        functools.partial(forward_kernel, terms, shares, strips),
+        functools.partial(forward_kernel, terms, strips),
         out_shape=(jax.ShapeDtypeStruct((rows, width), BF16),) * count,
-        in_specs=[ANY] * sum(terms) + [VMEM],
+        in_specs=[ANY] * (sum(terms) + 1),
         out_specs=(VMEM,) * count,
         scratch_shapes=[
             pltpu.VMEM((total, width), BF16),
             pltpu.VMEM((total, hidden), BF16),
             pltpu.VMEM((max(1, sum(terms) - count), rows, width), BF16),
+            pltpu.VMEM((shares, 2 * depth, hidden), BF16),
+            pltpu.VMEM((shares, depth, hidden), BF16),
             pltpu.SemaphoreType.DMA((sum(terms),)),
+            pltpu.SemaphoreType.DMA((len(strips) + 1,)),
         ],
-        compiler_params=pltpu.CompilerParams(vmem_limit_bytes=28 * MIB),
+        compiler_params=pltpu.CompilerParams(vmem_limit_bytes=58 * MIB),
         cost_estimate=pl.CostEstimate(
-            flops=6 * total * width * hidden, bytes_accessed=4 * MIB, transcendentals=0
+            flops=6 * total * width * hidden, bytes_accessed=20 * MIB, transcendentals=0
         ),
         name="feed_forward",
     )(*sum(xs, []), weights)
@@ -493,7 +511,9 @@
     mixed, state = delta(xs, where, lengths, slot_request, conv_weight, norm_gain[None, :], heads)
     ys = project(mixed, where, owners_of(count), out_parts)
     stream, normed = norm(sum_line(ys, count), residual[0], mlp_gain[None, :])
-    ys = forward(gather_line(normed, count), weights, n_req)
+    blocks = gather_line(normed, count)
+    half = (count + 1) // 2
+    ys = forward(blocks[:half], weights, n_req) + forward(blocks[half:], weights, n_req)
     hidden = finish(sum_line(ys, count), where, lengths, slot_request, stream)
     return hidden[None], state[None], conv_edge[None]
 

time: 235 us -> 224 us (0.953)
  waiting for transfers between devices: 108 us -> 87.2 us
  starting transfers between devices: 62.6 us -> 74 us
  local copies, waits for them, and re-layouts: 15.4 us -> 5.55 us
  Pallas kernels: 29.1 us -> 37.8 us
    ppermute x15, waiting for transfers between devices: 104 us -> 82.8 us  [along(): return lax.ppermute(value, 'seq', pairs)]
    ppermute x15, starting transfers between devices: 22 us -> 33.4 us  [along(): return lax.ppermute(value, 'seq', pairs)]
    unnamed x44 -> x42, local copies, waits for them, and re-layouts: 15.4 us -> 5.53 us
    pallas_call x1 -> x2, Pallas kernels: 10.2 us -> 18.9 us  [forward(): pl.pallas_call(functools.partial(forward_kernel, terms, strips), out_shap...]
  transfers between devices with their start and end apart: 24 -> 24, of which waited for: 14 -> 12; matrix products, arithmetic and copies ran while one was open for 3% -> 3% of each run, Pallas kernels for 7% -> 16%
where the time goes in v3:
time: 224 us
  waiting for transfers between devices  87.2 us (39%)
  starting transfers between devices  74 us (33%)
  Pallas kernels  37.8 us (17%)
  between operations  14.4 us (6%)
  local copies, waits for them, and re-layouts  5.55 us (2%)
  other arithmetic  4.68 us (2%)
    ppermute x15, waiting for transfers between devices, along(): return lax.ppermute(value, 'seq', pairs)  82.8 us
    ppermute x15, starting transfers between devices, along(): return lax.ppermute(value, 'seq', pairs)  33.4 us
    ppermute x4, starting transfers between devices, flip(): lax.ppermute(value, 'req', [(i, i ^ bits) for i in range(lax.axis_size('r...  30.4 us
    pallas_call x2, Pallas kernels, forward(): pl.pallas_call(functools.partial(forward_kernel, terms, strips), out_shap...  18.9 us
    ppermute x3, starting transfers between devices, shift(): lax.ppermute(value, axis, [(i, (i + steps) % count) for i in range(count)])  8.53 us
    pallas_call x1, Pallas kernels, delta(): pl.pallas_call(functools.partial(delta_kernel, count, heads, piece), out_...  6.59 us
    unnamed x42, local copies, waits for them, and re-layouts  5.53 us
  transfers between devices with their start and end apart: 24, of which 12 were waited for; matrix products, arithmetic and copies ran while one was open for 3% of the time, Pallas kernels for 16%

profile of v3, /device:TPU:0, one launch (start us, length us, event | category | flops | bytes accessed | tf_op | source)
XLA Modules:
  0.0 223.6 jit_solution(5348273219211172561)
XLA Ops:
  7.2 0.0 all-gather.2.cloned.1.call-start
  7.2 1.6 collective-permute-start.3
  8.8 0.7 pad_add_fusion.refs_0_.refs_4_
  9.5 2.9 %pack.1 = (bf16[144,1536]{1,0:T(8,128)(2,1)}, bf16[144,1536]{1,0:T(8,128)(2,1)}, bf16[144,1536]{1,0:T(8,128)(2,1)}, bf16[144,1536]{1,0:T(8,128)(2,1)}) custom-call(s32[2]{0:T(128)} %pad_add_fusion.refs_0_.refs_4_, s32[8]{0:T(128)} %refs_5_.3, s32[8]{0:T(128)} %refs_6_.3, bf16[128,4096]{1,0:T(8,128)(2,1)} %bitcast.23, bf16[128,2048]{1,0:T(8,128)(2,1)} %bitcast.26, ...), custom_call_target="tpu_custom_call" | custom-call | tf_op jit(solution)/shard_map/pack/pallas_call | solution.py:145
  12.4 3.3 %collective-permute-start = (bf16[144,1536]{1,0:T(8,128)(2,1)}, bf16[144,1536]{1,0:T(8,128)(2,1)S(1)}, u32[]{:S(2)}, u32[]{:S(2)}) collective-permute-start(bf16[144,1536]{1,0:T(8,128)(2,1)} %get-tuple-element.21), channel_id=1, source_target_pairs={{0,1},{1,2},{2,3},{3,0},{4,5},{5,6},{6,7},{7,4},{8,9},{9,10},{10,1... | collective-permute-start | bytes 1327112 | tf_op jit(solution)/shard_map/ppermute | solution.py:42
  15.7 3.2 %collective-permute-start.1 = (bf16[144,1536]{1,0:T(8,128)(2,1)}, bf16[144,1536]{1,0:T(8,128)(2,1)S(1)}, u32[]{:S(2)}, u32[]{:S(2)}) collective-permute-start(bf16[144,1536]{1,0:T(8,128)(2,1)} %get-tuple-element.22), channel_id=1, source_target_pairs={{0,2},{1,3},{2,0},{3,1},{4,6},{5,7},{6,4},{7,5},{8,10},{9,11},{10,... | collective-permute-start | bytes 1327112 | tf_op jit(solution)/shard_map/ppermute | solution.py:42
  18.9 2.0 collective-permute-start.2
  20.9 1.4 copy.17
  22.4 0.0 copy-start.2
  22.4 0.0 copy-start.4
  22.4 0.0 copy-start.5
  22.4 0.0 copy-start.6
  22.5 25.3 %collective-permute-start.4 = (bf16[64,2048]{1,0:T(8,128)(2,1)S(1)}, bf16[64,2048]{1,0:T(8,128)(2,1)S(1)}, u32[]{:S(2)}, u32[]{:S(2)}) collective-permute-start(bf16[64,2048]{1,0:T(8,128)(2,1)S(1)} %collective-permute-done.3), channel_id=1, source_target_pairs={{0,8},{4,12},{8,0},{12,4},{16,24},{20,28},{24,16},{28,20},{1,9},{5... | collective-permute-start | bytes 786440 | tf_op jit(solution)/shard_map/ppermute | solution.py:46
  47.8 2.8 %pad_maximum_fusion = bf16[768,1408]{1,0:T(8,128)(2,1)} fusion(bf16[256,1408]{1,0:T(8,128)(2,1)S(1)} %bitcast.22, bf16[256,1408]{1,0:T(8,128)(2,1)} %param.26, bf16[256,1408]{1,0:T(8,128)(2,1)} %param.25), kind=kLoop, calls=%fused_computation | loop fusion | flops 6488064 | bytes 4325376 | tf_op jit(solution)/shard_map/concatenate | solution.py:509
  50.6 2.0 collective-permute-start.5
  52.6 3.0 %collective-permute-start.6 = (bf16[64,2048]{1,0:T(8,128)(2,1)S(1)}, bf16[64,2048]{1,0:T(8,128)(2,1)S(1)}, u32[]{:S(2)}, u32[]{:S(2)}) collective-permute-start(bf16[64,2048]{1,0:T(8,128)(2,1)S(1)} %collective-permute-done.3), channel_id=1, source_target_pairs={{0,24},{4,28},{8,16},{12,20},{16,8},{20,12},{24,0},{28,4},{1,25},{... | collective-permute-start | bytes 786440 | tf_op jit(solution)/shard_map/ppermute | solution.py:46
  55.6 3.7 %collective-permute-done.5 = bf16[64,2048]{1,0:T(8,128)(2,1)S(1)} collective-permute-done((bf16[64,2048]{1,0:T(8,128)(2,1)S(1)}, bf16[64,2048]{1,0:T(8,128)(2,1)S(1)}, u32[]{:S(2)}, u32[]{:S(2)}) %collective-permute-start.5) | collective-permute-done | bytes 262176 | tf_op jit(solution)/shard_map/ppermute | solution.py:46
  59.4 0.6 collective-permute-done.6
  60.0 0.0 all-gather.2.cloned.1.call-update
  60.1 0.1 collective-permute-start.7
  60.1 0.1 pad_add_fusion.1.refs_1_
  60.3 6.6 %delta_rule.1 = (bf16[4,128,512]{2,1,0:T(8,128)(2,1)S(1)}, f32[2,128,256]{2,1,0:T(8,128)}) custom-call(bf16[144,1536]{1,0:T(8,128)(2,1)S(1)} %copy-done.4, bf16[144,1536]{1,0:T(8,128)(2,1)S(1)} %collective-permute-done.refs_1_, bf16[144,1536]{1,0:T(8,128)(2,1)S(1)} %collective-permute-done.1.refs_2_, bf16[144,1536]{1,0:T(8,128)(2,1)S(1)} %collective-permute-done.2.refs_3_, ...), custom_call_target="tpu_custom_call" | custom-call | flops 4000000000 | bytes 4194304 | tf_op jit(solution)/shard_map/delta_rule/pallas_call | solution.py:273
  66.9 3.3 %output_projection.1 = (bf16[128,2048]{1,0:T(8,128)(2,1)S(1)}, bf16[128,2048]{1,0:T(8,128)(2,1)S(1)}, bf16[128,2048]{1,0:T(8,128)(2,1)S(1)}, bf16[128,2048]{1,0:T(8,128)(2,1)S(1)}) custom-call(s32[2]{0:T(128)S(1)} %copy-done.3, s32[4]{0:T(128)S(1)} %pad_add_fusion.1.refs_1_, bf16[4,128,512]{2,1,0:T(8,128)(2,1)S(1)} %get-tuple-element.24.refs_2_, ...), custom_call_target="tpu_custom_call" | custom-call | flops 1073741824 | bytes 4194304 | tf_op jit(solution)/shard_map/output_projection/pallas_call | solution.py:319
  70.2 0.0 copy-start
  70.2 0.8 copy-done
  71.0 7.9 %collective-permute-start.9 = (bf16[128,2048]{1,0:T(8,128)(2,1)S(1)}, bf16[128,2048]{1,0:T(8,128)(2,1)S(1)}, u32[]{:S(2)}, u32[]{:S(2)}) collective-permute-start(bf16[128,2048]{1,0:T(8,128)(2,1)S(1)} %get-tuple-element.27), channel_id=1, source_target_pairs={{0,1},{3,2},{4,5},{7,6},{8,9},{11,10},{12,13},{15,14},{16,17},{19,... | collective-permute-start | bytes 1572872 | tf_op jit(solution)/shard_map/ppermute | solution.py:54
  78.9 1.3 collective-permute-start.11
  80.2 0.1 collective-permute-start.8
  80.3 10.8 %collective-permute-done.9 = bf16[128,2048]{1,0:T(8,128)(2,1)S(1)} collective-permute-done((bf16[128,2048]{1,0:T(8,128)(2,1)S(1)}, bf16[128,2048]{1,0:T(8,128)(2,1)S(1)}, u32[]{:S(2)}, u32[]{:S(2)}) %collective-permute-start.9) | collective-permute-done | bytes 524320 | tf_op jit(solution)/shard_map/ppermute | solution.py:54
  91.1 0.1 add_convert_fusion.3
  91.2 0.7 collective-permute-start.10
  91.9 10.4 %collective-permute-done.11 = bf16[128,2048]{1,0:T(8,128)(2,1)S(1)} collective-permute-done((bf16[128,2048]{1,0:T(8,128)(2,1)S(1)}, bf16[128,2048]{1,0:T(8,128)(2,1)S(1)}, u32[]{:S(2)}, u32[]{:S(2)}) %collective-permute-start.11) | collective-permute-done | bytes 524320 | tf_op jit(solution)/shard_map/ppermute | solution.py:54
  102.3 0.1 add_convert_fusion.2
  102.4 1.3 collective-permute-start.12
  103.7 9.3 %collective-permute-done.8.refs_1_ = bf16[128,2048]{1,0:T(8,128)(2,1)S(1)} collective-permute-done((bf16[128,2048]{1,0:T(8,128)(2,1)S(1)}, bf16[128,2048]{1,0:T(8,128)(2,1)S(1)}, u32[]{:S(2)}, u32[]{:S(2)}) %collective-permute-start.8) | collective-permute-done | bytes 524320 | tf_op jit(solution)/shard_map/ppermute | solution.py:54
  113.1 6.3 %collective-permute-done.12.refs_3_ = bf16[128,2048]{1,0:T(8,128)(2,1)S(1)} collective-permute-done((bf16[128,2048]{1,0:T(8,128)(2,1)S(1)}, bf16[128,2048]{1,0:T(8,128)(2,1)S(1)}, u32[]{:S(2)}, u32[]{:S(2)}) %collective-permute-start.12) | collective-permute-done | bytes 524320 | tf_op jit(solution)/shard_map/ppermute | solution.py:54
  119.3 0.8 copy-done.18
  120.1 3.2 %stream_norm.1 = (bf16[128,2048]{1,0:T(8,128)(2,1)}, bf16[128,2048]{1,0:T(8,128)(2,1)}) custom-call(bf16[128,2048]{1,0:T(8,128)(2,1)} %copy-done, bf16[128,2048]{1,0:T(8,128)(2,1)} %copy-done.9, bf16[128,2048]{1,0:T(8,128)(2,1)} %copy-done.15, bf16[128,2048]{1,0:T(8,128)(2,1)} %copy-done.18, bf16[128,2048]{1,0:T(8,128)(2,1)} %bitcast.24, f32[1,2048]{1,0:T(1,128)} %bitcast.27), custom_call_target="tpu_custom_call" | custom-call | tf_op jit(solution)/shard_map/stream_norm/pallas_call | solution.py:347
  123.3 1.3 collective-permute-start.17
  124.7 0.7 collective-permute-start.15
  125.4 10.4 %collective-permute-done.17.refs_2_ = bf16[128,2048]{1,0:T(8,128)(2,1)S(1)} collective-permute-done((bf16[128,2048]{1,0:T(8,128)(2,1)}, bf16[128,2048]{1,0:T(8,128)(2,1)S(1)}, u32[]{:S(2)}, u32[]{:S(2)}) %collective-permute-start.17) | collective-permute-done | bytes 524320 | tf_op jit(solution)/shard_map/ppermute | solution.py:54
  135.7 1.3 collective-permute-start.18
  137.1 1.5 collective-permute-start.16
  138.5 12.5 %collective-permute-start.13 = (bf16[128,2048]{1,0:T(8,128)(2,1)}, bf16[128,2048]{1,0:T(8,128)(2,1)S(1)}, u32[]{:S(2)}, u32[]{:S(2)}) collective-permute-start(bf16[128,2048]{1,0:T(8,128)(2,1)} %get-tuple-element.29.refs_0_), channel_id=1, source_target_pairs={{0,1},{1,0},{2,3},{3,2},{4,5},{5,4},{6,7},{7,6},{8,9},{9,8},{10,11... | collective-permute-start | bytes 1572872 | tf_op jit(solution)/shard_map/ppermute | solution.py:54
  151.1 0.8 copy-done.16
  151.9 11.2 %collective-permute-done.16.refs_1_ = bf16[128,2048]{1,0:T(8,128)(2,1)} collective-permute-done((bf16[128,2048]{1,0:T(8,128)(2,1)S(1)}, bf16[128,2048]{1,0:T(8,128)(2,1)}, u32[]{:S(2)}, u32[]{:S(2)}) %collective-permute-start.16) | collective-permute-done | bytes 524320 | tf_op jit(solution)/shard_map/ppermute | solution.py:54
  163.1 9.6 %feed_forward.3 = (bf16[128,2048]{1,0:T(8,128)(2,1)}, bf16[128,2048]{1,0:T(8,128)(2,1)}) custom-call(bf16[128,2048]{1,0:T(8,128)(2,1)} %copy-done.13, bf16[128,2048]{1,0:T(8,128)(2,1)} %collective-permute-done.16.refs_1_, bf16[128,2048]{1,0:T(8,128)(2,1)} %copy-done.10, bf16[128,2048]{1,0:T(8,128)(2,1)} %copy-done.16, ...), custom_call_target="tpu_custom_call" | custom-call | flops 4429185024 | bytes 20971520 | tf_op jit(solution)/shard_map/feed_forward/pallas_call | solution.py:425
  172.7 1.4 collective-permute-start.19
  174.1 1.5 collective-permute-start.21
  175.6 0.0 copy-start.11
  175.6 0.8 copy-done.11
  176.3 9.3 %feed_forward.2 = (bf16[128,2048]{1,0:T(8,128)(2,1)}, bf16[128,2048]{1,0:T(8,128)(2,1)}) custom-call(bf16[128,2048]{1,0:T(8,128)(2,1)} %get-tuple-element.29.refs_0_, bf16[128,2048]{1,0:T(8,128)(2,1)} %copy-done.11, bf16[6144,1408]{1,0:T(8,128)(2,1)} %all-gather.2.cloned.1.call-done.refs_2_.refs_4_), custom_call_target="tpu_custom_call" | custom-call | flops 4429185024 | bytes 20971520 | tf_op jit(solution)/shard_map/feed_forward/pallas_call | solution.py:425
  185.6 0.1 collective-permute-start.14
  185.7 1.0 collective-permute-done.19
  186.7 0.1 add_convert_fusion.1
  186.8 0.7 collective-permute-start.20
  187.5 10.4 %collective-permute-done.21 = bf16[128,2048]{1,0:T(8,128)(2,1)S(1)} collective-permute-done((bf16[128,2048]{1,0:T(8,128)(2,1)}, bf16[128,2048]{1,0:T(8,128)(2,1)S(1)}, u32[]{:S(2)}, u32[]{:S(2)}) %collective-permute-start.21) | collective-permute-done | bytes 524320 | tf_op jit(solution)/shard_map/ppermute | solution.py:54
  197.9 0.1 add_convert_fusion
  198.1 1.3 collective-permute-start.22
  199.4 0.6 fusion
  200.0 7.5 %collective-permute-done.14.refs_1_ = bf16[128,2048]{1,0:T(8,128)(2,1)S(1)} collective-permute-done((bf16[128,2048]{1,0:T(8,128)(2,1)}, bf16[128,2048]{1,0:T(8,128)(2,1)S(1)}, u32[]{:S(2)}, u32[]{:S(2)}) %collective-permute-start.14) | collective-permute-done | bytes 524320 | tf_op jit(solution)/shard_map/ppermute | solution.py:54
  207.5 5.6 %collective-permute-done.22.refs_3_ = bf16[128,2048]{1,0:T(8,128)(2,1)S(1)} collective-permute-done((bf16[128,2048]{1,0:T(8,128)(2,1)S(1)}, bf16[128,2048]{1,0:T(8,128)(2,1)S(1)}, u32[]{:S(2)}, u32[]{:S(2)}) %collective-permute-start.22) | collective-permute-done | bytes 524320 | tf_op jit(solution)/shard_map/ppermute | solution.py:54
  213.1 0.8 copy-done.17
  213.9 2.8 %last_sum.1 = bf16[128,2048]{1,0:T(8,128)(2,1)} custom-call(bf16[128,2048]{1,0:T(8,128)(2,1)} %get-tuple-element.31.refs_0_, bf16[128,2048]{1,0:T(8,128)(2,1)} %copy-done.7, bf16[128,2048]{1,0:T(8,128)(2,1)} %copy-done.12, bf16[128,2048]{1,0:T(8,128)(2,1)} %copy-done.17, s32[2]{0:T(128)} %pad_add_fusion.refs_0_.refs_4_, s32[8]{0:T(128)} %refs_5_.3, ...), custom_call_target="tpu_custom_call" | custom-call | tf_op jit(solution)/shard_map/last_sum/pallas_call | solution.py:460
  (43 shorter events, 0.2 us)
Async XLA Ops:
  7.2 155.9 %all-gather.2.cloned.1.call-start = ((), (), s32[]{:S(2)}) async-start(), calls=%async_computation | async-start | bytes 19464192 | tf_op jit(solution)/shard_map/all_gather | solution.py:510
  7.2 15.2 %collective-permute-start.3 = (bf16[64,2048]{1,0:T(8,128)(2,1)}, bf16[64,2048]{1,0:T(8,128)(2,1)S(1)}, u32[]{:S(2)}, u32[]{:S(2)}) collective-permute-start(bf16[64,2048]{1,0:T(8,128)(2,1)} %param.23), channel_id=1, source_target_pairs={{0,0},{1,4},{2,8},{3,12},{4,16},{5,20},{6,24},{7,28},{8,1},{9,5},{... | collective-permute-start | bytes 786440 | tf_op jit(solution)/shard_map/ppermute | solution.py:500
  12.4 47.6 %collective-permute-start = (bf16[144,1536]{1,0:T(8,128)(2,1)}, bf16[144,1536]{1,0:T(8,128)(2,1)S(1)}, u32[]{:S(2)}, u32[]{:S(2)}) collective-permute-start(bf16[144,1536]{1,0:T(8,128)(2,1)} %get-tuple-element.21), channel_id=1, source_target_pairs={{0,1},{1,2},{2,3},{3,0},{4,5},{5,6},{6,7},{7,4},{8,9},{9,10},{10,1... | collective-permute-start | bytes 1327112 | tf_op jit(solution)/shard_map/ppermute | solution.py:42
  15.7 44.3 %collective-permute-start.1 = (bf16[144,1536]{1,0:T(8,128)(2,1)}, bf16[144,1536]{1,0:T(8,128)(2,1)S(1)}, u32[]{:S(2)}, u32[]{:S(2)}) collective-permute-start(bf16[144,1536]{1,0:T(8,128)(2,1)} %get-tuple-element.22), channel_id=1, source_target_pairs={{0,2},{1,3},{2,0},{3,1},{4,6},{5,7},{6,4},{7,5},{8,10},{9,11},{10,... | collective-permute-start | bytes 1327112 | tf_op jit(solution)/shard_map/ppermute | solution.py:42
  18.9 41.1 %collective-permute-start.2 = (bf16[144,1536]{1,0:T(8,128)(2,1)}, bf16[144,1536]{1,0:T(8,128)(2,1)S(1)}, u32[]{:S(2)}, u32[]{:S(2)}) collective-permute-start(bf16[144,1536]{1,0:T(8,128)(2,1)} %get-tuple-element.23), channel_id=1, source_target_pairs={{0,3},{1,0},{2,1},{3,2},{4,7},{5,4},{6,5},{7,6},{8,11},{9,8},{10,9... | collective-permute-start | bytes 1327112 | tf_op jit(solution)/shard_map/ppermute | solution.py:42
  22.4 37.8 %copy-start.1 = (s32[8]{0:T(128)S(1)}, s32[8]{0:T(128)}, u32[]{:S(2)}) copy-start(s32[8]{0:T(128)} %refs_5_.3) | copy-start | bytes 100
  22.4 37.8 %copy-start.2 = (s32[8]{0:T(128)S(1)}, s32[8]{0:T(128)}, u32[]{:S(2)}) copy-start(s32[8]{0:T(128)} %refs_6_.3) | copy-start | bytes 100
  22.4 37.8 %copy-start.3 = (s32[2]{0:T(128)S(1)}, s32[2]{0:T(128)}, u32[]{:S(2)}) copy-start(s32[2]{0:T(128)} %pad_add_fusion.refs_0_.refs_4_) | copy-start | bytes 28
  22.4 37.8 %copy-start.4 = (bf16[144,1536]{1,0:T(8,128)(2,1)S(1)}, bf16[144,1536]{1,0:T(8,128)(2,1)}, u32[]{:S(2)}) copy-start(bf16[144,1536]{1,0:T(8,128)(2,1)} %get-tuple-element.20.refs_0_) | copy-start | bytes 1327108
  22.4 37.8 %copy-start.5 = (f32[4,4096]{1,0:T(4,128)S(1)}, f32[4,4096]{1,0:T(4,128)}, u32[]{:S(2)}) copy-start(f32[4,4096]{1,0:T(4,128)} %refs_7_.1) | copy-start | bytes 196612
  22.4 37.8 %copy-start.6 = (f32[256]{0:T(256)S(1)}, f32[256]{0:T(256)}, u32[]{:S(2)}) copy-start(f32[256]{0:T(256)} %param.22) | copy-start | bytes 3076
  22.5 30.2 %collective-permute-start.4 = (bf16[64,2048]{1,0:T(8,128)(2,1)S(1)}, bf16[64,2048]{1,0:T(8,128)(2,1)S(1)}, u32[]{:S(2)}, u32[]{:S(2)}) collective-permute-start(bf16[64,2048]{1,0:T(8,128)(2,1)S(1)} %collective-permute-done.3), channel_id=1, source_target_pairs={{0,8},{4,12},{8,0},{12,4},{16,24},{20,28},{24,16},{28,20},{1,9},{5... | collective-permute-start | bytes 786440 | tf_op jit(solution)/shard_map/ppermute | solution.py:46
  50.6 8.8 %collective-permute-start.5 = (bf16[64,2048]{1,0:T(8,128)(2,1)S(1)}, bf16[64,2048]{1,0:T(8,128)(2,1)S(1)}, u32[]{:S(2)}, u32[]{:S(2)}) collective-permute-start(bf16[64,2048]{1,0:T(8,128)(2,1)S(1)} %collective-permute-done.3), channel_id=1, source_target_pairs={{0,16},{4,20},{8,24},{12,28},{16,0},{20,4},{24,8},{28,12},{1,17},{... | collective-permute-start | bytes 786440 | tf_op jit(solution)/shard_map/ppermute | solution.py:46
  52.6 7.3 %collective-permute-start.6 = (bf16[64,2048]{1,0:T(8,128)(2,1)S(1)}, bf16[64,2048]{1,0:T(8,128)(2,1)S(1)}, u32[]{:S(2)}, u32[]{:S(2)}) collective-permute-start(bf16[64,2048]{1,0:T(8,128)(2,1)S(1)} %collective-permute-done.3), channel_id=1, source_target_pairs={{0,24},{4,28},{8,16},{12,20},{16,8},{20,12},{24,0},{28,4},{1,25},{... | collective-permute-start | bytes 786440 | tf_op jit(solution)/shard_map/ppermute | solution.py:46
  60.1 6.8 %collective-permute-start.7 = (bf16[256,2048]{1,0:T(8,128)(2,1)S(1)}, bf16[256,2048]{1,0:T(8,128)(2,1)}, u32[]{:S(2)}, u32[]{:S(2)}) collective-permute-start(bf16[256,2048]{1,0:T(8,128)(2,1)S(1)} %constant_dynamic-update-slice_fusion.refs_3_), channel_id=1, source_target_pairs={{0,4},{4,0},{8,12},{12,8},{16,20},{20,16},{24,28},{28,24},{1,5},{5... | collective-permute-start | bytes 3145736 | tf_op jit(solution)/shard_map/ppermute | solution.py:46
  70.2 0.8 copy-start
  71.0 20.1 %collective-permute-start.9 = (bf16[128,2048]{1,0:T(8,128)(2,1)S(1)}, bf16[128,2048]{1,0:T(8,128)(2,1)S(1)}, u32[]{:S(2)}, u32[]{:S(2)}) collective-permute-start(bf16[128,2048]{1,0:T(8,128)(2,1)S(1)} %get-tuple-element.27), channel_id=1, source_target_pairs={{0,1},{3,2},{4,5},{7,6},{8,9},{11,10},{12,13},{15,14},{16,17},{19,... | collective-permute-start | bytes 1572872 | tf_op jit(solution)/shard_map/ppermute | solution.py:54
  78.9 23.4 %collective-permute-start.11 = (bf16[128,2048]{1,0:T(8,128)(2,1)S(1)}, bf16[128,2048]{1,0:T(8,128)(2,1)S(1)}, u32[]{:S(2)}, u32[]{:S(2)}) collective-permute-start(bf16[128,2048]{1,0:T(8,128)(2,1)S(1)} %get-tuple-element.28), channel_id=1, source_target_pairs={{0,1},{3,2},{4,5},{7,6},{8,9},{11,10},{12,13},{15,14},{16,17},{19,... | collective-permute-start | bytes 1572872 | tf_op jit(solution)/shard_map/ppermute | solution.py:54
  80.2 32.9 %collective-permute-start.8 = (bf16[128,2048]{1,0:T(8,128)(2,1)S(1)}, bf16[128,2048]{1,0:T(8,128)(2,1)S(1)}, u32[]{:S(2)}, u32[]{:S(2)}) collective-permute-start(bf16[128,2048]{1,0:T(8,128)(2,1)S(1)} %get-tuple-element.26), channel_id=1, source_target_pairs={{0,1},{1,0},{2,3},{3,2},{4,5},{5,4},{6,7},{7,6},{8,9},{9,8},{10,11... | collective-permute-start | bytes 1572872 | tf_op jit(solution)/shard_map/ppermute | solution.py:54
  91.2 21.9 %collective-permute-start.10 = (bf16[128,2048]{1,0:T(8,128)(2,1)S(1)}, bf16[128,2048]{1,0:T(8,128)(2,1)S(1)}, u32[]{:S(2)}, u32[]{:S(2)}) collective-permute-start(bf16[128,2048]{1,0:T(8,128)(2,1)S(1)} %add_convert_fusion.3), channel_id=1, source_target_pairs={{1,2},{2,1},{5,6},{6,5},{9,10},{10,9},{13,14},{14,13},{17,18},{18,... | collective-permute-start | bytes 1572872 | tf_op jit(solution)/shard_map/ppermute | solution.py:54
  102.4 16.9 %collective-permute-start.12 = (bf16[128,2048]{1,0:T(8,128)(2,1)S(1)}, bf16[128,2048]{1,0:T(8,128)(2,1)S(1)}, u32[]{:S(2)}, u32[]{:S(2)}) collective-permute-start(bf16[128,2048]{1,0:T(8,128)(2,1)S(1)} %add_convert_fusion.2), channel_id=1, source_target_pairs={{2,0},{1,3},{6,4},{5,7},{10,8},{9,11},{14,12},{13,15},{18,16},{17,... | collective-permute-start | bytes 1572872 | tf_op jit(solution)/shard_map/ppermute | solution.py:54
  113.1 6.3 %copy-start.9 = (bf16[128,2048]{1,0:T(8,128)(2,1)}, bf16[128,2048]{1,0:T(8,128)(2,1)S(1)}, u32[]{:S(2)}) copy-start(bf16[128,2048]{1,0:T(8,128)(2,1)S(1)} %collective-permute-done.8.refs_1_) | copy-start | bytes 1572868
  113.1 6.3 %copy-start.15 = (bf16[128,2048]{1,0:T(8,128)(2,1)}, bf16[128,2048]{1,0:T(8,128)(2,1)S(1)}, u32[]{:S(2)}) copy-start(bf16[128,2048]{1,0:T(8,128)(2,1)S(1)} %collective-permute-done.10.refs_2_) | copy-start | bytes 1572868
  119.3 0.8 copy-start.18
  123.3 12.4 %collective-permute-start.17 = (bf16[128,2048]{1,0:T(8,128)(2,1)}, bf16[128,2048]{1,0:T(8,128)(2,1)S(1)}, u32[]{:S(2)}, u32[]{:S(2)}) collective-permute-start(bf16[128,2048]{1,0:T(8,128)(2,1)} %get-tuple-element.29.refs_0_), channel_id=1, source_target_pairs={{0,2},{3,1},{4,6},{7,5},{8,10},{11,9},{12,14},{15,13},{16,18},{19,... | collective-permute-start | bytes 1572872 | tf_op jit(solution)/shard_map/ppermute | solution.py:54
  124.7 12.4 %collective-permute-start.15 = (bf16[128,2048]{1,0:T(8,128)(2,1)}, bf16[128,2048]{1,0:T(8,128)(2,1)S(1)}, u32[]{:S(2)}, u32[]{:S(2)}) collective-permute-start(bf16[128,2048]{1,0:T(8,128)(2,1)} %get-tuple-element.29.refs_0_), channel_id=1, source_target_pairs={{1,2},{2,1},{5,6},{6,5},{9,10},{10,9},{13,14},{14,13},{17,18},{18,... | collective-permute-start | bytes 1572872 | tf_op jit(solution)/shard_map/ppermute | solution.py:54
  135.7 27.3 %copy-start.10 = (bf16[128,2048]{1,0:T(8,128)(2,1)}, bf16[128,2048]{1,0:T(8,128)(2,1)S(1)}, u32[]{:S(2)}) copy-start(bf16[128,2048]{1,0:T(8,128)(2,1)S(1)} %collective-permute-done.17.refs_2_) | copy-start | bytes 1572868
  135.7 15.3 %collective-permute-start.18 = (bf16[128,2048]{1,0:T(8,128)(2,1)S(1)}, bf16[128,2048]{1,0:T(8,128)(2,1)S(1)}, u32[]{:S(2)}, u32[]{:S(2)}) collective-permute-start(bf16[128,2048]{1,0:T(8,128)(2,1)S(1)} %collective-permute-done.17.refs_2_), channel_id=1, source_target_pairs={{1,0},{2,3},{5,4},{6,7},{9,8},{10,11},{13,12},{14,15},{17,16},{18,... | collective-permute-start | bytes 1572872 | tf_op jit(solution)/shard_map/ppermute | solution.py:54
  137.0 26.0 %copy-start.13 = (bf16[128,2048]{1,0:T(8,128)(2,1)}, bf16[128,2048]{1,0:T(8,128)(2,1)S(1)}, u32[]{:S(2)}) copy-start(bf16[128,2048]{1,0:T(8,128)(2,1)S(1)} %collective-permute-done.15.refs_0_) | copy-start | bytes 1572868
  137.1 26.0 %collective-permute-start.16 = (bf16[128,2048]{1,0:T(8,128)(2,1)S(1)}, bf16[128,2048]{1,0:T(8,128)(2,1)}, u32[]{:S(2)}, u32[]{:S(2)}) collective-permute-start(bf16[128,2048]{1,0:T(8,128)(2,1)S(1)} %collective-permute-done.15.refs_0_), channel_id=1, source_target_pairs={{1,0},{2,3},{5,4},{6,7},{9,8},{10,11},{13,12},{14,15},{17,16},{18,... | collective-permute-start | bytes 1572872 | tf_op jit(solution)/shard_map/ppermute | solution.py:54
  138.5 37.0 %collective-permute-start.13 = (bf16[128,2048]{1,0:T(8,128)(2,1)}, bf16[128,2048]{1,0:T(8,128)(2,1)S(1)}, u32[]{:S(2)}, u32[]{:S(2)}) collective-permute-start(bf16[128,2048]{1,0:T(8,128)(2,1)} %get-tuple-element.29.refs_0_), channel_id=1, source_target_pairs={{0,1},{1,0},{2,3},{3,2},{4,5},{5,4},{6,7},{7,6},{8,9},{9,8},{10,11... | collective-permute-start | bytes 1572872 | tf_op jit(solution)/shard_map/ppermute | solution.py:54
  151.1 0.8 copy-start.16
  172.7 14.0 %collective-permute-start.19 = (bf16[128,2048]{1,0:T(8,128)(2,1)}, bf16[128,2048]{1,0:T(8,128)(2,1)S(1)}, u32[]{:S(2)}, u32[]{:S(2)}) collective-permute-start(bf16[128,2048]{1,0:T(8,128)(2,1)} %get-tuple-element.33), channel_id=1, source_target_pairs={{0,1},{3,2},{4,5},{7,6},{8,9},{11,10},{12,13},{15,14},{16,17},{19,... | collective-permute-start | bytes 1572872 | tf_op jit(solution)/shard_map/ppermute | solution.py:54
  174.1 12.7 %copy-start.14 = (bf16[128,2048]{1,0:T(8,128)(2,1)S(1)}, bf16[128,2048]{1,0:T(8,128)(2,1)}, u32[]{:S(2)}) copy-start(bf16[128,2048]{1,0:T(8,128)(2,1)} %get-tuple-element.33) | copy-start | bytes 1572868
  174.1 23.9 %copy-start.8 = (bf16[128,2048]{1,0:T(8,128)(2,1)S(1)}, bf16[128,2048]{1,0:T(8,128)(2,1)}, u32[]{:S(2)}) copy-start(bf16[128,2048]{1,0:T(8,128)(2,1)} %get-tuple-element.34) | copy-start | bytes 1572868
  174.1 23.9 %collective-permute-start.21 = (bf16[128,2048]{1,0:T(8,128)(2,1)}, bf16[128,2048]{1,0:T(8,128)(2,1)S(1)}, u32[]{:S(2)}, u32[]{:S(2)}) collective-permute-start(bf16[128,2048]{1,0:T(8,128)(2,1)} %get-tuple-element.34), channel_id=1, source_target_pairs={{0,1},{3,2},{4,5},{7,6},{8,9},{11,10},{12,13},{15,14},{16,17},{19,... | collective-permute-start | bytes 1572872 | tf_op jit(solution)/shard_map/ppermute | solution.py:54
  175.6 0.8 copy-start.11
  185.6 21.8 %collective-permute-start.14 = (bf16[128,2048]{1,0:T(8,128)(2,1)}, bf16[128,2048]{1,0:T(8,128)(2,1)S(1)}, u32[]{:S(2)}, u32[]{:S(2)}) collective-permute-start(bf16[128,2048]{1,0:T(8,128)(2,1)} %get-tuple-element.32), channel_id=1, source_target_pairs={{0,1},{1,0},{2,3},{3,2},{4,5},{5,4},{6,7},{7,6},{8,9},{9,8},{10,11... | collective-permute-start | bytes 1572872 | tf_op jit(solution)/shard_map/ppermute | solution.py:54
  186.8 20.6 %collective-permute-start.20 = (bf16[128,2048]{1,0:T(8,128)(2,1)S(1)}, bf16[128,2048]{1,0:T(8,128)(2,1)S(1)}, u32[]{:S(2)}, u32[]{:S(2)}) collective-permute-start(bf16[128,2048]{1,0:T(8,128)(2,1)S(1)} %add_convert_fusion.1), channel_id=1, source_target_pairs={{1,2},{2,1},{5,6},{6,5},{9,10},{10,9},{13,14},{14,13},{17,18},{18,... | collective-permute-start | bytes 1572872 | tf_op jit(solution)/shard_map/ppermute | solution.py:54
  198.1 15.0 %collective-permute-start.22 = (bf16[128,2048]{1,0:T(8,128)(2,1)S(1)}, bf16[128,2048]{1,0:T(8,128)(2,1)S(1)}, u32[]{:S(2)}, u32[]{:S(2)}) collective-permute-start(bf16[128,2048]{1,0:T(8,128)(2,1)S(1)} %add_convert_fusion), channel_id=1, source_target_pairs={{2,0},{1,3},{6,4},{5,7},{10,8},{9,11},{14,12},{13,15},{18,16},{17,... | collective-permute-start | bytes 1572872 | tf_op jit(solution)/shard_map/ppermute | solution.py:54
  207.5 5.6 %copy-start.7 = (bf16[128,2048]{1,0:T(8,128)(2,1)}, bf16[128,2048]{1,0:T(8,128)(2,1)S(1)}, u32[]{:S(2)}) copy-start(bf16[128,2048]{1,0:T(8,128)(2,1)S(1)} %collective-permute-done.14.refs_1_) | copy-start | bytes 1572868
  207.5 5.6 %copy-start.12 = (bf16[128,2048]{1,0:T(8,128)(2,1)}, bf16[128,2048]{1,0:T(8,128)(2,1)S(1)}, u32[]{:S(2)}) copy-start(bf16[128,2048]{1,0:T(8,128)(2,1)S(1)} %collective-permute-done.20.refs_2_) | copy-start | bytes 1572868
  213.1 0.8 copy-start.17
Sparse Core Ops, SparseCore 0:
  60.2 96.5 all-gather.1

commit v4 on v3

--- a/solution.py
+++ b/solution.py
@@ -74,16 +74,28 @@
 
 
 def sum_line(parts, count):
+    done = ()
+
+    def part(k):
+        return parts[k](done) if callable(parts[k]) else parts[k]
+
     if count != 4:
-        return [parts[0]] + [shift(parts[k], "seq", count, count - k) for k in range(1, count)]
-    mine, near, middle, far = parts
-    far_in = along(far, count, [(0, 1), (3, 2)])
-    middle_in = along(middle, count, [(0, 1), (3, 2)])
-    near = along(near, count, [(0, 1), (1, 0), (2, 3), (3, 2)])
-    add = lambda u, v: (u.astype(F32) + v.astype(F32)).astype(BF16)
-    far = along(add(far, far_in), count, [(2, 0), (1, 3)])
-    middle = along(add(middle, middle_in), count, [(1, 2), (2, 1)])
-    return [mine, near, middle, far]
+        return [part(0)] + [shift(part(k), "seq", count, count - k) for k in range(1, count)]
+
+    def joined(k):
+        mine = part(k)
+        other = along(mine, count, [(0, 1), (3, 2)])
+        return (mine.astype(F32) + other.astype(F32)).astype(BF16), mine
+
+    far, done_far = joined(3)
+    far_back = along(far, count, [(2, 0), (1, 3)])
+    done = (done_far,)
+    middle, done_middle = joined(2)
+    done = (done_middle, far)
+    near, mine = part(1), part(0)
+    middle_back = along(after(middle, far_back, mine), count, [(1, 2), (2, 1)])
+    near_back = along(near, count, [(0, 1), (1, 0), (2, 3), (3, 2)])
+    return [mine, near_back, middle_back, far_back]
 
 
 def after(value, *earlier):
@@ -512,9 +524,19 @@
     ys = project(mixed, where, owners_of(count), out_parts)
     stream, normed = norm(sum_line(ys, count), residual[0], mlp_gain[None, :])
     blocks = gather_line(normed, count)
-    half = (count + 1) // 2
-    ys = forward(blocks[:half], weights, n_req) + forward(blocks[half:], weights, n_req)
-    hidden = finish(sum_line(ys, count), where, lengths, slot_request, stream)
+    first = min(2, count)
+    nearest = []
+
+    def near(k, done):
+        if not nearest:
+            nearest.extend(forward(after(blocks[:first], *done), weights, n_req))
+        return nearest[k]
+
+    def far(k, done):
+        return forward(after([blocks[k]], *done, *blocks[first - 1]), weights, n_req)[0]
+
+    parts = [functools.partial(near if k < first else far, k) for k in range(count)]
+    hidden = finish(sum_line(parts, count), where, lengths, slot_request, stream)
     return hidden[None], state[None], conv_edge[None]
 
 

time: 224 us -> 220 us (0.982)
  waiting for transfers between devices: 87.2 us -> 75.7 us
  Pallas kernels: 37.8 us -> 46.6 us
    ppermute x15, waiting for transfers between devices: 82.8 us -> 65.3 us  [along(): return lax.ppermute(value, 'seq', pairs)]
    pallas_call x2 -> x3, Pallas kernels: 18.9 us -> 27.9 us  [forward(): pl.pallas_call(functools.partial(forward_kernel, terms, strips), out_shap...]
    all_gather x1, waiting for transfers between devices: 0.01 us -> 5.99 us  [local(): lax.all_gather(after(weights, out_parts[0], *xs[1:]), 'req', axis=0, tile...]
    unnamed x42 -> x40, local copies, waits for them, and re-layouts: 5.53 us -> 4.29 us
  transfers between devices with their start and end apart: 24 -> 24, of which waited for: 12 -> 13; matrix products, arithmetic and copies ran while one was open for 3% -> 3% of each run, Pallas kernels for 16% -> 20%
where the time goes in v4:
time: 220 us
  waiting for transfers between devices  75.7 us (34%)
  starting transfers between devices  74.3 us (34%)
  Pallas kernels  46.6 us (21%)
  between operations  14.4 us (7%)
  other arithmetic  4.62 us (2%)
  local copies, waits for them, and re-layouts  4.3 us (2%)
    ppermute x15, waiting for transfers between devices, along(): return lax.ppermute(value, 'seq', pairs)  65.3 us
    ppermute x15, starting transfers between devices, along(): return lax.ppermute(value, 'seq', pairs)  33.7 us
    ppermute x4, starting transfers between devices, flip(): lax.ppermute(value, 'req', [(i, i ^ bits) for i in range(lax.axis_size('r...  30.4 us
    pallas_call x3, Pallas kernels, forward(): pl.pallas_call(functools.partial(forward_kernel, terms, strips), out_shap...  27.9 us
    ppermute x3, starting transfers between devices, shift(): lax.ppermute(value, axis, [(i, (i + steps) % count) for i in range(count)])  8.53 us
    pallas_call x1, Pallas kernels, delta(): pl.pallas_call(functools.partial(delta_kernel, count, heads, piece), out_...  6.59 us
    all_gather x1, waiting for transfers between devices, local(): lax.all_gather(after(weights, out_parts[0], *xs[1:]), 'req', axis=0, tile...  5.99 us
  transfers between devices with their start and end apart: 24, of which 13 were waited for; matrix products, arithmetic and copies ran while one was open for 3% of the time, Pallas kernels for 20%

profile of v4, /device:TPU:0, one launch (start us, length us, event | category | flops | bytes accessed | tf_op | source)
XLA Modules:
  0.0 219.8 jit_solution(5488418517024693441)
XLA Ops:
  7.2 0.0 all-gather.2.cloned.1.call-start
  7.2 1.6 collective-permute-start.3
  8.8 0.6 pad_add_fusion.refs_0_.refs_4_
  9.4 2.9 %pack.1 = (bf16[144,1536]{1,0:T(8,128)(2,1)}, bf16[144,1536]{1,0:T(8,128)(2,1)}, bf16[144,1536]{1,0:T(8,128)(2,1)}, bf16[144,1536]{1,0:T(8,128)(2,1)}) custom-call(s32[2]{0:T(128)} %pad_add_fusion.refs_0_.refs_4_, s32[8]{0:T(128)} %refs_5_.3, s32[8]{0:T(128)} %refs_6_.3, bf16[128,4096]{1,0:T(8,128)(2,1)} %bitcast.23, bf16[128,2048]{1,0:T(8,128)(2,1)} %bitcast.26, ...), custom_call_target="tpu_custom_call" | custom-call | tf_op jit(solution)/shard_map/pack/pallas_call | solution.py:157
  12.3 3.3 %collective-permute-start = (bf16[144,1536]{1,0:T(8,128)(2,1)}, bf16[144,1536]{1,0:T(8,128)(2,1)S(1)}, u32[]{:S(2)}, u32[]{:S(2)}) collective-permute-start(bf16[144,1536]{1,0:T(8,128)(2,1)} %get-tuple-element.27), channel_id=1, source_target_pairs={{0,1},{1,2},{2,3},{3,0},{4,5},{5,6},{6,7},{7,4},{8,9},{9,10},{10,1... | collective-permute-start | bytes 1327112 | tf_op jit(solution)/shard_map/ppermute | solution.py:42
  15.7 3.2 %collective-permute-start.1 = (bf16[144,1536]{1,0:T(8,128)(2,1)}, bf16[144,1536]{1,0:T(8,128)(2,1)S(1)}, u32[]{:S(2)}, u32[]{:S(2)}) collective-permute-start(bf16[144,1536]{1,0:T(8,128)(2,1)} %get-tuple-element.28), channel_id=1, source_target_pairs={{0,2},{1,3},{2,0},{3,1},{4,6},{5,7},{6,4},{7,5},{8,10},{9,11},{10,... | collective-permute-start | bytes 1327112 | tf_op jit(solution)/shard_map/ppermute | solution.py:42
  18.8 2.0 collective-permute-start.2
  20.9 1.4 copy.17
  22.3 0.0 copy-start.2
  22.3 0.0 copy-start.4
  22.4 0.0 copy-start.6
  22.4 25.4 %collective-permute-start.4 = (bf16[64,2048]{1,0:T(8,128)(2,1)S(1)}, bf16[64,2048]{1,0:T(8,128)(2,1)S(1)}, u32[]{:S(2)}, u32[]{:S(2)}) collective-permute-start(bf16[64,2048]{1,0:T(8,128)(2,1)S(1)} %collective-permute-done.3), channel_id=1, source_target_pairs={{0,8},{4,12},{8,0},{12,4},{16,24},{20,28},{24,16},{28,20},{1,9},{5... | collective-permute-start | bytes 786440 | tf_op jit(solution)/shard_map/ppermute | solution.py:46
  47.8 2.8 %pad_maximum_fusion = bf16[768,1408]{1,0:T(8,128)(2,1)} fusion(bf16[256,1408]{1,0:T(8,128)(2,1)S(1)} %bitcast.22, bf16[256,1408]{1,0:T(8,128)(2,1)} %param.26, bf16[256,1408]{1,0:T(8,128)(2,1)} %param.25), kind=kLoop, calls=%fused_computation | loop fusion | flops 6488064 | bytes 4325376 | tf_op jit(solution)/shard_map/concatenate | solution.py:521
  50.6 2.0 collective-permute-start.5
  52.7 2.9 %collective-permute-start.6 = (bf16[64,2048]{1,0:T(8,128)(2,1)S(1)}, bf16[64,2048]{1,0:T(8,128)(2,1)S(1)}, u32[]{:S(2)}, u32[]{:S(2)}) collective-permute-start(bf16[64,2048]{1,0:T(8,128)(2,1)S(1)} %collective-permute-done.3), channel_id=1, source_target_pairs={{0,24},{4,28},{8,16},{12,20},{16,8},{20,12},{24,0},{28,4},{1,25},{... | collective-permute-start | bytes 786440 | tf_op jit(solution)/shard_map/ppermute | solution.py:46
  55.6 3.7 %collective-permute-done.5 = bf16[64,2048]{1,0:T(8,128)(2,1)S(1)} collective-permute-done((bf16[64,2048]{1,0:T(8,128)(2,1)S(1)}, bf16[64,2048]{1,0:T(8,128)(2,1)S(1)}, u32[]{:S(2)}, u32[]{:S(2)}) %collective-permute-start.5) | collective-permute-done | bytes 262176 | tf_op jit(solution)/shard_map/ppermute | solution.py:46
  59.4 0.6 collective-permute-done.6
  60.0 0.0 all-gather.2.cloned.1.call-update
  60.1 0.1 collective-permute-start.7
  60.2 0.1 pad_add_fusion.1.refs_1_
  60.3 6.6 %delta_rule.1 = (bf16[4,128,512]{2,1,0:T(8,128)(2,1)S(1)}, f32[2,128,256]{2,1,0:T(8,128)}) custom-call(bf16[144,1536]{1,0:T(8,128)(2,1)S(1)} %copy-done.4, bf16[144,1536]{1,0:T(8,128)(2,1)S(1)} %collective-permute-done.refs_1_, bf16[144,1536]{1,0:T(8,128)(2,1)S(1)} %collective-permute-done.1.refs_2_, bf16[144,1536]{1,0:T(8,128)(2,1)S(1)} %collective-permute-done.2.refs_3_, ...), custom_call_target="tpu_custom_call" | custom-call | flops 4000000000 | bytes 4194304 | tf_op jit(solution)/shard_map/delta_rule/pallas_call | solution.py:285
  66.9 3.3 %output_projection.1 = (bf16[128,2048]{1,0:T(8,128)(2,1)S(1)}, bf16[128,2048]{1,0:T(8,128)(2,1)S(1)}, bf16[128,2048]{1,0:T(8,128)(2,1)S(1)}, bf16[128,2048]{1,0:T(8,128)(2,1)S(1)}) custom-call(s32[2]{0:T(128)S(1)} %copy-done.3, s32[4]{0:T(128)S(1)} %pad_add_fusion.1.refs_1_, bf16[4,128,512]{2,1,0:T(8,128)(2,1)S(1)} %get-tuple-element.30.refs_2_, ...), custom_call_target="tpu_custom_call" | custom-call | flops 1073741824 | bytes 4194304 | tf_op jit(solution)/shard_map/output_projection/pallas_call | solution.py:331
  70.2 0.0 copy-start
  70.2 0.8 copy-done
  71.0 7.9 %collective-permute-start.10 = (bf16[128,2048]{1,0:T(8,128)(2,1)S(1)}, bf16[128,2048]{1,0:T(8,128)(2,1)S(1)}, u32[]{:S(2)}, u32[]{:S(2)}) collective-permute-start(bf16[128,2048]{1,0:T(8,128)(2,1)S(1)} %get-tuple-element.34), channel_id=1, source_target_pairs={{0,1},{3,2},{4,5},{7,6},{8,9},{11,10},{12,13},{15,14},{16,17},{19,... | collective-permute-start | bytes 1572872 | tf_op jit(solution)/shard_map/ppermute | solution.py:54
  78.9 1.3 collective-permute-start.9
  80.2 10.9 %collective-permute-done.10 = bf16[128,2048]{1,0:T(8,128)(2,1)S(1)} collective-permute-done((bf16[128,2048]{1,0:T(8,128)(2,1)S(1)}, bf16[128,2048]{1,0:T(8,128)(2,1)S(1)}, u32[]{:S(2)}, u32[]{:S(2)}) %collective-permute-start.10) | collective-permute-done | bytes 524320 | tf_op jit(solution)/shard_map/ppermute | solution.py:54
  91.1 0.1 add_convert_fusion.2
  91.2 1.3 collective-permute-start.11
  92.5 2.6 %collective-permute-start.8 = (bf16[128,2048]{1,0:T(8,128)(2,1)S(1)}, bf16[128,2048]{1,0:T(8,128)(2,1)S(1)}, u32[]{:S(2)}, u32[]{:S(2)}) collective-permute-start(bf16[128,2048]{1,0:T(8,128)(2,1)S(1)} %get-tuple-element.32), channel_id=1, source_target_pairs={{0,1},{1,0},{2,3},{3,2},{4,5},{5,4},{6,7},{7,6},{8,9},{9,8},{10,11... | collective-permute-start | bytes 1572872 | tf_op jit(solution)/shard_map/ppermute | solution.py:54
  95.1 7.2 %collective-permute-done.9 = bf16[128,2048]{1,0:T(8,128)(2,1)S(1)} collective-permute-done((bf16[128,2048]{1,0:T(8,128)(2,1)S(1)}, bf16[128,2048]{1,0:T(8,128)(2,1)S(1)}, u32[]{:S(2)}, u32[]{:S(2)}) %collective-permute-start.9) | collective-permute-done | bytes 524320 | tf_op jit(solution)/shard_map/ppermute | solution.py:54
  102.3 0.1 add_convert_fusion.3
  102.4 4.7 %collective-permute-done.11.refs_3_ = bf16[128,2048]{1,0:T(8,128)(2,1)S(1)} collective-permute-done((bf16[128,2048]{1,0:T(8,128)(2,1)S(1)}, bf16[128,2048]{1,0:T(8,128)(2,1)S(1)}, u32[]{:S(2)}, u32[]{:S(2)}) %collective-permute-start.11) | collective-permute-done | bytes 524320 | tf_op jit(solution)/shard_map/ppermute | solution.py:54
  107.1 0.7 collective-permute-start.12
  107.8 9.9 %collective-permute-done.8.refs_1_ = bf16[128,2048]{1,0:T(8,128)(2,1)S(1)} collective-permute-done((bf16[128,2048]{1,0:T(8,128)(2,1)S(1)}, bf16[128,2048]{1,0:T(8,128)(2,1)S(1)}, u32[]{:S(2)}, u32[]{:S(2)}) %collective-permute-start.8) | collective-permute-done | bytes 524320 | tf_op jit(solution)/shard_map/ppermute | solution.py:54
  117.7 0.8 copy-done.15
  118.5 0.2 copy-done.17
  118.6 3.0 %stream_norm.1 = (bf16[128,2048]{1,0:T(8,128)(2,1)}, bf16[128,2048]{1,0:T(8,128)(2,1)}) custom-call(bf16[128,2048]{1,0:T(8,128)(2,1)} %copy-done, bf16[128,2048]{1,0:T(8,128)(2,1)} %copy-done.15, bf16[128,2048]{1,0:T(8,128)(2,1)} %copy-done.17, bf16[128,2048]{1,0:T(8,128)(2,1)} %copy-done.14, bf16[128,2048]{1,0:T(8,128)(2,1)} %bitcast.24, f32[1,2048]{1,0:T(1,128)} %bitcast.27), custom_call_target="tpu_custom_call" | custom-call | tf_op jit(solution)/shard_map/stream_norm/pallas_call | solution.py:359
  121.7 4.6 %collective-permute-start.16 = (bf16[128,2048]{1,0:T(8,128)(2,1)}, bf16[128,2048]{1,0:T(8,128)(2,1)S(1)}, u32[]{:S(2)}, u32[]{:S(2)}) collective-permute-start(bf16[128,2048]{1,0:T(8,128)(2,1)} %get-tuple-element.42.refs_0_), channel_id=1, source_target_pairs={{0,2},{3,1},{4,6},{7,5},{8,10},{11,9},{12,14},{15,13},{16,18},{19,... | collective-permute-start | bytes 1572872 | tf_op jit(solution)/shard_map/ppermute | solution.py:54
  126.3 0.7 collective-permute-start.14
  127.0 1.2 collective-permute-start.13
  128.2 10.7 %collective-permute-done.16.refs_0_ = bf16[128,2048]{1,0:T(8,128)(2,1)S(1)} collective-permute-done((bf16[128,2048]{1,0:T(8,128)(2,1)}, bf16[128,2048]{1,0:T(8,128)(2,1)S(1)}, u32[]{:S(2)}, u32[]{:S(2)}) %collective-permute-start.16) | collective-permute-done | bytes 524320 | tf_op jit(solution)/shard_map/ppermute | solution.py:54
  139.0 1.3 collective-permute-start.17
  140.3 1.5 collective-permute-start.15
  141.8 4.9 %collective-permute-done.13.refs_1_ = bf16[128,2048]{1,0:T(8,128)(2,1)S(1)} collective-permute-done((bf16[128,2048]{1,0:T(8,128)(2,1)}, bf16[128,2048]{1,0:T(8,128)(2,1)S(1)}, u32[]{:S(2)}, u32[]{:S(2)}) %collective-permute-start.13) | collective-permute-done | bytes 524320 | tf_op jit(solution)/shard_map/ppermute | solution.py:54
  146.7 4.1 %collective-permute-done.17.refs_1_ = bf16[128,2048]{1,0:T(8,128)(2,1)} collective-permute-done((bf16[128,2048]{1,0:T(8,128)(2,1)S(1)}, bf16[128,2048]{1,0:T(8,128)(2,1)}, u32[]{:S(2)}, u32[]{:S(2)}) %collective-permute-start.17) | collective-permute-done | bytes 524320 | tf_op jit(solution)/shard_map/ppermute | solution.py:54
  150.8 6.0 %all-gather.2.cloned.1.call-done.refs_2_ = bf16[6144,1408]{1,0:T(8,128)(2,1)} async-done(((bf16[768,1408]{1,0:T(8,128)(2,1)}), bf16[6144,1408]{1,0:T(8,128)(2,1)}) %all-gather.2.cloned.1.call-update) | async-done | bytes 17301520 | tf_op jit(solution)/shard_map/all_gather | solution.py:522
  156.8 9.3 %feed_forward.3 = bf16[128,2048]{1,0:T(8,128)(2,1)} custom-call(bf16[128,2048]{1,0:T(8,128)(2,1)} %copy-done.13, bf16[128,2048]{1,0:T(8,128)(2,1)} %collective-permute-done.17.refs_1_, bf16[6144,1408]{1,0:T(8,128)(2,1)} %all-gather.2.cloned.1.call-done.refs_2_), custom_call_target="tpu_custom_call" | custom-call | flops 2214592512 | bytes 20971520 | tf_op jit(solution)/shard_map/feed_forward/pallas_call | solution.py:437
  166.1 3.6 %collective-permute-start.18 = (bf16[128,2048]{1,0:T(8,128)(2,1)}, bf16[128,2048]{1,0:T(8,128)(2,1)S(1)}, u32[]{:S(2)}, u32[]{:S(2)}) collective-permute-start(bf16[128,2048]{1,0:T(8,128)(2,1)} %feed_forward.3), channel_id=1, source_target_pairs={{0,1},{3,2},{4,5},{7,6},{8,9},{11,10},{12,13},{15,14},{16,17},{19,... | collective-permute-start | bytes 1572872 | tf_op jit(solution)/shard_map/ppermute | solution.py:54
  169.7 9.3 %feed_forward.4 = bf16[128,2048]{1,0:T(8,128)(2,1)} custom-call(bf16[128,2048]{1,0:T(8,128)(2,1)} %copy-done.11, bf16[128,2048]{1,0:T(8,128)(2,1)} %collective-permute-done.15.refs_1_, bf16[6144,1408]{1,0:T(8,128)(2,1)} %all-gather.2.cloned.1.call-done.refs_2_), custom_call_target="tpu_custom_call" | custom-call | flops 2214592512 | bytes 20971520 | tf_op jit(solution)/shard_map/feed_forward/pallas_call | solution.py:437
  179.0 1.3 collective-permute-start.20
  180.3 1.8 collective-permute-done.18
  182.1 0.1 add_convert_fusion.1
  182.2 1.4 collective-permute-start.21
  183.7 9.3 %feed_forward.5 = (bf16[128,2048]{1,0:T(8,128)(2,1)}, bf16[128,2048]{1,0:T(8,128)(2,1)}) custom-call(bf16[128,2048]{1,0:T(8,128)(2,1)} %get-tuple-element.42.refs_0_, bf16[128,2048]{1,0:T(8,128)(2,1)} %copy-done.9, bf16[6144,1408]{1,0:T(8,128)(2,1)} %all-gather.2.cloned.1.call-done.refs_2_), custom_call_target="tpu_custom_call" | custom-call | flops 4429185024 | bytes 20971520 | tf_op jit(solution)/shard_map/feed_forward/pallas_call | solution.py:437
  193.0 3.7 %collective-permute-start.19 = (bf16[128,2048]{1,0:T(8,128)(2,1)}, bf16[128,2048]{1,0:T(8,128)(2,1)S(1)}, u32[]{:S(2)}, u32[]{:S(2)}) collective-permute-start(bf16[128,2048]{1,0:T(8,128)(2,1)} %get-tuple-element.45), channel_id=1, source_target_pairs={{0,1},{1,0},{2,3},{3,2},{4,5},{5,4},{6,7},{7,6},{8,9},{9,8},{10,11... | collective-permute-start | bytes 1572872 | tf_op jit(solution)/shard_map/ppermute | solution.py:54
  196.6 0.1 add_convert_fusion
  196.8 1.3 collective-permute-done.21.refs_3_
  198.0 0.7 collective-permute-start.22
  198.7 0.6 fusion
  199.3 9.8 %collective-permute-done.19.refs_1_ = bf16[128,2048]{1,0:T(8,128)(2,1)S(1)} collective-permute-done((bf16[128,2048]{1,0:T(8,128)(2,1)}, bf16[128,2048]{1,0:T(8,128)(2,1)S(1)}, u32[]{:S(2)}, u32[]{:S(2)}) %collective-permute-start.19) | collective-permute-done | bytes 524320 | tf_op jit(solution)/shard_map/ppermute | solution.py:54
  209.2 0.8 copy-done.12
  210.0 0.2 copy-done.16
  210.1 2.8 %last_sum.1 = bf16[128,2048]{1,0:T(8,128)(2,1)} custom-call(bf16[128,2048]{1,0:T(8,128)(2,1)} %get-tuple-element.44.refs_0_, bf16[128,2048]{1,0:T(8,128)(2,1)} %copy-done.12, bf16[128,2048]{1,0:T(8,128)(2,1)} %copy-done.16, bf16[128,2048]{1,0:T(8,128)(2,1)} %copy-done.10, s32[2]{0:T(128)} %pad_add_fusion.refs_0_.refs_4_, s32[8]{0:T(128)} %refs_5_.3, ...), custom_call_target="tpu_custom_call" | custom-call | tf_op jit(solution)/shard_map/last_sum/pallas_call | solution.py:472
  (42 shorter events, 0.2 us)
Async XLA Ops:
  7.2 149.6 %all-gather.2.cloned.1.call-start = ((), (), s32[]{:S(2)}) async-start(), calls=%async_computation | async-start | bytes 19464192 | tf_op jit(solution)/shard_map/all_gather | solution.py:522
  7.2 15.2 %collective-permute-start.3 = (bf16[64,2048]{1,0:T(8,128)(2,1)}, bf16[64,2048]{1,0:T(8,128)(2,1)S(1)}, u32[]{:S(2)}, u32[]{:S(2)}) collective-permute-start(bf16[64,2048]{1,0:T(8,128)(2,1)} %param.23), channel_id=1, source_target_pairs={{0,0},{1,4},{2,8},{3,12},{4,16},{5,20},{6,24},{7,28},{8,1},{9,5},{... | collective-permute-start | bytes 786440 | tf_op jit(solution)/shard_map/ppermute | solution.py:512
  12.3 47.7 %collective-permute-start = (bf16[144,1536]{1,0:T(8,128)(2,1)}, bf16[144,1536]{1,0:T(8,128)(2,1)S(1)}, u32[]{:S(2)}, u32[]{:S(2)}) collective-permute-start(bf16[144,1536]{1,0:T(8,128)(2,1)} %get-tuple-element.27), channel_id=1, source_target_pairs={{0,1},{1,2},{2,3},{3,0},{4,5},{5,6},{6,7},{7,4},{8,9},{9,10},{10,1... | collective-permute-start | bytes 1327112 | tf_op jit(solution)/shard_map/ppermute | solution.py:42
  15.7 44.4 %collective-permute-start.1 = (bf16[144,1536]{1,0:T(8,128)(2,1)}, bf16[144,1536]{1,0:T(8,128)(2,1)S(1)}, u32[]{:S(2)}, u32[]{:S(2)}) collective-permute-start(bf16[144,1536]{1,0:T(8,128)(2,1)} %get-tuple-element.28), channel_id=1, source_target_pairs={{0,2},{1,3},{2,0},{3,1},{4,6},{5,7},{6,4},{7,5},{8,10},{9,11},{10,... | collective-permute-start | bytes 1327112 | tf_op jit(solution)/shard_map/ppermute | solution.py:42
  18.8 41.2 %collective-permute-start.2 = (bf16[144,1536]{1,0:T(8,128)(2,1)}, bf16[144,1536]{1,0:T(8,128)(2,1)S(1)}, u32[]{:S(2)}, u32[]{:S(2)}) collective-permute-start(bf16[144,1536]{1,0:T(8,128)(2,1)} %get-tuple-element.29), channel_id=1, source_target_pairs={{0,3},{1,0},{2,1},{3,2},{4,7},{5,4},{6,5},{7,6},{8,11},{9,8},{10,9... | collective-permute-start | bytes 1327112 | tf_op jit(solution)/shard_map/ppermute | solution.py:42
  22.3 37.9 %copy-start.1 = (s32[8]{0:T(128)S(1)}, s32[8]{0:T(128)}, u32[]{:S(2)}) copy-start(s32[8]{0:T(128)} %refs_5_.3) | copy-start | bytes 100
  22.3 37.9 %copy-start.2 = (s32[8]{0:T(128)S(1)}, s32[8]{0:T(128)}, u32[]{:S(2)}) copy-start(s32[8]{0:T(128)} %refs_6_.3) | copy-start | bytes 100
  22.3 37.9 %copy-start.3 = (s32[2]{0:T(128)S(1)}, s32[2]{0:T(128)}, u32[]{:S(2)}) copy-start(s32[2]{0:T(128)} %pad_add_fusion.refs_0_.refs_4_) | copy-start | bytes 28
  22.3 37.9 %copy-start.4 = (bf16[144,1536]{1,0:T(8,128)(2,1)S(1)}, bf16[144,1536]{1,0:T(8,128)(2,1)}, u32[]{:S(2)}) copy-start(bf16[144,1536]{1,0:T(8,128)(2,1)} %get-tuple-element.26.refs_0_) | copy-start | bytes 1327108
  22.4 37.9 %copy-start.5 = (f32[4,4096]{1,0:T(4,128)S(1)}, f32[4,4096]{1,0:T(4,128)}, u32[]{:S(2)}) copy-start(f32[4,4096]{1,0:T(4,128)} %refs_7_.1) | copy-start | bytes 196612
  22.4 37.9 %copy-start.6 = (f32[256]{0:T(256)S(1)}, f32[256]{0:T(256)}, u32[]{:S(2)}) copy-start(f32[256]{0:T(256)} %param.22) | copy-start | bytes 3076
  22.4 30.3 %collective-permute-start.4 = (bf16[64,2048]{1,0:T(8,128)(2,1)S(1)}, bf16[64,2048]{1,0:T(8,128)(2,1)S(1)}, u32[]{:S(2)}, u32[]{:S(2)}) collective-permute-start(bf16[64,2048]{1,0:T(8,128)(2,1)S(1)} %collective-permute-done.3), channel_id=1, source_target_pairs={{0,8},{4,12},{8,0},{12,4},{16,24},{20,28},{24,16},{28,20},{1,9},{5... | collective-permute-start | bytes 786440 | tf_op jit(solution)/shard_map/ppermute | solution.py:46
  50.6 8.8 %collective-permute-start.5 = (bf16[64,2048]{1,0:T(8,128)(2,1)S(1)}, bf16[64,2048]{1,0:T(8,128)(2,1)S(1)}, u32[]{:S(2)}, u32[]{:S(2)}) collective-permute-start(bf16[64,2048]{1,0:T(8,128)(2,1)S(1)} %collective-permute-done.3), channel_id=1, source_target_pairs={{0,16},{4,20},{8,24},{12,28},{16,0},{20,4},{24,8},{28,12},{1,17},{... | collective-permute-start | bytes 786440 | tf_op jit(solution)/shard_map/ppermute | solution.py:46
  52.7 7.3 %collective-permute-start.6 = (bf16[64,2048]{1,0:T(8,128)(2,1)S(1)}, bf16[64,2048]{1,0:T(8,128)(2,1)S(1)}, u32[]{:S(2)}, u32[]{:S(2)}) collective-permute-start(bf16[64,2048]{1,0:T(8,128)(2,1)S(1)} %collective-permute-done.3), channel_id=1, source_target_pairs={{0,24},{4,28},{8,16},{12,20},{16,8},{20,12},{24,0},{28,4},{1,25},{... | collective-permute-start | bytes 786440 | tf_op jit(solution)/shard_map/ppermute | solution.py:46
  60.1 6.8 %collective-permute-start.7 = (bf16[256,2048]{1,0:T(8,128)(2,1)S(1)}, bf16[256,2048]{1,0:T(8,128)(2,1)}, u32[]{:S(2)}, u32[]{:S(2)}) collective-permute-start(bf16[256,2048]{1,0:T(8,128)(2,1)S(1)} %constant_dynamic-update-slice_fusion.refs_3_), channel_id=1, source_target_pairs={{0,4},{4,0},{8,12},{12,8},{16,20},{20,16},{24,28},{28,24},{1,5},{5... | collective-permute-start | bytes 3145736 | tf_op jit(solution)/shard_map/ppermute | solution.py:46
  70.2 0.8 copy-start
  71.0 20.1 %collective-permute-start.10 = (bf16[128,2048]{1,0:T(8,128)(2,1)S(1)}, bf16[128,2048]{1,0:T(8,128)(2,1)S(1)}, u32[]{:S(2)}, u32[]{:S(2)}) collective-permute-start(bf16[128,2048]{1,0:T(8,128)(2,1)S(1)} %get-tuple-element.34), channel_id=1, source_target_pairs={{0,1},{3,2},{4,5},{7,6},{8,9},{11,10},{12,13},{15,14},{16,17},{19,... | collective-permute-start | bytes 1572872 | tf_op jit(solution)/shard_map/ppermute | solution.py:54
  78.9 23.4 %collective-permute-start.9 = (bf16[128,2048]{1,0:T(8,128)(2,1)S(1)}, bf16[128,2048]{1,0:T(8,128)(2,1)S(1)}, u32[]{:S(2)}, u32[]{:S(2)}) collective-permute-start(bf16[128,2048]{1,0:T(8,128)(2,1)S(1)} %get-tuple-element.33), channel_id=1, source_target_pairs={{0,1},{3,2},{4,5},{7,6},{8,9},{11,10},{12,13},{15,14},{16,17},{19,... | collective-permute-start | bytes 1572872 | tf_op jit(solution)/shard_map/ppermute | solution.py:54
  91.2 15.9 %collective-permute-start.11 = (bf16[128,2048]{1,0:T(8,128)(2,1)S(1)}, bf16[128,2048]{1,0:T(8,128)(2,1)S(1)}, u32[]{:S(2)}, u32[]{:S(2)}) collective-permute-start(bf16[128,2048]{1,0:T(8,128)(2,1)S(1)} %add_convert_fusion.2), channel_id=1, source_target_pairs={{2,0},{1,3},{6,4},{5,7},{10,8},{9,11},{14,12},{13,15},{18,16},{17,... | collective-permute-start | bytes 1572872 | tf_op jit(solution)/shard_map/ppermute | solution.py:54
  92.5 25.2 %collective-permute-start.8 = (bf16[128,2048]{1,0:T(8,128)(2,1)S(1)}, bf16[128,2048]{1,0:T(8,128)(2,1)S(1)}, u32[]{:S(2)}, u32[]{:S(2)}) collective-permute-start(bf16[128,2048]{1,0:T(8,128)(2,1)S(1)} %get-tuple-element.32), channel_id=1, source_target_pairs={{0,1},{1,0},{2,3},{3,2},{4,5},{5,4},{6,7},{7,6},{8,9},{9,8},{10,11... | collective-permute-start | bytes 1572872 | tf_op jit(solution)/shard_map/ppermute | solution.py:54
  107.1 10.6 %copy-start.14 = (bf16[128,2048]{1,0:T(8,128)(2,1)}, bf16[128,2048]{1,0:T(8,128)(2,1)S(1)}, u32[]{:S(2)}) copy-start(bf16[128,2048]{1,0:T(8,128)(2,1)S(1)} %collective-permute-done.11.refs_3_) | copy-start | bytes 1572868
  107.1 10.6 %collective-permute-start.12 = (bf16[128,2048]{1,0:T(8,128)(2,1)S(1)}, bf16[128,2048]{1,0:T(8,128)(2,1)S(1)}, u32[]{:S(2)}, u32[]{:S(2)}) collective-permute-start(bf16[128,2048]{1,0:T(8,128)(2,1)S(1)} %add_convert_fusion.3), channel_id=1, source_target_pairs={{1,2},{2,1},{5,6},{6,5},{9,10},{10,9},{13,14},{14,13},{17,18},{18,... | collective-permute-start | bytes 1572872 | tf_op jit(solution)/shard_map/ppermute | solution.py:54
  117.7 0.8 copy-start.15
  117.7 1.0 copy-start.17
  121.7 17.3 %collective-permute-start.16 = (bf16[128,2048]{1,0:T(8,128)(2,1)}, bf16[128,2048]{1,0:T(8,128)(2,1)S(1)}, u32[]{:S(2)}, u32[]{:S(2)}) collective-permute-start(bf16[128,2048]{1,0:T(8,128)(2,1)} %get-tuple-element.42.refs_0_), channel_id=1, source_target_pairs={{0,2},{3,1},{4,6},{7,5},{8,10},{11,9},{12,14},{15,13},{16,18},{19,... | collective-permute-start | bytes 1572872 | tf_op jit(solution)/shard_map/ppermute | solution.py:54
  126.3 13.9 %collective-permute-start.14 = (bf16[128,2048]{1,0:T(8,128)(2,1)}, bf16[128,2048]{1,0:T(8,128)(2,1)S(1)}, u32[]{:S(2)}, u32[]{:S(2)}) collective-permute-start(bf16[128,2048]{1,0:T(8,128)(2,1)} %get-tuple-element.42.refs_0_), channel_id=1, source_target_pairs={{1,2},{2,1},{5,6},{6,5},{9,10},{10,9},{13,14},{14,13},{17,18},{18,... | collective-permute-start | bytes 1572872 | tf_op jit(solution)/shard_map/ppermute | solution.py:54
  127.0 19.7 %collective-permute-start.13 = (bf16[128,2048]{1,0:T(8,128)(2,1)}, bf16[128,2048]{1,0:T(8,128)(2,1)S(1)}, u32[]{:S(2)}, u32[]{:S(2)}) collective-permute-start(bf16[128,2048]{1,0:T(8,128)(2,1)} %get-tuple-element.42.refs_0_), channel_id=1, source_target_pairs={{0,1},{1,0},{2,3},{3,2},{4,5},{5,4},{6,7},{7,6},{8,9},{9,8},{10,11... | collective-permute-start | bytes 1572872 | tf_op jit(solution)/shard_map/ppermute | solution.py:54
  139.0 17.8 %copy-start.13 = (bf16[128,2048]{1,0:T(8,128)(2,1)}, bf16[128,2048]{1,0:T(8,128)(2,1)S(1)}, u32[]{:S(2)}) copy-start(bf16[128,2048]{1,0:T(8,128)(2,1)S(1)} %collective-permute-done.16.refs_0_) | copy-start | bytes 1572868
  139.0 11.8 %collective-permute-start.17 = (bf16[128,2048]{1,0:T(8,128)(2,1)S(1)}, bf16[128,2048]{1,0:T(8,128)(2,1)}, u32[]{:S(2)}, u32[]{:S(2)}) collective-permute-start(bf16[128,2048]{1,0:T(8,128)(2,1)S(1)} %collective-permute-done.16.refs_0_), channel_id=1, source_target_pairs={{1,0},{2,3},{5,4},{6,7},{9,8},{10,11},{13,12},{14,15},{17,16},{18,... | collective-permute-start | bytes 1572872 | tf_op jit(solution)/shard_map/ppermute | solution.py:54
  140.3 25.8 %copy-start.11 = (bf16[128,2048]{1,0:T(8,128)(2,1)}, bf16[128,2048]{1,0:T(8,128)(2,1)S(1)}, u32[]{:S(2)}) copy-start(bf16[128,2048]{1,0:T(8,128)(2,1)S(1)} %collective-permute-done.14.refs_0_) | copy-start | bytes 1572868
  140.3 29.4 %collective-permute-start.15 = (bf16[128,2048]{1,0:T(8,128)(2,1)S(1)}, bf16[128,2048]{1,0:T(8,128)(2,1)}, u32[]{:S(2)}, u32[]{:S(2)}) collective-permute-start(bf16[128,2048]{1,0:T(8,128)(2,1)S(1)} %collective-permute-done.14.refs_0_), channel_id=1, source_target_pairs={{1,0},{2,3},{5,4},{6,7},{9,8},{10,11},{13,12},{14,15},{17,16},{18,... | collective-permute-start | bytes 1572872 | tf_op jit(solution)/shard_map/ppermute | solution.py:54
  146.7 19.4 %copy-start.9 = (bf16[128,2048]{1,0:T(8,128)(2,1)}, bf16[128,2048]{1,0:T(8,128)(2,1)S(1)}, u32[]{:S(2)}) copy-start(bf16[128,2048]{1,0:T(8,128)(2,1)S(1)} %collective-permute-done.13.refs_1_) | copy-start | bytes 1572868
  166.1 16.0 %copy-start.8 = (bf16[128,2048]{1,0:T(8,128)(2,1)S(1)}, bf16[128,2048]{1,0:T(8,128)(2,1)}, u32[]{:S(2)}) copy-start(bf16[128,2048]{1,0:T(8,128)(2,1)} %feed_forward.3) | copy-start | bytes 1572868
  166.1 16.0 %collective-permute-start.18 = (bf16[128,2048]{1,0:T(8,128)(2,1)}, bf16[128,2048]{1,0:T(8,128)(2,1)S(1)}, u32[]{:S(2)}, u32[]{:S(2)}) collective-permute-start(bf16[128,2048]{1,0:T(8,128)(2,1)} %feed_forward.3), channel_id=1, source_target_pairs={{0,1},{3,2},{4,5},{7,6},{8,9},{11,10},{12,13},{15,14},{16,17},{19,... | collective-permute-start | bytes 1572872 | tf_op jit(solution)/shard_map/ppermute | solution.py:54
  179.0 17.7 %collective-permute-start.20 = (bf16[128,2048]{1,0:T(8,128)(2,1)}, bf16[128,2048]{1,0:T(8,128)(2,1)S(1)}, u32[]{:S(2)}, u32[]{:S(2)}) collective-permute-start(bf16[128,2048]{1,0:T(8,128)(2,1)} %feed_forward.4), channel_id=1, source_target_pairs={{0,1},{3,2},{4,5},{7,6},{8,9},{11,10},{12,13},{15,14},{16,17},{19,... | collective-permute-start | bytes 1572872 | tf_op jit(solution)/shard_map/ppermute | solution.py:54
  182.2 14.4 %copy-start.7 = (bf16[128,2048]{1,0:T(8,128)(2,1)S(1)}, bf16[128,2048]{1,0:T(8,128)(2,1)}, u32[]{:S(2)}) copy-start(bf16[128,2048]{1,0:T(8,128)(2,1)} %feed_forward.4) | copy-start | bytes 1572868
  182.2 15.8 %collective-permute-start.21 = (bf16[128,2048]{1,0:T(8,128)(2,1)S(1)}, bf16[128,2048]{1,0:T(8,128)(2,1)S(1)}, u32[]{:S(2)}, u32[]{:S(2)}) collective-permute-start(bf16[128,2048]{1,0:T(8,128)(2,1)S(1)} %add_convert_fusion.1), channel_id=1, source_target_pairs={{2,0},{1,3},{6,4},{5,7},{10,8},{9,11},{14,12},{13,15},{18,16},{17,... | collective-permute-start | bytes 1572872 | tf_op jit(solution)/shard_map/ppermute | solution.py:54
  193.0 16.2 %collective-permute-start.19 = (bf16[128,2048]{1,0:T(8,128)(2,1)}, bf16[128,2048]{1,0:T(8,128)(2,1)S(1)}, u32[]{:S(2)}, u32[]{:S(2)}) collective-permute-start(bf16[128,2048]{1,0:T(8,128)(2,1)} %get-tuple-element.45), channel_id=1, source_target_pairs={{0,1},{1,0},{2,3},{3,2},{4,5},{5,4},{6,7},{7,6},{8,9},{9,8},{10,11... | collective-permute-start | bytes 1572872 | tf_op jit(solution)/shard_map/ppermute | solution.py:54
  198.0 11.1 %copy-start.10 = (bf16[128,2048]{1,0:T(8,128)(2,1)}, bf16[128,2048]{1,0:T(8,128)(2,1)S(1)}, u32[]{:S(2)}) copy-start(bf16[128,2048]{1,0:T(8,128)(2,1)S(1)} %collective-permute-done.21.refs_3_) | copy-start | bytes 1572868
  198.0 11.1 %collective-permute-start.22 = (bf16[128,2048]{1,0:T(8,128)(2,1)S(1)}, bf16[128,2048]{1,0:T(8,128)(2,1)S(1)}, u32[]{:S(2)}, u32[]{:S(2)}) collective-permute-start(bf16[128,2048]{1,0:T(8,128)(2,1)S(1)} %add_convert_fusion), channel_id=1, source_target_pairs={{1,2},{2,1},{5,6},{6,5},{9,10},{10,9},{13,14},{14,13},{17,18},{18,... | collective-permute-start | bytes 1572872 | tf_op jit(solution)/shard_map/ppermute | solution.py:54
  209.2 0.8 copy-start.12
  209.2 1.0 copy-start.16
Sparse Core Ops, SparseCore 0:
  60.2 96.5 all-gather.1

commit v5 on v4

--- a/solution.py
+++ b/solution.py
@@ -62,12 +62,12 @@
     return jnp.stack([me, me ^ 1, jnp.where(low, 2, 1), jnp.where(low, 3, 0)]).astype(jnp.int32)
 
 
-def gather_line(value, count):
+def gather_line(value, count, *earlier):
     if count != 4:
         return [[value]] + [[shift(value, "seq", count, k)] for k in range(1, count)]
     middle = along(value, count, [(1, 2), (2, 1)])
     far = along(value, count, [(0, 2), (3, 1)])
-    middle_on = along(middle, count, [(1, 0), (2, 3)])
+    middle_on = along(after(middle, *earlier), count, [(1, 0), (2, 3)])
     far_on = along(far, count, [(1, 0), (2, 3)])
     near = along(value, count, [(0, 1), (1, 0), (2, 3), (3, 2)])
     return [[value], [near], [middle, middle_on], [far, far_on]]
@@ -88,12 +88,12 @@
         return (mine.astype(F32) + other.astype(F32)).astype(BF16), mine
 
     far, done_far = joined(3)
-    far_back = along(far, count, [(2, 0), (1, 3)])
     done = (done_far,)
     middle, done_middle = joined(2)
-    done = (done_middle, far)
+    done = (done_middle,)
     near, mine = part(1), part(0)
-    middle_back = along(after(middle, far_back, mine), count, [(1, 2), (2, 1)])
+    far_back = along(after(far, mine), count, [(2, 0), (1, 3)])
+    middle_back = along(after(middle, mine), count, [(1, 2), (2, 1)])
     near_back = along(near, count, [(0, 1), (1, 0), (2, 3), (3, 2)])
     return [mine, near_back, middle_back, far_back]
 
@@ -370,12 +370,13 @@
     return [[next(refs) for _ in range(count)] for count in counts]
 
 
-def forward_kernel(terms, strips, *refs):
-    x_refs, weights, refs = refs[: sum(terms)], refs[sum(terms)], refs[sum(terms) + 1 :]
+def forward_kernel(terms, shares, strips, *refs):
+    x_refs, refs = refs[: sum(terms)], refs[sum(terms) :]
+    early, weights, refs = refs[0], refs[1], refs[2:]
     count = len(terms)
-    outs, (x, inner, spare, gate_up, down, sems, weight_sems) = refs[:count], refs[count:]
+    outs, (x, inner, spare, sems) = refs[:count], refs[count:]
     rows = x_refs[0].shape[0]
-    shares, depth, hidden = down.shape
+    depth = x.shape[1] // shares
     copies, spares = [], iter(range(sum(terms)))
     for k, arrays in enumerate(unflatten(x_refs, terms)):
         copies.append([])
@@ -385,75 +386,64 @@
             copy = pltpu.make_async_copy(array, target, sems.at[spot])
             copy.start()
             copies[k].append((copy, None if i == 0 else spot - k - 1))
-    weights = weights.reshape(shares, 3 * depth, hidden)
-    weight_copies = []
-    for i, strip in enumerate(strips):
-        columns = pl.ds(*strip)
-        weight_copies.append(
-            pltpu.make_async_copy(
-                weights.at[:, : 2 * depth, columns], gate_up.at[:, :, columns], weight_sems.at[i]
-            )
-        )
-    weight_copies.append(
-        pltpu.make_async_copy(weights.at[:, 2 * depth :, :], down, weight_sems.at[len(strips)])
-    )
-    for copy in weight_copies:
-        copy.start()
     for k, group in enumerate(copies):
         for copy, spot in group:
             copy.wait()
             if spot is not None:
                 x[k * rows : (k + 1) * rows, :] += spare[spot]
 
-    def product(which, start, size):
+    half = depth // 2
+
+    def product(sources, start, size):
         total = None
         for r in range(shares):
-            term = jnp.dot(
-                x[:, r * depth : (r + 1) * depth],
-                gate_up[r, which * depth : (which + 1) * depth, start : start + size],
-                preferred_element_type=F32,
-            )
-            total = term if total is None else total + term
+            at = r * depth
+            for source, low, height in sources:
+                low = low + r * (half if source is early else 5 * half)
+                term = jnp.dot(
+                    x[:, at : at + height],
+                    source[low : low + height, start : start + size],
+                    preferred_element_type=F32,
+                )
+                total = term if total is None else total + term
+                at += height
         return total
 
-    for (start, size), copy in zip(strips, weight_copies):
-        copy.wait()
-        opened, upward = product(0, start, size), product(1, start, size)
+    gate_rows = [(weights, 0, depth)]
+    up_rows = [(early, 0, half), (weights, depth, half)]
+    for start, size in strips:
+        opened, upward = product(gate_rows, start, size), product(up_rows, start, size)
         inner[:, start : start + size] = (silu(opened) * upward).astype(BF16)
-    weight_copies[-1].wait()
     for r in range(shares):
-        term = dot_nt(inner[...], down[r]).astype(BF16)
+        low = (5 * r + 3) * half
+        term = dot_nt(inner[...], weights[low : low + depth, :]).astype(BF16)
         for k in range(count):
             outs[k][:, r * depth : (r + 1) * depth] = term[k * rows : (k + 1) * rows]
 
 
-def forward(xs, weights, shares):
+def forward(xs, early, weights, shares):
     rows, width = xs[0][0].shape
     count, hidden = len(xs), weights.shape[1]
-    depth = width // shares
     total = count * rows
     strips = [(start, min(STRIP, hidden - start)) for start in range(0, hidden, STRIP)]
     terms = [len(arrays) for arrays in xs]
     return pl.pallas_call(
-        functools.partial(forward_kernel, terms, strips),
+        functools.partial(forward_kernel, terms, shares, strips),
         out_shape=(jax.ShapeDtypeStruct((rows, width), BF16),) * count,
-        in_specs=[ANY] * (sum(terms) + 1),
+        in_specs=[ANY] * sum(terms) + [VMEM] * 2,
         out_specs=(VMEM,) * count,
         scratch_shapes=[
             pltpu.VMEM((total, width), BF16),
             pltpu.VMEM((total, hidden), BF16),
             pltpu.VMEM((max(1, sum(terms) - count), rows, width), BF16),
-            pltpu.VMEM((shares, 2 * depth, hidden), BF16),
-            pltpu.VMEM((shares, depth, hidden), BF16),
             pltpu.SemaphoreType.DMA((sum(terms),)),
-            pltpu.SemaphoreType.DMA((len(strips) + 1,)),
         ],
-        compiler_params=pltpu.CompilerParams(vmem_limit_bytes=58 * MIB),
+        compiler_params=pltpu.CompilerParams(vmem_limit_bytes=24 * MIB),
         cost_estimate=pl.CostEstimate(
             flops=6 * total * width * hidden, bytes_accessed=20 * MIB, transcendentals=0
         ),
         name="feed_forward",
-    )(*sum(xs, []), weights)
+    )(*sum(xs, []), early, weights)
 
 
 def finish_kernel(count, *refs):
@@ -518,22 +508,25 @@
         out_parts = gather_cube(placed)
     else:
         out_parts = [lax.all_gather(placed, "req", axis=0, tiled=True)]
-    weights = jnp.concatenate([w_gate, w_up, w_down.T], axis=0)
-    weights = lax.all_gather(after(weights, out_parts[0], *xs[1:]), "req", axis=0, tiled=True)
+    half = w_up.shape[0] // 2
+    early = lax.all_gather(w_up[:half], "req", axis=0, tiled=True)
+    weights = jnp.concatenate([w_gate, w_up[half:], w_down.T], axis=0)
+    weights = after(weights, early, out_parts[0], *xs[1:])
+    weights = lax.all_gather(weights, "req", axis=0, tiled=True)
     mixed, state = delta(xs, where, lengths, slot_request, conv_weight, norm_gain[None, :], heads)
     ys = project(mixed, where, owners_of(count), out_parts)
     stream, normed = norm(sum_line(ys, count), residual[0], mlp_gain[None, :])
-    blocks = gather_line(normed, count)
+    blocks = gather_line(normed, count, weights)
     first = min(2, count)
     nearest = []
 
     def near(k, done):
         if not nearest:
-            nearest.extend(forward(after(blocks[:first], *done), weights, n_req))
+            nearest.extend(forward(after(blocks[:first], *done), early, weights, n_req))
         return nearest[k]
 
     def far(k, done):
-        return forward(after([blocks[k]], *done, *blocks[first - 1]), weights, n_req)[0]
+        return forward(after([blocks[k]], *done, *blocks[first - 1]), early, weights, n_req)[0]
 
     parts = [functools.partial(near if k < first else far, k) for k in range(count)]
     hidden = finish(sum_line(parts, count), where, lengths, slot_request, stream)

time: 220 us -> 215 us (0.977)
  starting transfers between devices: 74.3 us -> 58.2 us
  waiting for transfers between devices: 75.7 us -> 89.1 us
  Pallas kernels: 46.6 us -> 36 us
  local copies, waits for them, and re-layouts: 4.3 us -> 11.4 us
    ppermute x15, starting transfers between devices: 33.7 us -> 20.4 us  [along(): return lax.ppermute(value, 'seq', pairs)]
    pallas_call x3, Pallas kernels: 27.9 us -> 17.3 us  [forward(): pl.pallas_call(functools.partial(forward_kernel, terms, shares, strips),...]
    ppermute x15, waiting for transfers between devices: 65.3 us -> 72.1 us  [along(): return lax.ppermute(value, 'seq', pairs)]
    ppermute x4, waiting for transfers between devices: 4.35 us -> 10.3 us  [flip(): lax.ppermute(value, 'req', [(i, i ^ bits) for i in range(lax.axis_size('r...]
    unnamed x40 -> x48, local copies, waits for them, and re-layouts: 4.29 us -> 9.53 us
    ppermute x4, starting transfers between devices: 30.4 us -> 27.5 us  [flip(): lax.ppermute(value, 'req', [(i, i ^ bits) for i in range(lax.axis_size('r...]
    all_gather x1 -> x2, waiting for transfers between devices: 5.99 us -> 6.71 us  [the longest x1 6.69 us: local(): weights = lax.all_gather(weights, 'req', axis=0, tiled=True)]
  transfers between devices with their start and end apart: 24 -> 25, of which waited for: 13 -> 11; matrix products, arithmetic and copies ran while one was open for 3% -> 4% of each run, Pallas kernels for 20% -> 15%
where the time goes in v5:
time: 215 us; the launch traced here: 214 us
  waiting for transfers between devices  89.1 us (41%)
  starting transfers between devices  58.2 us (27%)
  Pallas kernels  36 us (17%)
  between operations  14.5 us (7%)
  local copies, waits for them, and re-layouts  11.4 us (5%)
  other arithmetic  5.05 us (2%)
    ppermute x15, waiting for transfers between devices, along(): return lax.ppermute(value, 'seq', pairs)  72.1 us
    ppermute x4, starting transfers between devices, flip(): lax.ppermute(value, 'req', [(i, i ^ bits) for i in range(lax.axis_size('r...  27.5 us
    ppermute x15, starting transfers between devices, along(): return lax.ppermute(value, 'seq', pairs)  20.4 us
    pallas_call x3, Pallas kernels, forward(): pl.pallas_call(functools.partial(forward_kernel, terms, shares, strips),...  17.3 us
    ppermute x4, waiting for transfers between devices, flip(): lax.ppermute(value, 'req', [(i, i ^ bits) for i in range(lax.axis_size('r...  10.3 us
    unnamed x48, local copies, waits for them, and re-layouts  9.53 us
    ppermute x3, starting transfers between devices, shift(): lax.ppermute(value, axis, [(i, (i + steps) % count) for i in range(count)])  8.53 us
    all_gather x1, waiting for transfers between devices, local(): weights = lax.all_gather(weights, 'req', axis=0, tiled=True)  6.69 us
  transfers between devices with their start and end apart: 25, of which 11 were waited for; matrix products, arithmetic and copies ran while one was open for 4% of the time, Pallas kernels for 15%

profile of v5, /device:TPU:0, one launch (start us, length us, event | category | flops | bytes accessed | tf_op | source)
XLA Modules:
  0.0 214.3 jit_solution(15079239738160344671)
XLA Ops:
  7.2 0.0 all-gather.3.cloned.1.call-start
  7.2 1.9 fusion.1
  9.1 0.0 all-gather.3.cloned.1.call-update
  9.1 0.0 all-gather.5.cloned.1.call-start
  9.2 1.6 collective-permute-start.3
  10.8 0.6 pad_add_fusion.refs_0_.refs_4_
  11.3 2.9 %pack.1 = (bf16[144,1536]{1,0:T(8,128)(2,1)}, bf16[144,1536]{1,0:T(8,128)(2,1)}, bf16[144,1536]{1,0:T(8,128)(2,1)}, bf16[144,1536]{1,0:T(8,128)(2,1)}) custom-call(s32[2]{0:T(128)} %pad_add_fusion.refs_0_.refs_4_, s32[8]{0:T(128)} %refs_5_.3, s32[8]{0:T(128)} %refs_6_.3, bf16[128,4096]{1,0:T(8,128)(2,1)} %bitcast.25, bf16[128,2048]{1,0:T(8,128)(2,1)} %bitcast.28, ...), custom_call_target="tpu_custom_call" | custom-call | tf_op jit(solution)/shard_map/pack/pallas_call | solution.py:157
  14.3 3.3 %collective-permute-start = (bf16[144,1536]{1,0:T(8,128)(2,1)}, bf16[144,1536]{1,0:T(8,128)(2,1)S(1)}, u32[]{:S(2)}, u32[]{:S(2)}) collective-permute-start(bf16[144,1536]{1,0:T(8,128)(2,1)} %get-tuple-element.30), channel_id=1, source_target_pairs={{0,1},{1,2},{2,3},{3,0},{4,5},{5,6},{6,7},{7,4},{8,9},{9,10},{10,1... | collective-permute-start | bytes 1327112 | tf_op jit(solution)/shard_map/ppermute | solution.py:42
  17.6 3.2 %collective-permute-start.1 = (bf16[144,1536]{1,0:T(8,128)(2,1)}, bf16[144,1536]{1,0:T(8,128)(2,1)S(1)}, u32[]{:S(2)}, u32[]{:S(2)}) collective-permute-start(bf16[144,1536]{1,0:T(8,128)(2,1)} %get-tuple-element.31), channel_id=1, source_target_pairs={{0,2},{1,3},{2,0},{3,1},{4,6},{5,7},{6,4},{7,5},{8,10},{9,11},{10,... | collective-permute-start | bytes 1327112 | tf_op jit(solution)/shard_map/ppermute | solution.py:42
  20.8 2.0 collective-permute-start.2
  22.8 1.4 copy.17
  24.2 25.5 %collective-permute-start.4 = (bf16[64,2048]{1,0:T(8,128)(2,1)S(1)}, bf16[64,2048]{1,0:T(8,128)(2,1)}, u32[]{:S(2)}, u32[]{:S(2)}) collective-permute-start(bf16[64,2048]{1,0:T(8,128)(2,1)S(1)} %collective-permute-done.3), channel_id=1, source_target_pairs={{0,8},{4,12},{8,0},{12,4},{16,24},{20,28},{24,16},{28,20},{1,9},{5... | collective-permute-start | bytes 786440 | tf_op jit(solution)/shard_map/ppermute | solution.py:46
  49.7 0.0 copy-start.12
  49.8 2.5 %pad_maximum_fusion = bf16[640,1408]{1,0:T(8,128)(2,1)} fusion(bf16[256,1408]{1,0:T(8,128)(2,1)S(1)} %bitcast.24, bf16[128,1408]{1,0:T(8,128)(2,1)S(1)} %get-tuple-element.56, bf16[256,1408]{1,0:T(8,128)(2,1)} %param.25), kind=kLoop, calls=%fused_computation | loop fusion | flops 5406720 | bytes 3604480 | tf_op jit(solution)/shard_map/concatenate | solution.py:513
  52.3 2.0 collective-permute-start.5
  54.3 4.0 %collective-permute-done.4 = bf16[64,2048]{1,0:T(8,128)(2,1)} collective-permute-done((bf16[64,2048]{1,0:T(8,128)(2,1)S(1)}, bf16[64,2048]{1,0:T(8,128)(2,1)}, u32[]{:S(2)}, u32[]{:S(2)}) %collective-permute-start.4) | collective-permute-done | bytes 262176 | tf_op jit(solution)/shard_map/ppermute | solution.py:46
  58.3 1.0 constant_dynamic-update-slice_fusion.2
  59.3 6.3 %collective-permute-done.6 = bf16[64,2048]{1,0:T(8,128)(2,1)S(1)} collective-permute-done((bf16[64,2048]{1,0:T(8,128)(2,1)S(1)}, bf16[64,2048]{1,0:T(8,128)(2,1)S(1)}, u32[]{:S(2)}, u32[]{:S(2)}) %collective-permute-start.6) | collective-permute-done | bytes 262176 | tf_op jit(solution)/shard_map/ppermute | solution.py:46
  65.6 0.0 all-gather.3.cloned.1.call-done.refs_2_
  65.7 0.0 all-gather.5.cloned.1.call-update
  65.7 0.1 collective-permute-start.7
  65.8 0.1 pad_add_fusion.1.refs_1_
  65.9 6.6 %delta_rule.1 = (bf16[4,128,512]{2,1,0:T(8,128)(2,1)S(1)}, f32[2,128,256]{2,1,0:T(8,128)}) custom-call(bf16[144,1536]{1,0:T(8,128)(2,1)S(1)} %copy-done.8, bf16[144,1536]{1,0:T(8,128)(2,1)S(1)} %collective-permute-done.refs_1_, bf16[144,1536]{1,0:T(8,128)(2,1)S(1)} %collective-permute-done.1.refs_2_, bf16[144,1536]{1,0:T(8,128)(2,1)S(1)} %collective-permute-done.2.refs_3_, ...), custom_call_target="tpu_custom_call" | custom-call | flops 4000000000 | bytes 4194304 | tf_op jit(solution)/shard_map/delta_rule/pallas_call | solution.py:285
  72.5 3.3 %output_projection.1 = (bf16[128,2048]{1,0:T(8,128)(2,1)S(1)}, bf16[128,2048]{1,0:T(8,128)(2,1)S(1)}, bf16[128,2048]{1,0:T(8,128)(2,1)S(1)}, bf16[128,2048]{1,0:T(8,128)(2,1)S(1)}) custom-call(s32[2]{0:T(128)S(1)} %copy-done.7, s32[4]{0:T(128)S(1)} %pad_add_fusion.1.refs_1_, bf16[4,128,512]{2,1,0:T(8,128)(2,1)S(1)} %get-tuple-element.33.refs_2_, ...), custom_call_target="tpu_custom_call" | custom-call | flops 1073741824 | bytes 4194304 | tf_op jit(solution)/shard_map/output_projection/pallas_call | solution.py:331
  75.9 0.0 copy-start.3
  75.9 0.8 copy-done.3
  76.7 4.3 %collective-permute-start.9 = (bf16[128,2048]{1,0:T(8,128)(2,1)S(1)}, bf16[128,2048]{1,0:T(8,128)(2,1)S(1)}, u32[]{:S(2)}, u32[]{:S(2)}) collective-permute-start(bf16[128,2048]{1,0:T(8,128)(2,1)S(1)} %get-tuple-element.36), channel_id=1, source_target_pairs={{0,1},{3,2},{4,5},{7,6},{8,9},{11,10},{12,13},{15,14},{16,17},{19,... | collective-permute-start | bytes 1572872 | tf_op jit(solution)/shard_map/ppermute | solution.py:54
  81.0 1.3 collective-permute-start.11
  82.3 0.1 collective-permute-start.8
  82.4 10.8 %collective-permute-done.9 = bf16[128,2048]{1,0:T(8,128)(2,1)S(1)} collective-permute-done((bf16[128,2048]{1,0:T(8,128)(2,1)S(1)}, bf16[128,2048]{1,0:T(8,128)(2,1)S(1)}, u32[]{:S(2)}, u32[]{:S(2)}) %collective-permute-start.9) | collective-permute-done | bytes 524320 | tf_op jit(solution)/shard_map/ppermute | solution.py:54
  93.2 0.1 add_convert_fusion.3
  93.3 1.5 collective-permute-start.10
  94.8 9.6 %collective-permute-done.11 = bf16[128,2048]{1,0:T(8,128)(2,1)S(1)} collective-permute-done((bf16[128,2048]{1,0:T(8,128)(2,1)S(1)}, bf16[128,2048]{1,0:T(8,128)(2,1)S(1)}, u32[]{:S(2)}, u32[]{:S(2)}) %collective-permute-start.11) | collective-permute-done | bytes 524320 | tf_op jit(solution)/shard_map/ppermute | solution.py:54
  104.4 0.1 add_convert_fusion.2
  104.5 1.3 collective-permute-start.12
  105.8 9.3 %collective-permute-done.8.refs_1_ = bf16[128,2048]{1,0:T(8,128)(2,1)S(1)} collective-permute-done((bf16[128,2048]{1,0:T(8,128)(2,1)S(1)}, bf16[128,2048]{1,0:T(8,128)(2,1)S(1)}, u32[]{:S(2)}, u32[]{:S(2)}) %collective-permute-start.8) | collective-permute-done | bytes 524320 | tf_op jit(solution)/shard_map/ppermute | solution.py:54
  115.2 6.4 %collective-permute-done.12.refs_3_ = bf16[128,2048]{1,0:T(8,128)(2,1)} collective-permute-done((bf16[128,2048]{1,0:T(8,128)(2,1)S(1)}, bf16[128,2048]{1,0:T(8,128)(2,1)}, u32[]{:S(2)}, u32[]{:S(2)}) %collective-permute-start.12) | collective-permute-done | bytes 524320 | tf_op jit(solution)/shard_map/ppermute | solution.py:54
  121.5 3.0 %stream_norm.1 = (bf16[128,2048]{1,0:T(8,128)(2,1)}, bf16[128,2048]{1,0:T(8,128)(2,1)}) custom-call(bf16[128,2048]{1,0:T(8,128)(2,1)} %copy-done.3, bf16[128,2048]{1,0:T(8,128)(2,1)} %copy-done.15, bf16[128,2048]{1,0:T(8,128)(2,1)} %collective-permute-done.10.refs_2_, bf16[128,2048]{1,0:T(8,128)(2,1)} %collective-permute-done.12.refs_3_, ...), custom_call_target="tpu_custom_call" | custom-call | tf_op jit(solution)/shard_map/stream_norm/pallas_call | solution.py:359
  124.6 2.1 collective-permute-start.16
  126.7 1.5 collective-permute-start.14
  128.2 10.5 %collective-permute-done.16.refs_0_ = bf16[128,2048]{1,0:T(8,128)(2,1)} collective-permute-done((bf16[128,2048]{1,0:T(8,128)(2,1)}, bf16[128,2048]{1,0:T(8,128)(2,1)}, u32[]{:S(2)}, u32[]{:S(2)}) %collective-permute-start.16) | collective-permute-done | bytes 524320 | tf_op jit(solution)/shard_map/ppermute | solution.py:54
  138.6 1.3 collective-permute-start.17
  139.9 6.7 %all-gather.5.cloned.1.call-done.refs_3_ = bf16[5120,1408]{1,0:T(8,128)(2,1)} async-done(((bf16[640,1408]{1,0:T(8,128)(2,1)}), bf16[5120,1408]{1,0:T(8,128)(2,1)}) %all-gather.5.cloned.1.call-update) | async-done | bytes 14417936 | tf_op jit(solution)/shard_map/all_gather | solution.py:515
  146.6 1.5 collective-permute-start.15
  148.1 0.0 collective-permute-done.13.refs_1_
  148.1 4.4 %collective-permute-done.17.refs_1_ = bf16[128,2048]{1,0:T(8,128)(2,1)} collective-permute-done((bf16[128,2048]{1,0:T(8,128)(2,1)}, bf16[128,2048]{1,0:T(8,128)(2,1)}, u32[]{:S(2)}, u32[]{:S(2)}) %collective-permute-start.17) | collective-permute-done | bytes 524320 | tf_op jit(solution)/shard_map/ppermute | solution.py:54
  152.6 5.1 %copy-done = bf16[5120,1408]{1,0:T(8,128)(2,1)S(1)} copy-done((bf16[5120,1408]{1,0:T(8,128)(2,1)S(1)}, bf16[5120,1408]{1,0:T(8,128)(2,1)}, u32[]{:S(2)}) %copy-start) | copy-done | bytes 14417944
  157.7 5.5 %feed_forward.3 = bf16[128,2048]{1,0:T(8,128)(2,1)S(1)} custom-call(bf16[128,2048]{1,0:T(8,128)(2,1)} %collective-permute-done.16.refs_0_, bf16[128,2048]{1,0:T(8,128)(2,1)} %collective-permute-done.17.refs_1_, bf16[1024,1408]{1,0:T(8,128)(2,1)S(1)} %copy-done.1, bf16[5120,1408]{1,0:T(8,128)(2,1)S(1)} %copy-done), custom_call_target="tpu_custom_call" | custom-call | flops 2214592512 | bytes 20971520 | tf_op jit(solution)/shard_map/feed_forward/pallas_call | solution.py:430
  163.2 1.9 collective-permute-start.21
  165.1 5.2 %feed_forward.4 = bf16[128,2048]{1,0:T(8,128)(2,1)S(1)} custom-call(bf16[128,2048]{1,0:T(8,128)(2,1)} %collective-permute-done.14.refs_0_, bf16[128,2048]{1,0:T(8,128)(2,1)S(1)} %collective-permute-done.15.refs_1_, bf16[1024,1408]{1,0:T(8,128)(2,1)S(1)} %copy-done.1, bf16[5120,1408]{1,0:T(8,128)(2,1)S(1)} %copy-done), custom_call_target="tpu_custom_call" | custom-call | flops 2214592512 | bytes 20971520 | tf_op jit(solution)/shard_map/feed_forward/pallas_call | solution.py:430
  170.3 1.7 collective-permute-start.19
  172.1 6.6 %feed_forward.5 = (bf16[128,2048]{1,0:T(8,128)(2,1)S(1)}, bf16[128,2048]{1,0:T(8,128)(2,1)S(1)}) custom-call(bf16[128,2048]{1,0:T(8,128)(2,1)S(1)} %copy-done.2, bf16[128,2048]{1,0:T(8,128)(2,1)S(1)} %collective-permute-done.13.refs_1_, bf16[1024,1408]{1,0:T(8,128)(2,1)S(1)} %copy-done.1, bf16[5120,1408]{1,0:T(8,128)(2,1)S(1)} %bitcast.22), custom_call_target="tpu_custom_call" | custom-call | flops 4429185024 | bytes 20971520 | tf_op jit(solution)/shard_map/feed_forward/pallas_call | solution.py:430
  178.7 0.1 collective-permute-start.18
  178.8 0.1 add_convert_fusion
  178.9 1.3 collective-permute-start.22
  180.2 8.4 %collective-permute-done.19 = bf16[128,2048]{1,0:T(8,128)(2,1)S(1)} collective-permute-done((bf16[128,2048]{1,0:T(8,128)(2,1)S(1)}, bf16[128,2048]{1,0:T(8,128)(2,1)S(1)}, u32[]{:S(2)}, u32[]{:S(2)}) %collective-permute-start.19) | collective-permute-done | bytes 524320 | tf_op jit(solution)/shard_map/ppermute | solution.py:54
  188.6 0.1 add_convert_fusion.1
  188.8 0.7 collective-permute-start.20
  189.5 1.4 fusion
  190.8 12.7 %collective-permute-done.18.refs_1_ = bf16[128,2048]{1,0:T(8,128)(2,1)S(1)} collective-permute-done((bf16[128,2048]{1,0:T(8,128)(2,1)S(1)}, bf16[128,2048]{1,0:T(8,128)(2,1)S(1)}, u32[]{:S(2)}, u32[]{:S(2)}) %collective-permute-start.18) | collective-permute-done | bytes 524320 | tf_op jit(solution)/shard_map/ppermute | solution.py:54
  203.5 0.8 copy-done.14
  204.3 0.2 copy-done.16
  204.5 0.1 copy-done.17
  204.6 2.8 %last_sum.1 = bf16[128,2048]{1,0:T(8,128)(2,1)} custom-call(bf16[128,2048]{1,0:T(8,128)(2,1)} %copy-done.4, bf16[128,2048]{1,0:T(8,128)(2,1)} %copy-done.14, bf16[128,2048]{1,0:T(8,128)(2,1)} %copy-done.17, bf16[128,2048]{1,0:T(8,128)(2,1)} %copy-done.16, s32[2]{0:T(128)} %pad_add_fusion.refs_0_.refs_4_, s32[8]{0:T(128)} %refs_5_.3, s32[8]{0:T(128)} %refs_6_.3, ...), custom_call_target="tpu_custom_call" | custom-call | tf_op jit(solution)/shard_map/last_sum/pallas_call | solution.py:462
  (55 shorter events, 0.2 us)
Async XLA Ops:
  7.2 58.5 %all-gather.3.cloned.1.call-start = ((), (), s32[]{:S(2)}) async-start(), calls=%async_computation | async-start | bytes 3244032 | tf_op jit(solution)/shard_map/all_gather | solution.py:512
  9.1 137.5 %all-gather.5.cloned.1.call-start = ((), (), s32[]{:S(2)}) async-start(), calls=%async_computation.1 | async-start | bytes 16220160 | tf_op jit(solution)/shard_map/all_gather | solution.py:515
  9.2 15.1 %collective-permute-start.3 = (bf16[64,2048]{1,0:T(8,128)(2,1)}, bf16[64,2048]{1,0:T(8,128)(2,1)S(1)}, u32[]{:S(2)}, u32[]{:S(2)}) collective-permute-start(bf16[64,2048]{1,0:T(8,128)(2,1)} %param.23), channel_id=1, source_target_pairs={{0,0},{1,4},{2,8},{3,12},{4,16},{5,20},{6,24},{7,28},{8,1},{9,5},{... | collective-permute-start | bytes 786440 | tf_op jit(solution)/shard_map/ppermute | solution.py:502
  14.3 51.3 %collective-permute-start = (bf16[144,1536]{1,0:T(8,128)(2,1)}, bf16[144,1536]{1,0:T(8,128)(2,1)S(1)}, u32[]{:S(2)}, u32[]{:S(2)}) collective-permute-start(bf16[144,1536]{1,0:T(8,128)(2,1)} %get-tuple-element.30), channel_id=1, source_target_pairs={{0,1},{1,2},{2,3},{3,0},{4,5},{5,6},{6,7},{7,4},{8,9},{9,10},{10,1... | collective-permute-start | bytes 1327112 | tf_op jit(solution)/shard_map/ppermute | solution.py:42
  17.6 48.0 %collective-permute-start.1 = (bf16[144,1536]{1,0:T(8,128)(2,1)}, bf16[144,1536]{1,0:T(8,128)(2,1)S(1)}, u32[]{:S(2)}, u32[]{:S(2)}) collective-permute-start(bf16[144,1536]{1,0:T(8,128)(2,1)} %get-tuple-element.31), channel_id=1, source_target_pairs={{0,2},{1,3},{2,0},{3,1},{4,6},{5,7},{6,4},{7,5},{8,10},{9,11},{10,... | collective-permute-start | bytes 1327112 | tf_op jit(solution)/shard_map/ppermute | solution.py:42
  20.8 44.9 %collective-permute-start.2 = (bf16[144,1536]{1,0:T(8,128)(2,1)}, bf16[144,1536]{1,0:T(8,128)(2,1)S(1)}, u32[]{:S(2)}, u32[]{:S(2)}) collective-permute-start(bf16[144,1536]{1,0:T(8,128)(2,1)} %get-tuple-element.32), channel_id=1, source_target_pairs={{0,3},{1,0},{2,1},{3,2},{4,7},{5,4},{6,5},{7,6},{8,11},{9,8},{10,9... | collective-permute-start | bytes 1327112 | tf_op jit(solution)/shard_map/ppermute | solution.py:42
  24.2 34.0 %collective-permute-start.4 = (bf16[64,2048]{1,0:T(8,128)(2,1)S(1)}, bf16[64,2048]{1,0:T(8,128)(2,1)}, u32[]{:S(2)}, u32[]{:S(2)}) collective-permute-start(bf16[64,2048]{1,0:T(8,128)(2,1)S(1)} %collective-permute-done.3), channel_id=1, source_target_pairs={{0,8},{4,12},{8,0},{12,4},{16,24},{20,28},{24,16},{28,20},{1,9},{5... | collective-permute-start | bytes 786440 | tf_op jit(solution)/shard_map/ppermute | solution.py:46
  49.7 16.1 %copy-start.5 = (s32[8]{0:T(128)S(1)}, s32[8]{0:T(128)}, u32[]{:S(2)}) copy-start(s32[8]{0:T(128)} %refs_5_.3) | copy-start | bytes 100
  49.7 16.1 %copy-start.6 = (s32[8]{0:T(128)S(1)}, s32[8]{0:T(128)}, u32[]{:S(2)}) copy-start(s32[8]{0:T(128)} %refs_6_.3) | copy-start | bytes 100
  49.7 16.1 %copy-start.7 = (s32[2]{0:T(128)S(1)}, s32[2]{0:T(128)}, u32[]{:S(2)}) copy-start(s32[2]{0:T(128)} %pad_add_fusion.refs_0_.refs_4_) | copy-start | bytes 28
  49.7 16.1 %copy-start.8 = (bf16[144,1536]{1,0:T(8,128)(2,1)S(1)}, bf16[144,1536]{1,0:T(8,128)(2,1)}, u32[]{:S(2)}) copy-start(bf16[144,1536]{1,0:T(8,128)(2,1)} %get-tuple-element.29.refs_0_) | copy-start | bytes 1327108
  49.7 16.1 %copy-start.12 = (f32[4,4096]{1,0:T(4,128)S(1)}, f32[4,4096]{1,0:T(4,128)}, u32[]{:S(2)}) copy-start(f32[4,4096]{1,0:T(4,128)} %refs_7_.1) | copy-start | bytes 196612
  49.8 16.1 %copy-start.13 = (f32[256]{0:T(256)S(1)}, f32[256]{0:T(256)}, u32[]{:S(2)}) copy-start(f32[256]{0:T(256)} %param.22) | copy-start | bytes 3076
  52.3 7.0 %collective-permute-start.5 = (bf16[64,2048]{1,0:T(8,128)(2,1)S(1)}, bf16[64,2048]{1,0:T(8,128)(2,1)S(1)}, u32[]{:S(2)}, u32[]{:S(2)}) collective-permute-start(bf16[64,2048]{1,0:T(8,128)(2,1)S(1)} %collective-permute-done.3), channel_id=1, source_target_pairs={{0,16},{4,20},{8,24},{12,28},{16,0},{20,4},{24,8},{28,12},{1,17},{... | collective-permute-start | bytes 786440 | tf_op jit(solution)/shard_map/ppermute | solution.py:46
  58.3 7.3 %collective-permute-start.6 = (bf16[64,2048]{1,0:T(8,128)(2,1)S(1)}, bf16[64,2048]{1,0:T(8,128)(2,1)S(1)}, u32[]{:S(2)}, u32[]{:S(2)}) collective-permute-start(bf16[64,2048]{1,0:T(8,128)(2,1)S(1)} %collective-permute-done.3), channel_id=1, source_target_pairs={{0,24},{4,28},{8,16},{12,20},{16,8},{20,12},{24,0},{28,4},{1,25},{... | collective-permute-start | bytes 786440 | tf_op jit(solution)/shard_map/ppermute | solution.py:46
  65.6 6.9 %copy-start.9 = (bf16[144,1536]{1,0:T(8,128)(2,1)}, bf16[144,1536]{1,0:T(8,128)(2,1)S(1)}, u32[]{:S(2)}) copy-start(bf16[144,1536]{1,0:T(8,128)(2,1)S(1)} %collective-permute-done.refs_1_) | copy-start | bytes 1327108
  65.6 6.9 %copy-start.10 = (bf16[144,1536]{1,0:T(8,128)(2,1)}, bf16[144,1536]{1,0:T(8,128)(2,1)S(1)}, u32[]{:S(2)}) copy-start(bf16[144,1536]{1,0:T(8,128)(2,1)S(1)} %collective-permute-done.1.refs_2_) | copy-start | bytes 1327108
  65.6 6.9 %copy-start.11 = (bf16[144,1536]{1,0:T(8,128)(2,1)}, bf16[144,1536]{1,0:T(8,128)(2,1)S(1)}, u32[]{:S(2)}) copy-start(bf16[144,1536]{1,0:T(8,128)(2,1)S(1)} %collective-permute-done.2.refs_3_) | copy-start | bytes 1327108
  65.7 6.8 %collective-permute-start.7 = (bf16[256,2048]{1,0:T(8,128)(2,1)S(1)}, bf16[256,2048]{1,0:T(8,128)(2,1)}, u32[]{:S(2)}, u32[]{:S(2)}) collective-permute-start(bf16[256,2048]{1,0:T(8,128)(2,1)S(1)} %constant_dynamic-update-slice_fusion.refs_3_), channel_id=1, source_target_pairs={{0,4},{4,0},{8,12},{12,8},{16,20},{20,16},{24,28},{28,24},{1,5},{5... | collective-permute-start | bytes 3145736 | tf_op jit(solution)/shard_map/ppermute | solution.py:46
  75.9 0.8 copy-start.3
  76.7 75.9 %copy-start.1 = (bf16[1024,1408]{1,0:T(8,128)(2,1)S(1)}, bf16[1024,1408]{1,0:T(8,128)(2,1)}, u32[]{:S(2)}) copy-start(bf16[1024,1408]{1,0:T(8,128)(2,1)} %all-gather.3.cloned.1.call-done.refs_2_) | copy-start | bytes 8650756
  76.7 16.5 %collective-permute-start.9 = (bf16[128,2048]{1,0:T(8,128)(2,1)S(1)}, bf16[128,2048]{1,0:T(8,128)(2,1)S(1)}, u32[]{:S(2)}, u32[]{:S(2)}) collective-permute-start(bf16[128,2048]{1,0:T(8,128)(2,1)S(1)} %get-tuple-element.36), channel_id=1, source_target_pairs={{0,1},{3,2},{4,5},{7,6},{8,9},{11,10},{12,13},{15,14},{16,17},{19,... | collective-permute-start | bytes 1572872 | tf_op jit(solution)/shard_map/ppermute | solution.py:54
  81.0 23.4 %collective-permute-start.11 = (bf16[128,2048]{1,0:T(8,128)(2,1)S(1)}, bf16[128,2048]{1,0:T(8,128)(2,1)S(1)}, u32[]{:S(2)}, u32[]{:S(2)}) collective-permute-start(bf16[128,2048]{1,0:T(8,128)(2,1)S(1)} %get-tuple-element.38), channel_id=1, source_target_pairs={{0,1},{3,2},{4,5},{7,6},{8,9},{11,10},{12,13},{15,14},{16,17},{19,... | collective-permute-start | bytes 1572872 | tf_op jit(solution)/shard_map/ppermute | solution.py:54
  82.3 32.9 %collective-permute-start.8 = (bf16[128,2048]{1,0:T(8,128)(2,1)S(1)}, bf16[128,2048]{1,0:T(8,128)(2,1)S(1)}, u32[]{:S(2)}, u32[]{:S(2)}) collective-permute-start(bf16[128,2048]{1,0:T(8,128)(2,1)S(1)} %get-tuple-element.35), channel_id=1, source_target_pairs={{0,1},{1,0},{2,3},{3,2},{4,5},{5,4},{6,7},{7,6},{8,9},{9,8},{10,11... | collective-permute-start | bytes 1572872 | tf_op jit(solution)/shard_map/ppermute | solution.py:54
  93.3 21.9 %collective-permute-start.10 = (bf16[128,2048]{1,0:T(8,128)(2,1)S(1)}, bf16[128,2048]{1,0:T(8,128)(2,1)}, u32[]{:S(2)}, u32[]{:S(2)}) collective-permute-start(bf16[128,2048]{1,0:T(8,128)(2,1)S(1)} %add_convert_fusion.3), channel_id=1, source_target_pairs={{1,2},{2,1},{5,6},{6,5},{9,10},{10,9},{13,14},{14,13},{17,18},{18,... | collective-permute-start | bytes 1572872 | tf_op jit(solution)/shard_map/ppermute | solution.py:54
  104.5 17.0 %collective-permute-start.12 = (bf16[128,2048]{1,0:T(8,128)(2,1)S(1)}, bf16[128,2048]{1,0:T(8,128)(2,1)}, u32[]{:S(2)}, u32[]{:S(2)}) collective-permute-start(bf16[128,2048]{1,0:T(8,128)(2,1)S(1)} %add_convert_fusion.2), channel_id=1, source_target_pairs={{2,0},{1,3},{6,4},{5,7},{10,8},{9,11},{14,12},{13,15},{18,16},{17,... | collective-permute-start | bytes 1572872 | tf_op jit(solution)/shard_map/ppermute | solution.py:54
  115.2 6.4 %copy-start.15 = (bf16[128,2048]{1,0:T(8,128)(2,1)}, bf16[128,2048]{1,0:T(8,128)(2,1)S(1)}, u32[]{:S(2)}) copy-start(bf16[128,2048]{1,0:T(8,128)(2,1)S(1)} %collective-permute-done.8.refs_1_) | copy-start | bytes 1572868
  124.6 14.1 %collective-permute-start.16 = (bf16[128,2048]{1,0:T(8,128)(2,1)}, bf16[128,2048]{1,0:T(8,128)(2,1)}, u32[]{:S(2)}, u32[]{:S(2)}) collective-permute-start(bf16[128,2048]{1,0:T(8,128)(2,1)} %get-tuple-element.47.refs_0_), channel_id=1, source_target_pairs={{0,2},{3,1},{4,6},{7,5},{8,10},{11,9},{12,14},{15,13},{16,18},{19,... | collective-permute-start | bytes 1572872 | tf_op jit(solution)/shard_map/ppermute | solution.py:54
  126.7 13.2 %collective-permute-start.14 = (bf16[128,2048]{1,0:T(8,128)(2,1)}, bf16[128,2048]{1,0:T(8,128)(2,1)}, u32[]{:S(2)}, u32[]{:S(2)}) collective-permute-start(bf16[128,2048]{1,0:T(8,128)(2,1)} %get-tuple-element.47.refs_0_), channel_id=1, source_target_pairs={{1,2},{2,1},{5,6},{6,5},{9,10},{10,9},{13,14},{14,13},{17,18},{18,... | collective-permute-start | bytes 1572872 | tf_op jit(solution)/shard_map/ppermute | solution.py:54
  128.2 20.0 %collective-permute-start.13 = (bf16[128,2048]{1,0:T(8,128)(2,1)}, bf16[128,2048]{1,0:T(8,128)(2,1)S(1)}, u32[]{:S(2)}, u32[]{:S(2)}) collective-permute-start(bf16[128,2048]{1,0:T(8,128)(2,1)} %get-tuple-element.47.refs_0_), channel_id=1, source_target_pairs={{0,1},{1,0},{2,3},{3,2},{4,5},{5,4},{6,7},{7,6},{8,9},{9,8},{10,11... | collective-permute-start | bytes 1572872 | tf_op jit(solution)/shard_map/ppermute | solution.py:54
  138.6 13.9 %collective-permute-start.17 = (bf16[128,2048]{1,0:T(8,128)(2,1)}, bf16[128,2048]{1,0:T(8,128)(2,1)}, u32[]{:S(2)}, u32[]{:S(2)}) collective-permute-start(bf16[128,2048]{1,0:T(8,128)(2,1)} %collective-permute-done.16.refs_0_), channel_id=1, source_target_pairs={{1,0},{2,3},{5,4},{6,7},{9,8},{10,11},{13,12},{14,15},{17,16},{18,... | collective-permute-start | bytes 1572872 | tf_op jit(solution)/shard_map/ppermute | solution.py:54
  146.6 18.5 %collective-permute-start.15 = (bf16[128,2048]{1,0:T(8,128)(2,1)}, bf16[128,2048]{1,0:T(8,128)(2,1)S(1)}, u32[]{:S(2)}, u32[]{:S(2)}) collective-permute-start(bf16[128,2048]{1,0:T(8,128)(2,1)} %collective-permute-done.14.refs_0_), channel_id=1, source_target_pairs={{1,0},{2,3},{5,4},{6,7},{9,8},{10,11},{13,12},{14,15},{17,16},{18,... | collective-permute-start | bytes 1572872 | tf_op jit(solution)/shard_map/ppermute | solution.py:54
  152.6 5.1 %copy-start = (bf16[5120,1408]{1,0:T(8,128)(2,1)S(1)}, bf16[5120,1408]{1,0:T(8,128)(2,1)}, u32[]{:S(2)}) copy-start(bf16[5120,1408]{1,0:T(8,128)(2,1)} %all-gather.5.cloned.1.call-done.refs_3_) | copy-start | bytes 43253764
  157.7 14.4 %slice-start = ((s8[14417920]{0:T(1024)(128)(4,1)}), s8[4194304]{0:T(1024)(128)(4,1)S(1)}, s32[]{:S(2)}) async-start(s8[14417920]{0:T(1024)(128)(4,1)} %bitcast.21), calls=%async_computation.2 | async-start | bytes 8388608
  157.7 14.4 %slice-start.1 = ((s8[14417920]{0:T(1024)(128)(4,1)}), s8[4194304]{0:T(1024)(128)(4,1)S(1)}, s32[]{:S(2)}) async-start(s8[14417920]{0:T(1024)(128)(4,1)} %bitcast.21), calls=%async_computation.3 | async-start | bytes 8388608
  163.2 8.9 %slice-start.2 = ((s8[14417920]{0:T(1024)(128)(4,1)}), s8[4194304]{0:T(1024)(128)(4,1)S(1)}, s32[]{:S(2)}) async-start(s8[14417920]{0:T(1024)(128)(4,1)} %bitcast.21), calls=%async_computation.4 | async-start | bytes 8388608
  163.2 8.9 %slice-start.3 = ((s8[14417920]{0:T(1024)(128)(4,1)}), s8[1835008]{0:T(1024)(128)(4,1)S(1)}, s32[]{:S(2)}) async-start(s8[14417920]{0:T(1024)(128)(4,1)} %bitcast.21), calls=%async_computation.5 | async-start | bytes 3670016
  163.2 8.9 %copy-start.2 = (bf16[128,2048]{1,0:T(8,128)(2,1)S(1)}, bf16[128,2048]{1,0:T(8,128)(2,1)}, u32[]{:S(2)}) copy-start(bf16[128,2048]{1,0:T(8,128)(2,1)} %get-tuple-element.47.refs_0_) | copy-start | bytes 1572868
  163.2 15.6 %collective-permute-start.21 = (bf16[128,2048]{1,0:T(8,128)(2,1)S(1)}, bf16[128,2048]{1,0:T(8,128)(2,1)S(1)}, u32[]{:S(2)}, u32[]{:S(2)}) collective-permute-start(bf16[128,2048]{1,0:T(8,128)(2,1)S(1)} %feed_forward.3), channel_id=1, source_target_pairs={{0,1},{3,2},{4,5},{7,6},{8,9},{11,10},{12,13},{15,14},{16,17},{19,... | collective-permute-start | bytes 1572872 | tf_op jit(solution)/shard_map/ppermute | solution.py:54
  170.3 18.3 %collective-permute-start.19 = (bf16[128,2048]{1,0:T(8,128)(2,1)S(1)}, bf16[128,2048]{1,0:T(8,128)(2,1)S(1)}, u32[]{:S(2)}, u32[]{:S(2)}) collective-permute-start(bf16[128,2048]{1,0:T(8,128)(2,1)S(1)} %feed_forward.4), channel_id=1, source_target_pairs={{0,1},{3,2},{4,5},{7,6},{8,9},{11,10},{12,13},{15,14},{16,17},{19,... | collective-permute-start | bytes 1572872 | tf_op jit(solution)/shard_map/ppermute | solution.py:54
  178.7 10.0 %copy-start.4 = (bf16[128,2048]{1,0:T(8,128)(2,1)}, bf16[128,2048]{1,0:T(8,128)(2,1)S(1)}, u32[]{:S(2)}) copy-start(bf16[128,2048]{1,0:T(8,128)(2,1)S(1)} %get-tuple-element.49.refs_0_) | copy-start | bytes 1572868
  178.7 24.8 %collective-permute-start.18 = (bf16[128,2048]{1,0:T(8,128)(2,1)S(1)}, bf16[128,2048]{1,0:T(8,128)(2,1)S(1)}, u32[]{:S(2)}, u32[]{:S(2)}) collective-permute-start(bf16[128,2048]{1,0:T(8,128)(2,1)S(1)} %get-tuple-element.50), channel_id=1, source_target_pairs={{0,1},{1,0},{2,3},{3,2},{4,5},{5,4},{6,7},{7,6},{8,9},{9,8},{10,11... | collective-permute-start | bytes 1572872 | tf_op jit(solution)/shard_map/ppermute | solution.py:54
  178.9 24.6 %collective-permute-start.22 = (bf16[128,2048]{1,0:T(8,128)(2,1)S(1)}, bf16[128,2048]{1,0:T(8,128)(2,1)S(1)}, u32[]{:S(2)}, u32[]{:S(2)}) collective-permute-start(bf16[128,2048]{1,0:T(8,128)(2,1)S(1)} %add_convert_fusion), channel_id=1, source_target_pairs={{2,0},{1,3},{6,4},{5,7},{10,8},{9,11},{14,12},{13,15},{18,16},{17,... | collective-permute-start | bytes 1572872 | tf_op jit(solution)/shard_map/ppermute | solution.py:54
  188.8 14.8 %collective-permute-start.20 = (bf16[128,2048]{1,0:T(8,128)(2,1)S(1)}, bf16[128,2048]{1,0:T(8,128)(2,1)S(1)}, u32[]{:S(2)}, u32[]{:S(2)}) collective-permute-start(bf16[128,2048]{1,0:T(8,128)(2,1)S(1)} %add_convert_fusion.1), channel_id=1, source_target_pairs={{1,2},{2,1},{5,6},{6,5},{9,10},{10,9},{13,14},{14,13},{17,18},{18,... | collective-permute-start | bytes 1572872 | tf_op jit(solution)/shard_map/ppermute | solution.py:54
  203.5 0.8 copy-start.14
  203.5 1.0 copy-start.16
  203.5 1.1 copy-start.17
Sparse Core Ops, SparseCore 0:
  9.9 46.9 all-gather.2
  65.8 80.7 all-gather.4

commit v6 on v5

--- a/solution.py
+++ b/solution.py
@@ -394,25 +394,24 @@
 
     half = depth // 2
 
-    def product(sources, start, size):
+    def product(which, start, size):
         total = None
         for r in range(shares):
-            at = r * depth
-            for source, low, height in sources:
-                low = low + r * (half if source is early else 5 * half)
-                term = jnp.dot(
-                    x[:, at : at + height],
-                    source[low : low + height, start : start + size],
-                    preferred_element_type=F32,
-                )
-                total = term if total is None else total + term
-                at += height
+            columns, low = slice(start, start + size), 5 * r * half
+            if which == 0:
+                rhs = weights[low : low + depth, columns]
+            else:
+                ahead = early[r * half : (r + 1) * half, columns]
+                rest = weights[low + depth : low + depth + half, columns]
+                rhs = jnp.concatenate([ahead, rest], axis=0)
+            term = jnp.dot(
+                x[:, r * depth : (r + 1) * depth], rhs, preferred_element_type=F32
+            )
+            total = term if total is None else total + term
         return total
 
-    gate_rows = [(weights, 0, depth)]
-    up_rows = [(early, 0, half), (weights, depth, half)]
     for start, size in strips:
-        opened, upward = product(gate_rows, start, size), product(up_rows, start, size)
+        opened, upward = product(0, start, size), product(1, start, size)
         inner[:, start : start + size] = (silu(opened) * upward).astype(BF16)
     for r in range(shares):
         low = (5 * r + 3) * half

time: 215 us -> 213 us (level)
  Pallas kernels: 36 us -> 33.6 us
    pallas_call x3, Pallas kernels: 17.3 us -> 14.9 us  [forward(): pl.pallas_call(functools.partial(forward_kernel, terms, shares, strips),...]
  transfers between devices with their start and end apart: 25 -> 25, of which waited for: 11 -> 12; matrix products, arithmetic and copies ran while one was open for 4% -> 4% of each run, Pallas kernels for 15% -> 15%
where the time goes in v6:
time: 213 us; the launch traced here: 212 us
  waiting for transfers between devices  89.1 us (42%)
  starting transfers between devices  57.9 us (27%)
  Pallas kernels  33.6 us (16%)
  between operations  14.5 us (7%)
  local copies, waits for them, and re-layouts  11.4 us (5%)
  other arithmetic  5.05 us (2%)
    ppermute x15, waiting for transfers between devices, along(): return lax.ppermute(value, 'seq', pairs)  72.1 us
    ppermute x4, starting transfers between devices, flip(): lax.ppermute(value, 'req', [(i, i ^ bits) for i in range(lax.axis_size('r...  27.5 us
    ppermute x15, starting transfers between devices, along(): return lax.ppermute(value, 'seq', pairs)  20.2 us
    pallas_call x3, Pallas kernels, forward(): pl.pallas_call(functools.partial(forward_kernel, terms, shares, strips),...  14.9 us
    ppermute x4, waiting for transfers between devices, flip(): lax.ppermute(value, 'req', [(i, i ^ bits) for i in range(lax.axis_size('r...  10.3 us
    unnamed x48, local copies, waits for them, and re-layouts  9.53 us
    ppermute x3, starting transfers between devices, shift(): lax.ppermute(value, axis, [(i, (i + steps) % count) for i in range(count)])  8.53 us
    all_gather x1, waiting for transfers between devices, local(): weights = lax.all_gather(weights, 'req', axis=0, tiled=True)  6.69 us
  transfers between devices with their start and end apart: 25, of which 12 were waited for; matrix products, arithmetic and copies ran while one was open for 4% of the time, Pallas kernels for 15%

profile of v6, /device:TPU:0, one launch (start us, length us, event | category | flops | bytes accessed | tf_op | source)
XLA Modules:
  0.0 211.6 jit_solution(4309451546790769132)
XLA Ops:
  7.2 0.0 all-gather.3.cloned.1.call-start
  7.2 1.9 fusion.1
  9.1 0.0 all-gather.3.cloned.1.call-update
  9.1 0.0 all-gather.5.cloned.1.call-start
  9.2 1.6 collective-permute-start.3
  10.8 0.6 pad_add_fusion.refs_0_.refs_4_
  11.3 2.9 %pack.1 = (bf16[144,1536]{1,0:T(8,128)(2,1)}, bf16[144,1536]{1,0:T(8,128)(2,1)}, bf16[144,1536]{1,0:T(8,128)(2,1)}, bf16[144,1536]{1,0:T(8,128)(2,1)}) custom-call(s32[2]{0:T(128)} %pad_add_fusion.refs_0_.refs_4_, s32[8]{0:T(128)} %refs_5_.3, s32[8]{0:T(128)} %refs_6_.3, bf16[128,4096]{1,0:T(8,128)(2,1)} %bitcast.25, bf16[128,2048]{1,0:T(8,128)(2,1)} %bitcast.28, ...), custom_call_target="tpu_custom_call" | custom-call | tf_op jit(solution)/shard_map/pack/pallas_call | solution.py:157
  14.3 3.3 %collective-permute-start = (bf16[144,1536]{1,0:T(8,128)(2,1)}, bf16[144,1536]{1,0:T(8,128)(2,1)S(1)}, u32[]{:S(2)}, u32[]{:S(2)}) collective-permute-start(bf16[144,1536]{1,0:T(8,128)(2,1)} %get-tuple-element.30), channel_id=1, source_target_pairs={{0,1},{1,2},{2,3},{3,0},{4,5},{5,6},{6,7},{7,4},{8,9},{9,10},{10,1... | collective-permute-start | bytes 1327112 | tf_op jit(solution)/shard_map/ppermute | solution.py:42
  17.6 3.2 %collective-permute-start.1 = (bf16[144,1536]{1,0:T(8,128)(2,1)}, bf16[144,1536]{1,0:T(8,128)(2,1)S(1)}, u32[]{:S(2)}, u32[]{:S(2)}) collective-permute-start(bf16[144,1536]{1,0:T(8,128)(2,1)} %get-tuple-element.31), channel_id=1, source_target_pairs={{0,2},{1,3},{2,0},{3,1},{4,6},{5,7},{6,4},{7,5},{8,10},{9,11},{10,... | collective-permute-start | bytes 1327112 | tf_op jit(solution)/shard_map/ppermute | solution.py:42
  20.8 2.0 collective-permute-start.2
  22.8 1.4 copy.17
  24.2 25.5 %collective-permute-start.4 = (bf16[64,2048]{1,0:T(8,128)(2,1)S(1)}, bf16[64,2048]{1,0:T(8,128)(2,1)}, u32[]{:S(2)}, u32[]{:S(2)}) collective-permute-start(bf16[64,2048]{1,0:T(8,128)(2,1)S(1)} %collective-permute-done.3), channel_id=1, source_target_pairs={{0,8},{4,12},{8,0},{12,4},{16,24},{20,28},{24,16},{28,20},{1,9},{5... | collective-permute-start | bytes 786440 | tf_op jit(solution)/shard_map/ppermute | solution.py:46
  49.7 0.0 copy-start.12
  49.8 2.5 %pad_maximum_fusion = bf16[640,1408]{1,0:T(8,128)(2,1)} fusion(bf16[256,1408]{1,0:T(8,128)(2,1)S(1)} %bitcast.24, bf16[128,1408]{1,0:T(8,128)(2,1)S(1)} %get-tuple-element.56, bf16[256,1408]{1,0:T(8,128)(2,1)} %param.25), kind=kLoop, calls=%fused_computation | loop fusion | flops 5406720 | bytes 3604480 | tf_op jit(solution)/shard_map/concatenate | solution.py:512
  52.3 2.0 collective-permute-start.5
  54.3 4.0 %collective-permute-done.4 = bf16[64,2048]{1,0:T(8,128)(2,1)} collective-permute-done((bf16[64,2048]{1,0:T(8,128)(2,1)S(1)}, bf16[64,2048]{1,0:T(8,128)(2,1)}, u32[]{:S(2)}, u32[]{:S(2)}) %collective-permute-start.4) | collective-permute-done | bytes 262176 | tf_op jit(solution)/shard_map/ppermute | solution.py:46
  58.3 1.0 constant_dynamic-update-slice_fusion.2
  59.3 6.3 %collective-permute-done.6 = bf16[64,2048]{1,0:T(8,128)(2,1)S(1)} collective-permute-done((bf16[64,2048]{1,0:T(8,128)(2,1)S(1)}, bf16[64,2048]{1,0:T(8,128)(2,1)S(1)}, u32[]{:S(2)}, u32[]{:S(2)}) %collective-permute-start.6) | collective-permute-done | bytes 262176 | tf_op jit(solution)/shard_map/ppermute | solution.py:46
  65.6 0.0 all-gather.3.cloned.1.call-done.refs_2_
  65.7 0.0 all-gather.5.cloned.1.call-update
  65.7 0.1 collective-permute-start.7
  65.8 0.1 pad_add_fusion.1.refs_1_
  65.9 6.6 %delta_rule.1 = (bf16[4,128,512]{2,1,0:T(8,128)(2,1)S(1)}, f32[2,128,256]{2,1,0:T(8,128)}) custom-call(bf16[144,1536]{1,0:T(8,128)(2,1)S(1)} %copy-done.8, bf16[144,1536]{1,0:T(8,128)(2,1)S(1)} %collective-permute-done.refs_1_, bf16[144,1536]{1,0:T(8,128)(2,1)S(1)} %collective-permute-done.1.refs_2_, bf16[144,1536]{1,0:T(8,128)(2,1)S(1)} %collective-permute-done.2.refs_3_, ...), custom_call_target="tpu_custom_call" | custom-call | flops 4000000000 | bytes 4194304 | tf_op jit(solution)/shard_map/delta_rule/pallas_call | solution.py:285
  72.5 3.3 %output_projection.1 = (bf16[128,2048]{1,0:T(8,128)(2,1)S(1)}, bf16[128,2048]{1,0:T(8,128)(2,1)S(1)}, bf16[128,2048]{1,0:T(8,128)(2,1)S(1)}, bf16[128,2048]{1,0:T(8,128)(2,1)S(1)}) custom-call(s32[2]{0:T(128)S(1)} %copy-done.7, s32[4]{0:T(128)S(1)} %pad_add_fusion.1.refs_1_, bf16[4,128,512]{2,1,0:T(8,128)(2,1)S(1)} %get-tuple-element.33.refs_2_, ...), custom_call_target="tpu_custom_call" | custom-call | flops 1073741824 | bytes 4194304 | tf_op jit(solution)/shard_map/output_projection/pallas_call | solution.py:331
  75.9 0.8 copy-done.3
  76.7 4.3 %collective-permute-start.9 = (bf16[128,2048]{1,0:T(8,128)(2,1)S(1)}, bf16[128,2048]{1,0:T(8,128)(2,1)S(1)}, u32[]{:S(2)}, u32[]{:S(2)}) collective-permute-start(bf16[128,2048]{1,0:T(8,128)(2,1)S(1)} %get-tuple-element.36), channel_id=1, source_target_pairs={{0,1},{3,2},{4,5},{7,6},{8,9},{11,10},{12,13},{15,14},{16,17},{19,... | collective-permute-start | bytes 1572872 | tf_op jit(solution)/shard_map/ppermute | solution.py:54
  81.0 1.3 collective-permute-start.11
  82.3 0.1 collective-permute-start.8
  82.4 10.8 %collective-permute-done.9 = bf16[128,2048]{1,0:T(8,128)(2,1)S(1)} collective-permute-done((bf16[128,2048]{1,0:T(8,128)(2,1)S(1)}, bf16[128,2048]{1,0:T(8,128)(2,1)S(1)}, u32[]{:S(2)}, u32[]{:S(2)}) %collective-permute-start.9) | collective-permute-done | bytes 524320 | tf_op jit(solution)/shard_map/ppermute | solution.py:54
  93.2 0.1 add_convert_fusion.3
  93.3 1.5 collective-permute-start.10
  94.8 9.6 %collective-permute-done.11 = bf16[128,2048]{1,0:T(8,128)(2,1)S(1)} collective-permute-done((bf16[128,2048]{1,0:T(8,128)(2,1)S(1)}, bf16[128,2048]{1,0:T(8,128)(2,1)S(1)}, u32[]{:S(2)}, u32[]{:S(2)}) %collective-permute-start.11) | collective-permute-done | bytes 524320 | tf_op jit(solution)/shard_map/ppermute | solution.py:54
  104.4 0.1 add_convert_fusion.2
  104.5 1.3 collective-permute-start.12
  105.8 9.3 %collective-permute-done.8.refs_1_ = bf16[128,2048]{1,0:T(8,128)(2,1)S(1)} collective-permute-done((bf16[128,2048]{1,0:T(8,128)(2,1)S(1)}, bf16[128,2048]{1,0:T(8,128)(2,1)S(1)}, u32[]{:S(2)}, u32[]{:S(2)}) %collective-permute-start.8) | collective-permute-done | bytes 524320 | tf_op jit(solution)/shard_map/ppermute | solution.py:54
  115.2 6.4 %collective-permute-done.12.refs_3_ = bf16[128,2048]{1,0:T(8,128)(2,1)} collective-permute-done((bf16[128,2048]{1,0:T(8,128)(2,1)S(1)}, bf16[128,2048]{1,0:T(8,128)(2,1)}, u32[]{:S(2)}, u32[]{:S(2)}) %collective-permute-start.12) | collective-permute-done | bytes 524320 | tf_op jit(solution)/shard_map/ppermute | solution.py:54
  121.5 3.0 %stream_norm.1 = (bf16[128,2048]{1,0:T(8,128)(2,1)}, bf16[128,2048]{1,0:T(8,128)(2,1)}) custom-call(bf16[128,2048]{1,0:T(8,128)(2,1)} %copy-done.3, bf16[128,2048]{1,0:T(8,128)(2,1)} %copy-done.15, bf16[128,2048]{1,0:T(8,128)(2,1)} %collective-permute-done.10.refs_2_, bf16[128,2048]{1,0:T(8,128)(2,1)} %collective-permute-done.12.refs_3_, ...), custom_call_target="tpu_custom_call" | custom-call | tf_op jit(solution)/shard_map/stream_norm/pallas_call | solution.py:359
  124.6 2.1 %collective-permute-start.16 = (bf16[128,2048]{1,0:T(8,128)(2,1)}, bf16[128,2048]{1,0:T(8,128)(2,1)}, u32[]{:S(2)}, u32[]{:S(2)}) collective-permute-start(bf16[128,2048]{1,0:T(8,128)(2,1)} %get-tuple-element.47.refs_0_), channel_id=1, source_target_pairs={{0,2},{3,1},{4,6},{7,5},{8,10},{11,9},{12,14},{15,13},{16,18},{19,... | collective-permute-start | bytes 1572872 | tf_op jit(solution)/shard_map/ppermute | solution.py:54
  126.7 1.5 collective-permute-start.14
  128.2 10.5 %collective-permute-done.16.refs_0_ = bf16[128,2048]{1,0:T(8,128)(2,1)} collective-permute-done((bf16[128,2048]{1,0:T(8,128)(2,1)}, bf16[128,2048]{1,0:T(8,128)(2,1)}, u32[]{:S(2)}, u32[]{:S(2)}) %collective-permute-start.16) | collective-permute-done | bytes 524320 | tf_op jit(solution)/shard_map/ppermute | solution.py:54
  138.6 1.3 collective-permute-start.17
  139.9 6.7 %all-gather.5.cloned.1.call-done.refs_3_ = bf16[5120,1408]{1,0:T(8,128)(2,1)} async-done(((bf16[640,1408]{1,0:T(8,128)(2,1)}), bf16[5120,1408]{1,0:T(8,128)(2,1)}) %all-gather.5.cloned.1.call-update) | async-done | bytes 14417936 | tf_op jit(solution)/shard_map/all_gather | solution.py:514
  146.6 1.5 collective-permute-start.15
  148.1 0.0 collective-permute-done.13.refs_1_
  148.1 4.4 %collective-permute-done.17.refs_1_ = bf16[128,2048]{1,0:T(8,128)(2,1)} collective-permute-done((bf16[128,2048]{1,0:T(8,128)(2,1)}, bf16[128,2048]{1,0:T(8,128)(2,1)}, u32[]{:S(2)}, u32[]{:S(2)}) %collective-permute-start.17) | collective-permute-done | bytes 524320 | tf_op jit(solution)/shard_map/ppermute | solution.py:54
  152.6 5.1 %copy-done = bf16[5120,1408]{1,0:T(8,128)(2,1)S(1)} copy-done((bf16[5120,1408]{1,0:T(8,128)(2,1)S(1)}, bf16[5120,1408]{1,0:T(8,128)(2,1)}, u32[]{:S(2)}) %copy-start) | copy-done | bytes 14417944
  157.7 5.0 %feed_forward.3 = bf16[128,2048]{1,0:T(8,128)(2,1)S(1)} custom-call(bf16[128,2048]{1,0:T(8,128)(2,1)} %collective-permute-done.16.refs_0_, bf16[128,2048]{1,0:T(8,128)(2,1)} %collective-permute-done.17.refs_1_, bf16[1024,1408]{1,0:T(8,128)(2,1)S(1)} %copy-done.1, bf16[5120,1408]{1,0:T(8,128)(2,1)S(1)} %copy-done), custom_call_target="tpu_custom_call" | custom-call | flops 2214592512 | bytes 20971520 | tf_op jit(solution)/shard_map/feed_forward/pallas_call | solution.py:429
  162.7 1.9 collective-permute-start.21
  164.6 4.7 %feed_forward.4 = bf16[128,2048]{1,0:T(8,128)(2,1)S(1)} custom-call(bf16[128,2048]{1,0:T(8,128)(2,1)} %collective-permute-done.14.refs_0_, bf16[128,2048]{1,0:T(8,128)(2,1)S(1)} %collective-permute-done.15.refs_1_, bf16[1024,1408]{1,0:T(8,128)(2,1)S(1)} %copy-done.1, bf16[5120,1408]{1,0:T(8,128)(2,1)S(1)} %copy-done), custom_call_target="tpu_custom_call" | custom-call | flops 2214592512 | bytes 20971520 | tf_op jit(solution)/shard_map/feed_forward/pallas_call | solution.py:429
  169.3 1.5 collective-permute-start.19
  170.9 5.2 %feed_forward.5 = (bf16[128,2048]{1,0:T(8,128)(2,1)S(1)}, bf16[128,2048]{1,0:T(8,128)(2,1)S(1)}) custom-call(bf16[128,2048]{1,0:T(8,128)(2,1)S(1)} %copy-done.2, bf16[128,2048]{1,0:T(8,128)(2,1)S(1)} %collective-permute-done.13.refs_1_, bf16[1024,1408]{1,0:T(8,128)(2,1)S(1)} %copy-done.1, bf16[5120,1408]{1,0:T(8,128)(2,1)S(1)} %bitcast.22), custom_call_target="tpu_custom_call" | custom-call | flops 4429185024 | bytes 20971520 | tf_op jit(solution)/shard_map/feed_forward/pallas_call | solution.py:429
  176.0 0.1 collective-permute-start.18
  176.1 0.8 collective-permute-done.21
  176.9 0.1 add_convert_fusion
  177.0 1.3 collective-permute-start.22
  178.3 9.8 %collective-permute-done.19 = bf16[128,2048]{1,0:T(8,128)(2,1)S(1)} collective-permute-done((bf16[128,2048]{1,0:T(8,128)(2,1)S(1)}, bf16[128,2048]{1,0:T(8,128)(2,1)S(1)}, u32[]{:S(2)}, u32[]{:S(2)}) %collective-permute-start.19) | collective-permute-done | bytes 524320 | tf_op jit(solution)/shard_map/ppermute | solution.py:54
  188.1 0.1 add_convert_fusion.1
  188.3 0.7 collective-permute-start.20
  189.0 1.4 fusion
  190.4 10.5 %collective-permute-done.18.refs_1_ = bf16[128,2048]{1,0:T(8,128)(2,1)S(1)} collective-permute-done((bf16[128,2048]{1,0:T(8,128)(2,1)S(1)}, bf16[128,2048]{1,0:T(8,128)(2,1)S(1)}, u32[]{:S(2)}, u32[]{:S(2)}) %collective-permute-start.18) | collective-permute-done | bytes 524320 | tf_op jit(solution)/shard_map/ppermute | solution.py:54
  200.8 0.8 copy-done.14
  201.6 0.2 copy-done.16
  201.8 0.1 copy-done.17
  202.0 2.8 %last_sum.1 = bf16[128,2048]{1,0:T(8,128)(2,1)} custom-call(bf16[128,2048]{1,0:T(8,128)(2,1)} %copy-done.4, bf16[128,2048]{1,0:T(8,128)(2,1)} %copy-done.14, bf16[128,2048]{1,0:T(8,128)(2,1)} %copy-done.17, bf16[128,2048]{1,0:T(8,128)(2,1)} %copy-done.16, s32[2]{0:T(128)} %pad_add_fusion.refs_0_.refs_4_, s32[8]{0:T(128)} %refs_5_.3, s32[8]{0:T(128)} %refs_6_.3, ...), custom_call_target="tpu_custom_call" | custom-call | tf_op jit(solution)/shard_map/last_sum/pallas_call | solution.py:461
  (55 shorter events, 0.2 us)
Async XLA Ops:
  7.2 58.5 %all-gather.3.cloned.1.call-start = ((), (), s32[]{:S(2)}) async-start(), calls=%async_computation | async-start | bytes 3244032 | tf_op jit(solution)/shard_map/all_gather | solution.py:511
  9.1 137.5 %all-gather.5.cloned.1.call-start = ((), (), s32[]{:S(2)}) async-start(), calls=%async_computation.1 | async-start | bytes 16220160 | tf_op jit(solution)/shard_map/all_gather | solution.py:514
  9.2 15.1 %collective-permute-start.3 = (bf16[64,2048]{1,0:T(8,128)(2,1)}, bf16[64,2048]{1,0:T(8,128)(2,1)S(1)}, u32[]{:S(2)}, u32[]{:S(2)}) collective-permute-start(bf16[64,2048]{1,0:T(8,128)(2,1)} %param.23), channel_id=1, source_target_pairs={{0,0},{1,4},{2,8},{3,12},{4,16},{5,20},{6,24},{7,28},{8,1},{9,5},{... | collective-permute-start | bytes 786440 | tf_op jit(solution)/shard_map/ppermute | solution.py:501
  14.3 51.3 %collective-permute-start = (bf16[144,1536]{1,0:T(8,128)(2,1)}, bf16[144,1536]{1,0:T(8,128)(2,1)S(1)}, u32[]{:S(2)}, u32[]{:S(2)}) collective-permute-start(bf16[144,1536]{1,0:T(8,128)(2,1)} %get-tuple-element.30), channel_id=1, source_target_pairs={{0,1},{1,2},{2,3},{3,0},{4,5},{5,6},{6,7},{7,4},{8,9},{9,10},{10,1... | collective-permute-start | bytes 1327112 | tf_op jit(solution)/shard_map/ppermute | solution.py:42
  17.6 48.0 %collective-permute-start.1 = (bf16[144,1536]{1,0:T(8,128)(2,1)}, bf16[144,1536]{1,0:T(8,128)(2,1)S(1)}, u32[]{:S(2)}, u32[]{:S(2)}) collective-permute-start(bf16[144,1536]{1,0:T(8,128)(2,1)} %get-tuple-element.31), channel_id=1, source_target_pairs={{0,2},{1,3},{2,0},{3,1},{4,6},{5,7},{6,4},{7,5},{8,10},{9,11},{10,... | collective-permute-start | bytes 1327112 | tf_op jit(solution)/shard_map/ppermute | solution.py:42
  20.8 44.9 %collective-permute-start.2 = (bf16[144,1536]{1,0:T(8,128)(2,1)}, bf16[144,1536]{1,0:T(8,128)(2,1)S(1)}, u32[]{:S(2)}, u32[]{:S(2)}) collective-permute-start(bf16[144,1536]{1,0:T(8,128)(2,1)} %get-tuple-element.32), channel_id=1, source_target_pairs={{0,3},{1,0},{2,1},{3,2},{4,7},{5,4},{6,5},{7,6},{8,11},{9,8},{10,9... | collective-permute-start | bytes 1327112 | tf_op jit(solution)/shard_map/ppermute | solution.py:42
  24.2 34.0 %collective-permute-start.4 = (bf16[64,2048]{1,0:T(8,128)(2,1)S(1)}, bf16[64,2048]{1,0:T(8,128)(2,1)}, u32[]{:S(2)}, u32[]{:S(2)}) collective-permute-start(bf16[64,2048]{1,0:T(8,128)(2,1)S(1)} %collective-permute-done.3), channel_id=1, source_target_pairs={{0,8},{4,12},{8,0},{12,4},{16,24},{20,28},{24,16},{28,20},{1,9},{5... | collective-permute-start | bytes 786440 | tf_op jit(solution)/shard_map/ppermute | solution.py:46
  49.7 16.1 %copy-start.5 = (s32[8]{0:T(128)S(1)}, s32[8]{0:T(128)}, u32[]{:S(2)}) copy-start(s32[8]{0:T(128)} %refs_5_.3) | copy-start | bytes 100
  49.7 16.1 %copy-start.6 = (s32[8]{0:T(128)S(1)}, s32[8]{0:T(128)}, u32[]{:S(2)}) copy-start(s32[8]{0:T(128)} %refs_6_.3) | copy-start | bytes 100
  49.7 16.1 %copy-start.7 = (s32[2]{0:T(128)S(1)}, s32[2]{0:T(128)}, u32[]{:S(2)}) copy-start(s32[2]{0:T(128)} %pad_add_fusion.refs_0_.refs_4_) | copy-start | bytes 28
  49.7 16.1 %copy-start.8 = (bf16[144,1536]{1,0:T(8,128)(2,1)S(1)}, bf16[144,1536]{1,0:T(8,128)(2,1)}, u32[]{:S(2)}) copy-start(bf16[144,1536]{1,0:T(8,128)(2,1)} %get-tuple-element.29.refs_0_) | copy-start | bytes 1327108
  49.7 16.1 %copy-start.12 = (f32[4,4096]{1,0:T(4,128)S(1)}, f32[4,4096]{1,0:T(4,128)}, u32[]{:S(2)}) copy-start(f32[4,4096]{1,0:T(4,128)} %refs_7_.1) | copy-start | bytes 196612
  49.8 16.1 %copy-start.13 = (f32[256]{0:T(256)S(1)}, f32[256]{0:T(256)}, u32[]{:S(2)}) copy-start(f32[256]{0:T(256)} %param.22) | copy-start | bytes 3076
  52.3 7.0 %collective-permute-start.5 = (bf16[64,2048]{1,0:T(8,128)(2,1)S(1)}, bf16[64,2048]{1,0:T(8,128)(2,1)S(1)}, u32[]{:S(2)}, u32[]{:S(2)}) collective-permute-start(bf16[64,2048]{1,0:T(8,128)(2,1)S(1)} %collective-permute-done.3), channel_id=1, source_target_pairs={{0,16},{4,20},{8,24},{12,28},{16,0},{20,4},{24,8},{28,12},{1,17},{... | collective-permute-start | bytes 786440 | tf_op jit(solution)/shard_map/ppermute | solution.py:46
  58.3 7.3 %collective-permute-start.6 = (bf16[64,2048]{1,0:T(8,128)(2,1)S(1)}, bf16[64,2048]{1,0:T(8,128)(2,1)S(1)}, u32[]{:S(2)}, u32[]{:S(2)}) collective-permute-start(bf16[64,2048]{1,0:T(8,128)(2,1)S(1)} %collective-permute-done.3), channel_id=1, source_target_pairs={{0,24},{4,28},{8,16},{12,20},{16,8},{20,12},{24,0},{28,4},{1,25},{... | collective-permute-start | bytes 786440 | tf_op jit(solution)/shard_map/ppermute | solution.py:46
  65.6 6.9 %copy-start.9 = (bf16[144,1536]{1,0:T(8,128)(2,1)}, bf16[144,1536]{1,0:T(8,128)(2,1)S(1)}, u32[]{:S(2)}) copy-start(bf16[144,1536]{1,0:T(8,128)(2,1)S(1)} %collective-permute-done.refs_1_) | copy-start | bytes 1327108
  65.6 6.9 %copy-start.10 = (bf16[144,1536]{1,0:T(8,128)(2,1)}, bf16[144,1536]{1,0:T(8,128)(2,1)S(1)}, u32[]{:S(2)}) copy-start(bf16[144,1536]{1,0:T(8,128)(2,1)S(1)} %collective-permute-done.1.refs_2_) | copy-start | bytes 1327108
  65.6 6.9 %copy-start.11 = (bf16[144,1536]{1,0:T(8,128)(2,1)}, bf16[144,1536]{1,0:T(8,128)(2,1)S(1)}, u32[]{:S(2)}) copy-start(bf16[144,1536]{1,0:T(8,128)(2,1)S(1)} %collective-permute-done.2.refs_3_) | copy-start | bytes 1327108
  65.7 6.8 %collective-permute-start.7 = (bf16[256,2048]{1,0:T(8,128)(2,1)S(1)}, bf16[256,2048]{1,0:T(8,128)(2,1)}, u32[]{:S(2)}, u32[]{:S(2)}) collective-permute-start(bf16[256,2048]{1,0:T(8,128)(2,1)S(1)} %constant_dynamic-update-slice_fusion.refs_3_), channel_id=1, source_target_pairs={{0,4},{4,0},{8,12},{12,8},{16,20},{20,16},{24,28},{28,24},{1,5},{5... | collective-permute-start | bytes 3145736 | tf_op jit(solution)/shard_map/ppermute | solution.py:46
  75.9 0.8 copy-start.3
  76.7 75.9 %copy-start.1 = (bf16[1024,1408]{1,0:T(8,128)(2,1)S(1)}, bf16[1024,1408]{1,0:T(8,128)(2,1)}, u32[]{:S(2)}) copy-start(bf16[1024,1408]{1,0:T(8,128)(2,1)} %all-gather.3.cloned.1.call-done.refs_2_) | copy-start | bytes 8650756
  76.7 16.5 %collective-permute-start.9 = (bf16[128,2048]{1,0:T(8,128)(2,1)S(1)}, bf16[128,2048]{1,0:T(8,128)(2,1)S(1)}, u32[]{:S(2)}, u32[]{:S(2)}) collective-permute-start(bf16[128,2048]{1,0:T(8,128)(2,1)S(1)} %get-tuple-element.36), channel_id=1, source_target_pairs={{0,1},{3,2},{4,5},{7,6},{8,9},{11,10},{12,13},{15,14},{16,17},{19,... | collective-permute-start | bytes 1572872 | tf_op jit(solution)/shard_map/ppermute | solution.py:54
  81.0 23.4 %collective-permute-start.11 = (bf16[128,2048]{1,0:T(8,128)(2,1)S(1)}, bf16[128,2048]{1,0:T(8,128)(2,1)S(1)}, u32[]{:S(2)}, u32[]{:S(2)}) collective-permute-start(bf16[128,2048]{1,0:T(8,128)(2,1)S(1)} %get-tuple-element.38), channel_id=1, source_target_pairs={{0,1},{3,2},{4,5},{7,6},{8,9},{11,10},{12,13},{15,14},{16,17},{19,... | collective-permute-start | bytes 1572872 | tf_op jit(solution)/shard_map/ppermute | solution.py:54
  82.3 32.9 %collective-permute-start.8 = (bf16[128,2048]{1,0:T(8,128)(2,1)S(1)}, bf16[128,2048]{1,0:T(8,128)(2,1)S(1)}, u32[]{:S(2)}, u32[]{:S(2)}) collective-permute-start(bf16[128,2048]{1,0:T(8,128)(2,1)S(1)} %get-tuple-element.35), channel_id=1, source_target_pairs={{0,1},{1,0},{2,3},{3,2},{4,5},{5,4},{6,7},{7,6},{8,9},{9,8},{10,11... | collective-permute-start | bytes 1572872 | tf_op jit(solution)/shard_map/ppermute | solution.py:54
  93.3 21.9 %collective-permute-start.10 = (bf16[128,2048]{1,0:T(8,128)(2,1)S(1)}, bf16[128,2048]{1,0:T(8,128)(2,1)}, u32[]{:S(2)}, u32[]{:S(2)}) collective-permute-start(bf16[128,2048]{1,0:T(8,128)(2,1)S(1)} %add_convert_fusion.3), channel_id=1, source_target_pairs={{1,2},{2,1},{5,6},{6,5},{9,10},{10,9},{13,14},{14,13},{17,18},{18,... | collective-permute-start | bytes 1572872 | tf_op jit(solution)/shard_map/ppermute | solution.py:54
  104.5 17.0 %collective-permute-start.12 = (bf16[128,2048]{1,0:T(8,128)(2,1)S(1)}, bf16[128,2048]{1,0:T(8,128)(2,1)}, u32[]{:S(2)}, u32[]{:S(2)}) collective-permute-start(bf16[128,2048]{1,0:T(8,128)(2,1)S(1)} %add_convert_fusion.2), channel_id=1, source_target_pairs={{2,0},{1,3},{6,4},{5,7},{10,8},{9,11},{14,12},{13,15},{18,16},{17,... | collective-permute-start | bytes 1572872 | tf_op jit(solution)/shard_map/ppermute | solution.py:54
  115.2 6.4 %copy-start.15 = (bf16[128,2048]{1,0:T(8,128)(2,1)}, bf16[128,2048]{1,0:T(8,128)(2,1)S(1)}, u32[]{:S(2)}) copy-start(bf16[128,2048]{1,0:T(8,128)(2,1)S(1)} %collective-permute-done.8.refs_1_) | copy-start | bytes 1572868
  124.6 14.1 %collective-permute-start.16 = (bf16[128,2048]{1,0:T(8,128)(2,1)}, bf16[128,2048]{1,0:T(8,128)(2,1)}, u32[]{:S(2)}, u32[]{:S(2)}) collective-permute-start(bf16[128,2048]{1,0:T(8,128)(2,1)} %get-tuple-element.47.refs_0_), channel_id=1, source_target_pairs={{0,2},{3,1},{4,6},{7,5},{8,10},{11,9},{12,14},{15,13},{16,18},{19,... | collective-permute-start | bytes 1572872 | tf_op jit(solution)/shard_map/ppermute | solution.py:54
  126.7 13.2 %collective-permute-start.14 = (bf16[128,2048]{1,0:T(8,128)(2,1)}, bf16[128,2048]{1,0:T(8,128)(2,1)}, u32[]{:S(2)}, u32[]{:S(2)}) collective-permute-start(bf16[128,2048]{1,0:T(8,128)(2,1)} %get-tuple-element.47.refs_0_), channel_id=1, source_target_pairs={{1,2},{2,1},{5,6},{6,5},{9,10},{10,9},{13,14},{14,13},{17,18},{18,... | collective-permute-start | bytes 1572872 | tf_op jit(solution)/shard_map/ppermute | solution.py:54
  128.2 20.0 %collective-permute-start.13 = (bf16[128,2048]{1,0:T(8,128)(2,1)}, bf16[128,2048]{1,0:T(8,128)(2,1)S(1)}, u32[]{:S(2)}, u32[]{:S(2)}) collective-permute-start(bf16[128,2048]{1,0:T(8,128)(2,1)} %get-tuple-element.47.refs_0_), channel_id=1, source_target_pairs={{0,1},{1,0},{2,3},{3,2},{4,5},{5,4},{6,7},{7,6},{8,9},{9,8},{10,11... | collective-permute-start | bytes 1572872 | tf_op jit(solution)/shard_map/ppermute | solution.py:54
  138.6 13.9 %collective-permute-start.17 = (bf16[128,2048]{1,0:T(8,128)(2,1)}, bf16[128,2048]{1,0:T(8,128)(2,1)}, u32[]{:S(2)}, u32[]{:S(2)}) collective-permute-start(bf16[128,2048]{1,0:T(8,128)(2,1)} %collective-permute-done.16.refs_0_), channel_id=1, source_target_pairs={{1,0},{2,3},{5,4},{6,7},{9,8},{10,11},{13,12},{14,15},{17,16},{18,... | collective-permute-start | bytes 1572872 | tf_op jit(solution)/shard_map/ppermute | solution.py:54
  146.6 18.0 %collective-permute-start.15 = (bf16[128,2048]{1,0:T(8,128)(2,1)}, bf16[128,2048]{1,0:T(8,128)(2,1)S(1)}, u32[]{:S(2)}, u32[]{:S(2)}) collective-permute-start(bf16[128,2048]{1,0:T(8,128)(2,1)} %collective-permute-done.14.refs_0_), channel_id=1, source_target_pairs={{1,0},{2,3},{5,4},{6,7},{9,8},{10,11},{13,12},{14,15},{17,16},{18,... | collective-permute-start | bytes 1572872 | tf_op jit(solution)/shard_map/ppermute | solution.py:54
  152.6 5.1 %copy-start = (bf16[5120,1408]{1,0:T(8,128)(2,1)S(1)}, bf16[5120,1408]{1,0:T(8,128)(2,1)}, u32[]{:S(2)}) copy-start(bf16[5120,1408]{1,0:T(8,128)(2,1)} %all-gather.5.cloned.1.call-done.refs_3_) | copy-start | bytes 43253764
  157.7 13.1 %slice-start = ((s8[14417920]{0:T(1024)(128)(4,1)}), s8[4194304]{0:T(1024)(128)(4,1)S(1)}, s32[]{:S(2)}) async-start(s8[14417920]{0:T(1024)(128)(4,1)} %bitcast.21), calls=%async_computation.2 | async-start | bytes 8388608
  157.7 13.2 %slice-start.1 = ((s8[14417920]{0:T(1024)(128)(4,1)}), s8[4194304]{0:T(1024)(128)(4,1)S(1)}, s32[]{:S(2)}) async-start(s8[14417920]{0:T(1024)(128)(4,1)} %bitcast.21), calls=%async_computation.3 | async-start | bytes 8388608
  162.7 8.1 %slice-start.2 = ((s8[14417920]{0:T(1024)(128)(4,1)}), s8[4194304]{0:T(1024)(128)(4,1)S(1)}, s32[]{:S(2)}) async-start(s8[14417920]{0:T(1024)(128)(4,1)} %bitcast.21), calls=%async_computation.4 | async-start | bytes 8388608
  162.7 8.1 %slice-start.3 = ((s8[14417920]{0:T(1024)(128)(4,1)}), s8[1835008]{0:T(1024)(128)(4,1)S(1)}, s32[]{:S(2)}) async-start(s8[14417920]{0:T(1024)(128)(4,1)} %bitcast.21), calls=%async_computation.5 | async-start | bytes 3670016
  162.7 8.1 %copy-start.2 = (bf16[128,2048]{1,0:T(8,128)(2,1)S(1)}, bf16[128,2048]{1,0:T(8,128)(2,1)}, u32[]{:S(2)}) copy-start(bf16[128,2048]{1,0:T(8,128)(2,1)} %get-tuple-element.47.refs_0_) | copy-start | bytes 1572868
  162.7 14.2 %collective-permute-start.21 = (bf16[128,2048]{1,0:T(8,128)(2,1)S(1)}, bf16[128,2048]{1,0:T(8,128)(2,1)S(1)}, u32[]{:S(2)}, u32[]{:S(2)}) collective-permute-start(bf16[128,2048]{1,0:T(8,128)(2,1)S(1)} %feed_forward.3), channel_id=1, source_target_pairs={{0,1},{3,2},{4,5},{7,6},{8,9},{11,10},{12,13},{15,14},{16,17},{19,... | collective-permute-start | bytes 1572872 | tf_op jit(solution)/shard_map/ppermute | solution.py:54
  169.3 18.8 %collective-permute-start.19 = (bf16[128,2048]{1,0:T(8,128)(2,1)S(1)}, bf16[128,2048]{1,0:T(8,128)(2,1)S(1)}, u32[]{:S(2)}, u32[]{:S(2)}) collective-permute-start(bf16[128,2048]{1,0:T(8,128)(2,1)S(1)} %feed_forward.4), channel_id=1, source_target_pairs={{0,1},{3,2},{4,5},{7,6},{8,9},{11,10},{12,13},{15,14},{16,17},{19,... | collective-permute-start | bytes 1572872 | tf_op jit(solution)/shard_map/ppermute | solution.py:54
  176.0 12.2 %copy-start.4 = (bf16[128,2048]{1,0:T(8,128)(2,1)}, bf16[128,2048]{1,0:T(8,128)(2,1)S(1)}, u32[]{:S(2)}) copy-start(bf16[128,2048]{1,0:T(8,128)(2,1)S(1)} %get-tuple-element.49.refs_0_) | copy-start | bytes 1572868
  176.0 24.8 %collective-permute-start.18 = (bf16[128,2048]{1,0:T(8,128)(2,1)S(1)}, bf16[128,2048]{1,0:T(8,128)(2,1)S(1)}, u32[]{:S(2)}, u32[]{:S(2)}) collective-permute-start(bf16[128,2048]{1,0:T(8,128)(2,1)S(1)} %get-tuple-element.50), channel_id=1, source_target_pairs={{0,1},{1,0},{2,3},{3,2},{4,5},{5,4},{6,7},{7,6},{8,9},{9,8},{10,11... | collective-permute-start | bytes 1572872 | tf_op jit(solution)/shard_map/ppermute | solution.py:54
  177.0 23.8 %collective-permute-start.22 = (bf16[128,2048]{1,0:T(8,128)(2,1)S(1)}, bf16[128,2048]{1,0:T(8,128)(2,1)S(1)}, u32[]{:S(2)}, u32[]{:S(2)}) collective-permute-start(bf16[128,2048]{1,0:T(8,128)(2,1)S(1)} %add_convert_fusion), channel_id=1, source_target_pairs={{2,0},{1,3},{6,4},{5,7},{10,8},{9,11},{14,12},{13,15},{18,16},{17,... | collective-permute-start | bytes 1572872 | tf_op jit(solution)/shard_map/ppermute | solution.py:54
  188.3 12.6 %collective-permute-start.20 = (bf16[128,2048]{1,0:T(8,128)(2,1)S(1)}, bf16[128,2048]{1,0:T(8,128)(2,1)S(1)}, u32[]{:S(2)}, u32[]{:S(2)}) collective-permute-start(bf16[128,2048]{1,0:T(8,128)(2,1)S(1)} %add_convert_fusion.1), channel_id=1, source_target_pairs={{1,2},{2,1},{5,6},{6,5},{9,10},{10,9},{13,14},{14,13},{17,18},{18,... | collective-permute-start | bytes 1572872 | tf_op jit(solution)/shard_map/ppermute | solution.py:54
  200.8 0.8 copy-start.14
  200.8 1.0 copy-start.16
  200.8 1.1 copy-start.17
Sparse Core Ops, SparseCore 0:
  9.9 46.9 all-gather.2
  65.8 80.7 all-gather.4

commit v7 on v6

--- a/solution.py
+++ b/solution.py
@@ -356,11 +356,14 @@
 
 def norm(ys, residual, gain):
     count = len(ys)
+    rows, width = residual.shape
+    block = pl.BlockSpec((rows // 2, width), lambda i: (i, 0))
     return pl.pallas_call(
         functools.partial(norm_kernel, count),
         out_shape=(jax.ShapeDtypeStruct(residual.shape, BF16),) * 2,
-        in_specs=[VMEM] * (count + 2),
-        out_specs=(VMEM, VMEM),
+        grid=(2,),
+        in_specs=[block] * (count + 1) + [pl.BlockSpec((1, width), lambda i: (0, 0))],
+        out_specs=(block, block),
         name="stream_norm",
     )(*ys, residual, gain)
 
@@ -448,7 +451,8 @@
 def finish_kernel(count, *refs):
     y_refs, (where, lengths, slot_request, stream, out) = refs[:count], refs[count:]
     rows = stream.shape[0]
-    position = where[0] * rows + lax.broadcasted_iota(jnp.int32, (rows, 1), 0)
+    start = (where[0] * pl.num_programs(0) + pl.program_id(0)) * rows
+    position = start + lax.broadcasted_iota(jnp.int32, (rows, 1), 0)
     total = stream[...].astype(F32)
     for y in y_refs:
         total += y[...].astype(F32)
@@ -458,11 +462,14 @@
 
 def finish(ys, where, lengths, slot_request, stream):
     count = len(ys)
+    rows, width = stream.shape
+    block = pl.BlockSpec((rows // 2, width), lambda i: (i, 0))
     return pl.pallas_call(
         functools.partial(finish_kernel, count),
         out_shape=jax.ShapeDtypeStruct(stream.shape, BF16),
-        in_specs=[VMEM] * count + [SMEM] * 3 + [VMEM],
-        out_specs=VMEM,
+        grid=(2,),
+        in_specs=[block] * count + [SMEM] * 3 + [block],
+        out_specs=block,
         name="last_sum",
     )(*ys, where, lengths, slot_request, stream)
 

time: 213 us -> 212 us (level)
  transfers between devices with their start and end apart: 25 -> 25, of which waited for: 12 -> 12; matrix products, arithmetic and copies ran while one was open for 4% -> 4% of each run, Pallas kernels for 15% -> 14%
where the time goes in v7:
time: 212 us; the launch traced here: 211 us
  waiting for transfers between devices  89.1 us (42%)
  starting transfers between devices  57.9 us (27%)
  Pallas kernels  33 us (16%)
  between operations  14.5 us (7%)
  local copies, waits for them, and re-layouts  11.4 us (5%)
  other arithmetic  5.05 us (2%)
    ppermute x15, waiting for transfers between devices, along(): return lax.ppermute(value, 'seq', pairs)  71.8 us
    ppermute x4, starting transfers between devices, flip(): lax.ppermute(value, 'req', [(i, i ^ bits) for i in range(lax.axis_size('r...  27.5 us
    ppermute x15, starting transfers between devices, along(): return lax.ppermute(value, 'seq', pairs)  20.2 us
    pallas_call x3, Pallas kernels, forward(): pl.pallas_call(functools.partial(forward_kernel, terms, shares, strips),...  14.9 us
    ppermute x4, waiting for transfers between devices, flip(): lax.ppermute(value, 'req', [(i, i ^ bits) for i in range(lax.axis_size('r...  10.3 us
    unnamed x48, local copies, waits for them, and re-layouts  9.53 us
    ppermute x3, starting transfers between devices, shift(): lax.ppermute(value, axis, [(i, (i + steps) % count) for i in range(count)])  8.53 us
    all_gather x1, waiting for transfers between devices, local(): weights = lax.all_gather(weights, 'req', axis=0, tiled=True)  6.97 us
  transfers between devices with their start and end apart: 25, of which 12 were waited for; matrix products, arithmetic and copies ran while one was open for 4% of the time, Pallas kernels for 14%

profile of v7, /device:TPU:0, one launch (start us, length us, event | category | flops | bytes accessed | tf_op | source)
XLA Modules:
  0.0 211.1 jit_solution(11032454418695038078)
XLA Ops:
  7.2 0.0 all-gather.3.cloned.1.call-start
  7.2 1.9 fusion.1
  9.1 0.0 all-gather.3.cloned.1.call-update
  9.1 0.0 all-gather.5.cloned.1.call-start
  9.2 1.6 collective-permute-start.3
  10.8 0.6 pad_add_fusion.refs_0_.refs_4_
  11.3 2.9 %pack.1 = (bf16[144,1536]{1,0:T(8,128)(2,1)}, bf16[144,1536]{1,0:T(8,128)(2,1)}, bf16[144,1536]{1,0:T(8,128)(2,1)}, bf16[144,1536]{1,0:T(8,128)(2,1)}) custom-call(s32[2]{0:T(128)} %pad_add_fusion.refs_0_.refs_4_, s32[8]{0:T(128)} %refs_5_.3, s32[8]{0:T(128)} %refs_6_.3, bf16[128,4096]{1,0:T(8,128)(2,1)} %bitcast.25, bf16[128,2048]{1,0:T(8,128)(2,1)} %bitcast.28, ...), custom_call_target="tpu_custom_call" | custom-call | tf_op jit(solution)/shard_map/pack/pallas_call | solution.py:157
  14.3 3.3 %collective-permute-start = (bf16[144,1536]{1,0:T(8,128)(2,1)}, bf16[144,1536]{1,0:T(8,128)(2,1)S(1)}, u32[]{:S(2)}, u32[]{:S(2)}) collective-permute-start(bf16[144,1536]{1,0:T(8,128)(2,1)} %get-tuple-element.30), channel_id=1, source_target_pairs={{0,1},{1,2},{2,3},{3,0},{4,5},{5,6},{6,7},{7,4},{8,9},{9,10},{10,1... | collective-permute-start | bytes 1327112 | tf_op jit(solution)/shard_map/ppermute | solution.py:42
  17.6 3.2 %collective-permute-start.1 = (bf16[144,1536]{1,0:T(8,128)(2,1)}, bf16[144,1536]{1,0:T(8,128)(2,1)S(1)}, u32[]{:S(2)}, u32[]{:S(2)}) collective-permute-start(bf16[144,1536]{1,0:T(8,128)(2,1)} %get-tuple-element.31), channel_id=1, source_target_pairs={{0,2},{1,3},{2,0},{3,1},{4,6},{5,7},{6,4},{7,5},{8,10},{9,11},{10,... | collective-permute-start | bytes 1327112 | tf_op jit(solution)/shard_map/ppermute | solution.py:42
  20.8 2.0 collective-permute-start.2
  22.8 1.4 copy.17
  24.2 25.5 %collective-permute-start.4 = (bf16[64,2048]{1,0:T(8,128)(2,1)S(1)}, bf16[64,2048]{1,0:T(8,128)(2,1)}, u32[]{:S(2)}, u32[]{:S(2)}) collective-permute-start(bf16[64,2048]{1,0:T(8,128)(2,1)S(1)} %collective-permute-done.3), channel_id=1, source_target_pairs={{0,8},{4,12},{8,0},{12,4},{16,24},{20,28},{24,16},{28,20},{1,9},{5... | collective-permute-start | bytes 786440 | tf_op jit(solution)/shard_map/ppermute | solution.py:46
  49.7 0.0 copy-start.12
  49.8 0.0 copy-start.13
  49.8 2.5 %pad_maximum_fusion = bf16[640,1408]{1,0:T(8,128)(2,1)} fusion(bf16[256,1408]{1,0:T(8,128)(2,1)S(1)} %bitcast.24, bf16[128,1408]{1,0:T(8,128)(2,1)S(1)} %get-tuple-element.56, bf16[256,1408]{1,0:T(8,128)(2,1)} %param.25), kind=kLoop, calls=%fused_computation | loop fusion | flops 5406720 | bytes 3604480 | tf_op jit(solution)/shard_map/concatenate | solution.py:519
  52.3 2.0 collective-permute-start.5
  54.3 4.0 %collective-permute-done.4 = bf16[64,2048]{1,0:T(8,128)(2,1)} collective-permute-done((bf16[64,2048]{1,0:T(8,128)(2,1)S(1)}, bf16[64,2048]{1,0:T(8,128)(2,1)}, u32[]{:S(2)}, u32[]{:S(2)}) %collective-permute-start.4) | collective-permute-done | bytes 262176 | tf_op jit(solution)/shard_map/ppermute | solution.py:46
  58.3 1.0 constant_dynamic-update-slice_fusion.2
  59.3 6.3 %collective-permute-done.6 = bf16[64,2048]{1,0:T(8,128)(2,1)S(1)} collective-permute-done((bf16[64,2048]{1,0:T(8,128)(2,1)S(1)}, bf16[64,2048]{1,0:T(8,128)(2,1)S(1)}, u32[]{:S(2)}, u32[]{:S(2)}) %collective-permute-start.6) | collective-permute-done | bytes 262176 | tf_op jit(solution)/shard_map/ppermute | solution.py:46
  65.6 0.0 all-gather.3.cloned.1.call-done.refs_2_
  65.7 0.0 all-gather.5.cloned.1.call-update
  65.7 0.1 collective-permute-start.7
  65.8 0.1 pad_add_fusion.1.refs_1_
  65.9 6.6 %delta_rule.1 = (bf16[4,128,512]{2,1,0:T(8,128)(2,1)S(1)}, f32[2,128,256]{2,1,0:T(8,128)}) custom-call(bf16[144,1536]{1,0:T(8,128)(2,1)S(1)} %copy-done.8, bf16[144,1536]{1,0:T(8,128)(2,1)S(1)} %collective-permute-done.refs_1_, bf16[144,1536]{1,0:T(8,128)(2,1)S(1)} %collective-permute-done.1.refs_2_, bf16[144,1536]{1,0:T(8,128)(2,1)S(1)} %collective-permute-done.2.refs_3_, ...), custom_call_target="tpu_custom_call" | custom-call | flops 4000000000 | bytes 4194304 | tf_op jit(solution)/shard_map/delta_rule/pallas_call | solution.py:285
  72.5 3.3 %output_projection.1 = (bf16[128,2048]{1,0:T(8,128)(2,1)S(1)}, bf16[128,2048]{1,0:T(8,128)(2,1)S(1)}, bf16[128,2048]{1,0:T(8,128)(2,1)S(1)}, bf16[128,2048]{1,0:T(8,128)(2,1)S(1)}) custom-call(s32[2]{0:T(128)S(1)} %copy-done.7, s32[4]{0:T(128)S(1)} %pad_add_fusion.1.refs_1_, bf16[4,128,512]{2,1,0:T(8,128)(2,1)S(1)} %get-tuple-element.33.refs_2_, ...), custom_call_target="tpu_custom_call" | custom-call | flops 1073741824 | bytes 4194304 | tf_op jit(solution)/shard_map/output_projection/pallas_call | solution.py:331
  75.9 0.8 copy-done.3
  76.7 4.3 %collective-permute-start.9 = (bf16[128,2048]{1,0:T(8,128)(2,1)S(1)}, bf16[128,2048]{1,0:T(8,128)(2,1)S(1)}, u32[]{:S(2)}, u32[]{:S(2)}) collective-permute-start(bf16[128,2048]{1,0:T(8,128)(2,1)S(1)} %get-tuple-element.36), channel_id=1, source_target_pairs={{0,1},{3,2},{4,5},{7,6},{8,9},{11,10},{12,13},{15,14},{16,17},{19,... | collective-permute-start | bytes 1572872 | tf_op jit(solution)/shard_map/ppermute | solution.py:54
  81.0 1.3 collective-permute-start.11
  82.3 0.1 collective-permute-start.8
  82.4 10.8 %collective-permute-done.9 = bf16[128,2048]{1,0:T(8,128)(2,1)S(1)} collective-permute-done((bf16[128,2048]{1,0:T(8,128)(2,1)S(1)}, bf16[128,2048]{1,0:T(8,128)(2,1)S(1)}, u32[]{:S(2)}, u32[]{:S(2)}) %collective-permute-start.9) | collective-permute-done | bytes 524320 | tf_op jit(solution)/shard_map/ppermute | solution.py:54
  93.2 0.1 add_convert_fusion.3
  93.3 1.5 collective-permute-start.10
  94.8 9.6 %collective-permute-done.11 = bf16[128,2048]{1,0:T(8,128)(2,1)S(1)} collective-permute-done((bf16[128,2048]{1,0:T(8,128)(2,1)S(1)}, bf16[128,2048]{1,0:T(8,128)(2,1)S(1)}, u32[]{:S(2)}, u32[]{:S(2)}) %collective-permute-start.11) | collective-permute-done | bytes 524320 | tf_op jit(solution)/shard_map/ppermute | solution.py:54
  104.4 0.1 add_convert_fusion.2
  104.5 1.3 collective-permute-start.12
  105.8 9.3 %collective-permute-done.8.refs_1_ = bf16[128,2048]{1,0:T(8,128)(2,1)S(1)} collective-permute-done((bf16[128,2048]{1,0:T(8,128)(2,1)S(1)}, bf16[128,2048]{1,0:T(8,128)(2,1)S(1)}, u32[]{:S(2)}, u32[]{:S(2)}) %collective-permute-start.8) | collective-permute-done | bytes 524320 | tf_op jit(solution)/shard_map/ppermute | solution.py:54
  115.2 6.4 %collective-permute-done.12.refs_3_ = bf16[128,2048]{1,0:T(8,128)(2,1)} collective-permute-done((bf16[128,2048]{1,0:T(8,128)(2,1)S(1)}, bf16[128,2048]{1,0:T(8,128)(2,1)}, u32[]{:S(2)}, u32[]{:S(2)}) %collective-permute-start.12) | collective-permute-done | bytes 524320 | tf_op jit(solution)/shard_map/ppermute | solution.py:54
  121.5 2.8 %stream_norm.1 = (bf16[128,2048]{1,0:T(8,128)(2,1)}, bf16[128,2048]{1,0:T(8,128)(2,1)}) custom-call(bf16[128,2048]{1,0:T(8,128)(2,1)} %copy-done.3, bf16[128,2048]{1,0:T(8,128)(2,1)} %copy-done.15, bf16[128,2048]{1,0:T(8,128)(2,1)} %collective-permute-done.10.refs_2_, bf16[128,2048]{1,0:T(8,128)(2,1)} %collective-permute-done.12.refs_3_, ...), custom_call_target="tpu_custom_call" | custom-call | tf_op jit(solution)/shard_map/stream_norm/pallas_call | solution.py:361
  124.3 2.1 %collective-permute-start.16 = (bf16[128,2048]{1,0:T(8,128)(2,1)}, bf16[128,2048]{1,0:T(8,128)(2,1)}, u32[]{:S(2)}, u32[]{:S(2)}) collective-permute-start(bf16[128,2048]{1,0:T(8,128)(2,1)} %get-tuple-element.47.refs_0_), channel_id=1, source_target_pairs={{0,2},{3,1},{4,6},{7,5},{8,10},{11,9},{12,14},{15,13},{16,18},{19,... | collective-permute-start | bytes 1572872 | tf_op jit(solution)/shard_map/ppermute | solution.py:54
  126.4 1.5 collective-permute-start.14
  127.9 10.5 %collective-permute-done.16.refs_0_ = bf16[128,2048]{1,0:T(8,128)(2,1)} collective-permute-done((bf16[128,2048]{1,0:T(8,128)(2,1)}, bf16[128,2048]{1,0:T(8,128)(2,1)}, u32[]{:S(2)}, u32[]{:S(2)}) %collective-permute-start.16) | collective-permute-done | bytes 524320 | tf_op jit(solution)/shard_map/ppermute | solution.py:54
  138.4 1.3 collective-permute-start.17
  139.7 7.0 %all-gather.5.cloned.1.call-done.refs_3_ = bf16[5120,1408]{1,0:T(8,128)(2,1)} async-done(((bf16[640,1408]{1,0:T(8,128)(2,1)}), bf16[5120,1408]{1,0:T(8,128)(2,1)}) %all-gather.5.cloned.1.call-update) | async-done | bytes 14417936 | tf_op jit(solution)/shard_map/all_gather | solution.py:521
  146.6 1.5 collective-permute-start.15
  148.1 4.2 %collective-permute-done.17.refs_1_ = bf16[128,2048]{1,0:T(8,128)(2,1)} collective-permute-done((bf16[128,2048]{1,0:T(8,128)(2,1)}, bf16[128,2048]{1,0:T(8,128)(2,1)}, u32[]{:S(2)}, u32[]{:S(2)}) %collective-permute-start.17) | collective-permute-done | bytes 524320 | tf_op jit(solution)/shard_map/ppermute | solution.py:54
  152.3 5.1 %copy-done = bf16[5120,1408]{1,0:T(8,128)(2,1)S(1)} copy-done((bf16[5120,1408]{1,0:T(8,128)(2,1)S(1)}, bf16[5120,1408]{1,0:T(8,128)(2,1)}, u32[]{:S(2)}) %copy-start) | copy-done | bytes 14417944
  157.4 5.0 %feed_forward.3 = bf16[128,2048]{1,0:T(8,128)(2,1)S(1)} custom-call(bf16[128,2048]{1,0:T(8,128)(2,1)} %collective-permute-done.16.refs_0_, bf16[128,2048]{1,0:T(8,128)(2,1)} %collective-permute-done.17.refs_1_, bf16[1024,1408]{1,0:T(8,128)(2,1)S(1)} %copy-done.1, bf16[5120,1408]{1,0:T(8,128)(2,1)S(1)} %copy-done), custom_call_target="tpu_custom_call" | custom-call | flops 2214592512 | bytes 20971520 | tf_op jit(solution)/shard_map/feed_forward/pallas_call | solution.py:432
  162.4 1.9 collective-permute-start.21
  164.3 4.7 %feed_forward.4 = bf16[128,2048]{1,0:T(8,128)(2,1)S(1)} custom-call(bf16[128,2048]{1,0:T(8,128)(2,1)} %collective-permute-done.14.refs_0_, bf16[128,2048]{1,0:T(8,128)(2,1)S(1)} %collective-permute-done.15.refs_1_, bf16[1024,1408]{1,0:T(8,128)(2,1)S(1)} %copy-done.1, bf16[5120,1408]{1,0:T(8,128)(2,1)S(1)} %copy-done), custom_call_target="tpu_custom_call" | custom-call | flops 2214592512 | bytes 20971520 | tf_op jit(solution)/shard_map/feed_forward/pallas_call | solution.py:432
  169.0 1.5 collective-permute-start.19
  170.6 5.2 %feed_forward.5 = (bf16[128,2048]{1,0:T(8,128)(2,1)S(1)}, bf16[128,2048]{1,0:T(8,128)(2,1)S(1)}) custom-call(bf16[128,2048]{1,0:T(8,128)(2,1)S(1)} %copy-done.2, bf16[128,2048]{1,0:T(8,128)(2,1)S(1)} %collective-permute-done.13.refs_1_, bf16[1024,1408]{1,0:T(8,128)(2,1)S(1)} %copy-done.1, bf16[5120,1408]{1,0:T(8,128)(2,1)S(1)} %bitcast.22), custom_call_target="tpu_custom_call" | custom-call | flops 4429185024 | bytes 20971520 | tf_op jit(solution)/shard_map/feed_forward/pallas_call | solution.py:432
  175.7 0.1 collective-permute-start.18
  175.8 0.8 collective-permute-done.21
  176.6 0.1 add_convert_fusion
  176.7 1.3 collective-permute-start.22
  178.0 9.8 %collective-permute-done.19 = bf16[128,2048]{1,0:T(8,128)(2,1)S(1)} collective-permute-done((bf16[128,2048]{1,0:T(8,128)(2,1)S(1)}, bf16[128,2048]{1,0:T(8,128)(2,1)S(1)}, u32[]{:S(2)}, u32[]{:S(2)}) %collective-permute-start.19) | collective-permute-done | bytes 524320 | tf_op jit(solution)/shard_map/ppermute | solution.py:54
  187.8 0.1 add_convert_fusion.1
  188.0 0.7 collective-permute-start.20
  188.7 1.4 fusion
  190.1 10.5 %collective-permute-done.18.refs_1_ = bf16[128,2048]{1,0:T(8,128)(2,1)S(1)} collective-permute-done((bf16[128,2048]{1,0:T(8,128)(2,1)S(1)}, bf16[128,2048]{1,0:T(8,128)(2,1)S(1)}, u32[]{:S(2)}, u32[]{:S(2)}) %collective-permute-start.18) | collective-permute-done | bytes 524320 | tf_op jit(solution)/shard_map/ppermute | solution.py:54
  200.6 0.8 copy-done.14
  201.3 0.2 copy-done.16
  201.5 0.1 copy-done.17
  201.7 2.6 %last_sum.1 = bf16[128,2048]{1,0:T(8,128)(2,1)} custom-call(bf16[128,2048]{1,0:T(8,128)(2,1)} %copy-done.4, bf16[128,2048]{1,0:T(8,128)(2,1)} %copy-done.14, bf16[128,2048]{1,0:T(8,128)(2,1)} %copy-done.17, bf16[128,2048]{1,0:T(8,128)(2,1)} %copy-done.16, s32[2]{0:T(128)} %pad_add_fusion.refs_0_.refs_4_, s32[8]{0:T(128)} %refs_5_.3, s32[8]{0:T(128)} %refs_6_.3, ...), custom_call_target="tpu_custom_call" | custom-call | tf_op jit(solution)/shard_map/last_sum/pallas_call | solution.py:467
  (55 shorter events, 0.2 us)
Async XLA Ops:
  7.2 58.5 %all-gather.3.cloned.1.call-start = ((), (), s32[]{:S(2)}) async-start(), calls=%async_computation | async-start | bytes 3244032 | tf_op jit(solution)/shard_map/all_gather | solution.py:518
  9.1 137.5 %all-gather.5.cloned.1.call-start = ((), (), s32[]{:S(2)}) async-start(), calls=%async_computation.1 | async-start | bytes 16220160 | tf_op jit(solution)/shard_map/all_gather | solution.py:521
  9.2 15.1 %collective-permute-start.3 = (bf16[64,2048]{1,0:T(8,128)(2,1)}, bf16[64,2048]{1,0:T(8,128)(2,1)S(1)}, u32[]{:S(2)}, u32[]{:S(2)}) collective-permute-start(bf16[64,2048]{1,0:T(8,128)(2,1)} %param.23), channel_id=1, source_target_pairs={{0,0},{1,4},{2,8},{3,12},{4,16},{5,20},{6,24},{7,28},{8,1},{9,5},{... | collective-permute-start | bytes 786440 | tf_op jit(solution)/shard_map/ppermute | solution.py:508
  14.3 51.3 %collective-permute-start = (bf16[144,1536]{1,0:T(8,128)(2,1)}, bf16[144,1536]{1,0:T(8,128)(2,1)S(1)}, u32[]{:S(2)}, u32[]{:S(2)}) collective-permute-start(bf16[144,1536]{1,0:T(8,128)(2,1)} %get-tuple-element.30), channel_id=1, source_target_pairs={{0,1},{1,2},{2,3},{3,0},{4,5},{5,6},{6,7},{7,4},{8,9},{9,10},{10,1... | collective-permute-start | bytes 1327112 | tf_op jit(solution)/shard_map/ppermute | solution.py:42
  17.6 48.0 %collective-permute-start.1 = (bf16[144,1536]{1,0:T(8,128)(2,1)}, bf16[144,1536]{1,0:T(8,128)(2,1)S(1)}, u32[]{:S(2)}, u32[]{:S(2)}) collective-permute-start(bf16[144,1536]{1,0:T(8,128)(2,1)} %get-tuple-element.31), channel_id=1, source_target_pairs={{0,2},{1,3},{2,0},{3,1},{4,6},{5,7},{6,4},{7,5},{8,10},{9,11},{10,... | collective-permute-start | bytes 1327112 | tf_op jit(solution)/shard_map/ppermute | solution.py:42
  20.8 44.9 %collective-permute-start.2 = (bf16[144,1536]{1,0:T(8,128)(2,1)}, bf16[144,1536]{1,0:T(8,128)(2,1)S(1)}, u32[]{:S(2)}, u32[]{:S(2)}) collective-permute-start(bf16[144,1536]{1,0:T(8,128)(2,1)} %get-tuple-element.32), channel_id=1, source_target_pairs={{0,3},{1,0},{2,1},{3,2},{4,7},{5,4},{6,5},{7,6},{8,11},{9,8},{10,9... | collective-permute-start | bytes 1327112 | tf_op jit(solution)/shard_map/ppermute | solution.py:42
  24.2 34.0 %collective-permute-start.4 = (bf16[64,2048]{1,0:T(8,128)(2,1)S(1)}, bf16[64,2048]{1,0:T(8,128)(2,1)}, u32[]{:S(2)}, u32[]{:S(2)}) collective-permute-start(bf16[64,2048]{1,0:T(8,128)(2,1)S(1)} %collective-permute-done.3), channel_id=1, source_target_pairs={{0,8},{4,12},{8,0},{12,4},{16,24},{20,28},{24,16},{28,20},{1,9},{5... | collective-permute-start | bytes 786440 | tf_op jit(solution)/shard_map/ppermute | solution.py:46
  49.7 16.1 %copy-start.5 = (s32[8]{0:T(128)S(1)}, s32[8]{0:T(128)}, u32[]{:S(2)}) copy-start(s32[8]{0:T(128)} %refs_5_.3) | copy-start | bytes 100
  49.7 16.1 %copy-start.6 = (s32[8]{0:T(128)S(1)}, s32[8]{0:T(128)}, u32[]{:S(2)}) copy-start(s32[8]{0:T(128)} %refs_6_.3) | copy-start | bytes 100
  49.7 16.1 %copy-start.7 = (s32[2]{0:T(128)S(1)}, s32[2]{0:T(128)}, u32[]{:S(2)}) copy-start(s32[2]{0:T(128)} %pad_add_fusion.refs_0_.refs_4_) | copy-start | bytes 28
  49.7 16.1 %copy-start.8 = (bf16[144,1536]{1,0:T(8,128)(2,1)S(1)}, bf16[144,1536]{1,0:T(8,128)(2,1)}, u32[]{:S(2)}) copy-start(bf16[144,1536]{1,0:T(8,128)(2,1)} %get-tuple-element.29.refs_0_) | copy-start | bytes 1327108
  49.7 16.1 %copy-start.12 = (f32[4,4096]{1,0:T(4,128)S(1)}, f32[4,4096]{1,0:T(4,128)}, u32[]{:S(2)}) copy-start(f32[4,4096]{1,0:T(4,128)} %refs_7_.1) | copy-start | bytes 196612
  49.8 16.1 %copy-start.13 = (f32[256]{0:T(256)S(1)}, f32[256]{0:T(256)}, u32[]{:S(2)}) copy-start(f32[256]{0:T(256)} %param.22) | copy-start | bytes 3076
  52.3 7.0 %collective-permute-start.5 = (bf16[64,2048]{1,0:T(8,128)(2,1)S(1)}, bf16[64,2048]{1,0:T(8,128)(2,1)S(1)}, u32[]{:S(2)}, u32[]{:S(2)}) collective-permute-start(bf16[64,2048]{1,0:T(8,128)(2,1)S(1)} %collective-permute-done.3), channel_id=1, source_target_pairs={{0,16},{4,20},{8,24},{12,28},{16,0},{20,4},{24,8},{28,12},{1,17},{... | collective-permute-start | bytes 786440 | tf_op jit(solution)/shard_map/ppermute | solution.py:46
  58.3 7.3 %collective-permute-start.6 = (bf16[64,2048]{1,0:T(8,128)(2,1)S(1)}, bf16[64,2048]{1,0:T(8,128)(2,1)S(1)}, u32[]{:S(2)}, u32[]{:S(2)}) collective-permute-start(bf16[64,2048]{1,0:T(8,128)(2,1)S(1)} %collective-permute-done.3), channel_id=1, source_target_pairs={{0,24},{4,28},{8,16},{12,20},{16,8},{20,12},{24,0},{28,4},{1,25},{... | collective-permute-start | bytes 786440 | tf_op jit(solution)/shard_map/ppermute | solution.py:46
  65.6 6.9 %copy-start.9 = (bf16[144,1536]{1,0:T(8,128)(2,1)}, bf16[144,1536]{1,0:T(8,128)(2,1)S(1)}, u32[]{:S(2)}) copy-start(bf16[144,1536]{1,0:T(8,128)(2,1)S(1)} %collective-permute-done.refs_1_) | copy-start | bytes 1327108
  65.6 6.9 %copy-start.10 = (bf16[144,1536]{1,0:T(8,128)(2,1)}, bf16[144,1536]{1,0:T(8,128)(2,1)S(1)}, u32[]{:S(2)}) copy-start(bf16[144,1536]{1,0:T(8,128)(2,1)S(1)} %collective-permute-done.1.refs_2_) | copy-start | bytes 1327108
  65.6 6.9 %copy-start.11 = (bf16[144,1536]{1,0:T(8,128)(2,1)}, bf16[144,1536]{1,0:T(8,128)(2,1)S(1)}, u32[]{:S(2)}) copy-start(bf16[144,1536]{1,0:T(8,128)(2,1)S(1)} %collective-permute-done.2.refs_3_) | copy-start | bytes 1327108
  65.7 6.8 %collective-permute-start.7 = (bf16[256,2048]{1,0:T(8,128)(2,1)S(1)}, bf16[256,2048]{1,0:T(8,128)(2,1)}, u32[]{:S(2)}, u32[]{:S(2)}) collective-permute-start(bf16[256,2048]{1,0:T(8,128)(2,1)S(1)} %constant_dynamic-update-slice_fusion.refs_3_), channel_id=1, source_target_pairs={{0,4},{4,0},{8,12},{12,8},{16,20},{20,16},{24,28},{28,24},{1,5},{5... | collective-permute-start | bytes 3145736 | tf_op jit(solution)/shard_map/ppermute | solution.py:46
  75.9 0.8 copy-start.3
  76.7 75.6 %copy-start.1 = (bf16[1024,1408]{1,0:T(8,128)(2,1)S(1)}, bf16[1024,1408]{1,0:T(8,128)(2,1)}, u32[]{:S(2)}) copy-start(bf16[1024,1408]{1,0:T(8,128)(2,1)} %all-gather.3.cloned.1.call-done.refs_2_) | copy-start | bytes 8650756
  76.7 16.5 %collective-permute-start.9 = (bf16[128,2048]{1,0:T(8,128)(2,1)S(1)}, bf16[128,2048]{1,0:T(8,128)(2,1)S(1)}, u32[]{:S(2)}, u32[]{:S(2)}) collective-permute-start(bf16[128,2048]{1,0:T(8,128)(2,1)S(1)} %get-tuple-element.36), channel_id=1, source_target_pairs={{0,1},{3,2},{4,5},{7,6},{8,9},{11,10},{12,13},{15,14},{16,17},{19,... | collective-permute-start | bytes 1572872 | tf_op jit(solution)/shard_map/ppermute | solution.py:54
  81.0 23.4 %collective-permute-start.11 = (bf16[128,2048]{1,0:T(8,128)(2,1)S(1)}, bf16[128,2048]{1,0:T(8,128)(2,1)S(1)}, u32[]{:S(2)}, u32[]{:S(2)}) collective-permute-start(bf16[128,2048]{1,0:T(8,128)(2,1)S(1)} %get-tuple-element.38), channel_id=1, source_target_pairs={{0,1},{3,2},{4,5},{7,6},{8,9},{11,10},{12,13},{15,14},{16,17},{19,... | collective-permute-start | bytes 1572872 | tf_op jit(solution)/shard_map/ppermute | solution.py:54
  82.3 32.9 %collective-permute-start.8 = (bf16[128,2048]{1,0:T(8,128)(2,1)S(1)}, bf16[128,2048]{1,0:T(8,128)(2,1)S(1)}, u32[]{:S(2)}, u32[]{:S(2)}) collective-permute-start(bf16[128,2048]{1,0:T(8,128)(2,1)S(1)} %get-tuple-element.35), channel_id=1, source_target_pairs={{0,1},{1,0},{2,3},{3,2},{4,5},{5,4},{6,7},{7,6},{8,9},{9,8},{10,11... | collective-permute-start | bytes 1572872 | tf_op jit(solution)/shard_map/ppermute | solution.py:54
  93.3 21.9 %collective-permute-start.10 = (bf16[128,2048]{1,0:T(8,128)(2,1)S(1)}, bf16[128,2048]{1,0:T(8,128)(2,1)}, u32[]{:S(2)}, u32[]{:S(2)}) collective-permute-start(bf16[128,2048]{1,0:T(8,128)(2,1)S(1)} %add_convert_fusion.3), channel_id=1, source_target_pairs={{1,2},{2,1},{5,6},{6,5},{9,10},{10,9},{13,14},{14,13},{17,18},{18,... | collective-permute-start | bytes 1572872 | tf_op jit(solution)/shard_map/ppermute | solution.py:54
  104.5 17.0 %collective-permute-start.12 = (bf16[128,2048]{1,0:T(8,128)(2,1)S(1)}, bf16[128,2048]{1,0:T(8,128)(2,1)}, u32[]{:S(2)}, u32[]{:S(2)}) collective-permute-start(bf16[128,2048]{1,0:T(8,128)(2,1)S(1)} %add_convert_fusion.2), channel_id=1, source_target_pairs={{2,0},{1,3},{6,4},{5,7},{10,8},{9,11},{14,12},{13,15},{18,16},{17,... | collective-permute-start | bytes 1572872 | tf_op jit(solution)/shard_map/ppermute | solution.py:54
  115.2 6.4 %copy-start.15 = (bf16[128,2048]{1,0:T(8,128)(2,1)}, bf16[128,2048]{1,0:T(8,128)(2,1)S(1)}, u32[]{:S(2)}) copy-start(bf16[128,2048]{1,0:T(8,128)(2,1)S(1)} %collective-permute-done.8.refs_1_) | copy-start | bytes 1572868
  124.3 14.1 %collective-permute-start.16 = (bf16[128,2048]{1,0:T(8,128)(2,1)}, bf16[128,2048]{1,0:T(8,128)(2,1)}, u32[]{:S(2)}, u32[]{:S(2)}) collective-permute-start(bf16[128,2048]{1,0:T(8,128)(2,1)} %get-tuple-element.47.refs_0_), channel_id=1, source_target_pairs={{0,2},{3,1},{4,6},{7,5},{8,10},{11,9},{12,14},{15,13},{16,18},{19,... | collective-permute-start | bytes 1572872 | tf_op jit(solution)/shard_map/ppermute | solution.py:54
  126.4 13.2 %collective-permute-start.14 = (bf16[128,2048]{1,0:T(8,128)(2,1)}, bf16[128,2048]{1,0:T(8,128)(2,1)}, u32[]{:S(2)}, u32[]{:S(2)}) collective-permute-start(bf16[128,2048]{1,0:T(8,128)(2,1)} %get-tuple-element.47.refs_0_), channel_id=1, source_target_pairs={{1,2},{2,1},{5,6},{6,5},{9,10},{10,9},{13,14},{14,13},{17,18},{18,... | collective-permute-start | bytes 1572872 | tf_op jit(solution)/shard_map/ppermute | solution.py:54
  127.9 20.2 %collective-permute-start.13 = (bf16[128,2048]{1,0:T(8,128)(2,1)}, bf16[128,2048]{1,0:T(8,128)(2,1)S(1)}, u32[]{:S(2)}, u32[]{:S(2)}) collective-permute-start(bf16[128,2048]{1,0:T(8,128)(2,1)} %get-tuple-element.47.refs_0_), channel_id=1, source_target_pairs={{0,1},{1,0},{2,3},{3,2},{4,5},{5,4},{6,7},{7,6},{8,9},{9,8},{10,11... | collective-permute-start | bytes 1572872 | tf_op jit(solution)/shard_map/ppermute | solution.py:54
  138.4 13.9 %collective-permute-start.17 = (bf16[128,2048]{1,0:T(8,128)(2,1)}, bf16[128,2048]{1,0:T(8,128)(2,1)}, u32[]{:S(2)}, u32[]{:S(2)}) collective-permute-start(bf16[128,2048]{1,0:T(8,128)(2,1)} %collective-permute-done.16.refs_0_), channel_id=1, source_target_pairs={{1,0},{2,3},{5,4},{6,7},{9,8},{10,11},{13,12},{14,15},{17,16},{18,... | collective-permute-start | bytes 1572872 | tf_op jit(solution)/shard_map/ppermute | solution.py:54
  146.6 17.7 %collective-permute-start.15 = (bf16[128,2048]{1,0:T(8,128)(2,1)}, bf16[128,2048]{1,0:T(8,128)(2,1)S(1)}, u32[]{:S(2)}, u32[]{:S(2)}) collective-permute-start(bf16[128,2048]{1,0:T(8,128)(2,1)} %collective-permute-done.14.refs_0_), channel_id=1, source_target_pairs={{1,0},{2,3},{5,4},{6,7},{9,8},{10,11},{13,12},{14,15},{17,16},{18,... | collective-permute-start | bytes 1572872 | tf_op jit(solution)/shard_map/ppermute | solution.py:54
  152.3 5.1 %copy-start = (bf16[5120,1408]{1,0:T(8,128)(2,1)S(1)}, bf16[5120,1408]{1,0:T(8,128)(2,1)}, u32[]{:S(2)}) copy-start(bf16[5120,1408]{1,0:T(8,128)(2,1)} %all-gather.5.cloned.1.call-done.refs_3_) | copy-start | bytes 43253764
  157.4 13.1 %slice-start = ((s8[14417920]{0:T(1024)(128)(4,1)}), s8[4194304]{0:T(1024)(128)(4,1)S(1)}, s32[]{:S(2)}) async-start(s8[14417920]{0:T(1024)(128)(4,1)} %bitcast.21), calls=%async_computation.2 | async-start | bytes 8388608
  157.4 13.1 %slice-start.1 = ((s8[14417920]{0:T(1024)(128)(4,1)}), s8[4194304]{0:T(1024)(128)(4,1)S(1)}, s32[]{:S(2)}) async-start(s8[14417920]{0:T(1024)(128)(4,1)} %bitcast.21), calls=%async_computation.3 | async-start | bytes 8388608
  162.4 8.1 %slice-start.2 = ((s8[14417920]{0:T(1024)(128)(4,1)}), s8[4194304]{0:T(1024)(128)(4,1)S(1)}, s32[]{:S(2)}) async-start(s8[14417920]{0:T(1024)(128)(4,1)} %bitcast.21), calls=%async_computation.4 | async-start | bytes 8388608
  162.4 8.1 %slice-start.3 = ((s8[14417920]{0:T(1024)(128)(4,1)}), s8[1835008]{0:T(1024)(128)(4,1)S(1)}, s32[]{:S(2)}) async-start(s8[14417920]{0:T(1024)(128)(4,1)} %bitcast.21), calls=%async_computation.5 | async-start | bytes 3670016
  162.4 8.1 %copy-start.2 = (bf16[128,2048]{1,0:T(8,128)(2,1)S(1)}, bf16[128,2048]{1,0:T(8,128)(2,1)}, u32[]{:S(2)}) copy-start(bf16[128,2048]{1,0:T(8,128)(2,1)} %get-tuple-element.47.refs_0_) | copy-start | bytes 1572868
  162.4 14.2 %collective-permute-start.21 = (bf16[128,2048]{1,0:T(8,128)(2,1)S(1)}, bf16[128,2048]{1,0:T(8,128)(2,1)S(1)}, u32[]{:S(2)}, u32[]{:S(2)}) collective-permute-start(bf16[128,2048]{1,0:T(8,128)(2,1)S(1)} %feed_forward.3), channel_id=1, source_target_pairs={{0,1},{3,2},{4,5},{7,6},{8,9},{11,10},{12,13},{15,14},{16,17},{19,... | collective-permute-start | bytes 1572872 | tf_op jit(solution)/shard_map/ppermute | solution.py:54
  169.0 18.8 %collective-permute-start.19 = (bf16[128,2048]{1,0:T(8,128)(2,1)S(1)}, bf16[128,2048]{1,0:T(8,128)(2,1)S(1)}, u32[]{:S(2)}, u32[]{:S(2)}) collective-permute-start(bf16[128,2048]{1,0:T(8,128)(2,1)S(1)} %feed_forward.4), channel_id=1, source_target_pairs={{0,1},{3,2},{4,5},{7,6},{8,9},{11,10},{12,13},{15,14},{16,17},{19,... | collective-permute-start | bytes 1572872 | tf_op jit(solution)/shard_map/ppermute | solution.py:54
  175.7 12.2 %copy-start.4 = (bf16[128,2048]{1,0:T(8,128)(2,1)}, bf16[128,2048]{1,0:T(8,128)(2,1)S(1)}, u32[]{:S(2)}) copy-start(bf16[128,2048]{1,0:T(8,128)(2,1)S(1)} %get-tuple-element.49.refs_0_) | copy-start | bytes 1572868
  175.7 24.8 %collective-permute-start.18 = (bf16[128,2048]{1,0:T(8,128)(2,1)S(1)}, bf16[128,2048]{1,0:T(8,128)(2,1)S(1)}, u32[]{:S(2)}, u32[]{:S(2)}) collective-permute-start(bf16[128,2048]{1,0:T(8,128)(2,1)S(1)} %get-tuple-element.50), channel_id=1, source_target_pairs={{0,1},{1,0},{2,3},{3,2},{4,5},{5,4},{6,7},{7,6},{8,9},{9,8},{10,11... | collective-permute-start | bytes 1572872 | tf_op jit(solution)/shard_map/ppermute | solution.py:54
  176.7 23.8 %collective-permute-start.22 = (bf16[128,2048]{1,0:T(8,128)(2,1)S(1)}, bf16[128,2048]{1,0:T(8,128)(2,1)S(1)}, u32[]{:S(2)}, u32[]{:S(2)}) collective-permute-start(bf16[128,2048]{1,0:T(8,128)(2,1)S(1)} %add_convert_fusion), channel_id=1, source_target_pairs={{2,0},{1,3},{6,4},{5,7},{10,8},{9,11},{14,12},{13,15},{18,16},{17,... | collective-permute-start | bytes 1572872 | tf_op jit(solution)/shard_map/ppermute | solution.py:54
  188.0 12.6 %collective-permute-start.20 = (bf16[128,2048]{1,0:T(8,128)(2,1)S(1)}, bf16[128,2048]{1,0:T(8,128)(2,1)S(1)}, u32[]{:S(2)}, u32[]{:S(2)}) collective-permute-start(bf16[128,2048]{1,0:T(8,128)(2,1)S(1)} %add_convert_fusion.1), channel_id=1, source_target_pairs={{1,2},{2,1},{5,6},{6,5},{9,10},{10,9},{13,14},{14,13},{17,18},{18,... | collective-permute-start | bytes 1572872 | tf_op jit(solution)/shard_map/ppermute | solution.py:54
  200.5 0.8 copy-start.14
  200.6 1.0 copy-start.16
  200.6 1.1 copy-start.17
Sparse Core Ops, SparseCore 0:
  9.9 46.9 all-gather.2
  65.8 80.7 all-gather.4
